TPU v7x, 32 devices: a whole 2x2x4 slice. The times are simulated.
32 devices in a mesh: groups: 2 (over x), ctx: 16 (over z, y, core).
Axes of the slice: x: 2, y: 2, z: 4, core: 2. Of those that a mesh axis runs over, the one named last changes fastest.
Arguments:
- hidden_states: bfloat16 [16384, 4096], P(('groups', 'ctx')), parts along dimension 0, may hold values from -6 to 6
- query_weight: bfloat16 [4096, 1024], P('ctx'), may hold values from -0.09375 to 0.09375
- output_weight: bfloat16 [1024, 4096], P('ctx'), may hold values from -0.1875 to 0.1875
- keys: bfloat16 [16384, 128], P(('groups', 'ctx')), parts along dimension 0
- values: bfloat16 [16384, 128], P(('groups', 'ctx')), parts along dimension 0, may hold values from -6 to 6
- block_lists: int32 [32, 3], P('groups'), parts along dimension 0, may hold values from 0 to 15, as said below
Outputs:
- projected: bfloat16 [16384, 4096], P(('groups', 'ctx')), parts along dimension 0
There are 2 independent parts, one for each index of `groups`. A program takes and returns all parts, laid end to end along the dimension named above; an argument that names none is the same for every part. Nothing has to cross between parts.
Inputs may be any that keep to these rules, and one draw needn't show every extreme that they name: Each row of block_lists names 3 different key blocks. In a row b with b >= 3 all entries are smaller than b; entries at or after b are not attended.
All inputs are finite; a program needn't handle non-finite values.
Results may differ from a plain program's by a relative error of at most 0.003.
The roundings to bfloat16 on the way count: a program that leaves them out, or rounds other values in their place, can miss the bound.
Values may be sent and summed in bfloat16 or wider, within the bound.
No kernel may reach another device: no remote copies, remote signals or barrier semaphores. Data moves between devices by JAX's collectives and lax.ppermute only.
A program may use at most 128 MiB of HBM per device.

v0:
```python
import math

import jax
import jax.numpy as jnp
from jax import lax
from jax.sharding import PartitionSpec as P

BLOCK = 512
TOPK = 3


def per_device(hidden_states, query_weight, output_weight, keys, values, block_lists):
    tok_rows = hidden_states.shape[0]
    head_size = keys.shape[1]
    heads_count = query_weight.shape[1] // head_size
    devices = lax.axis_size("ctx")
    blocks_here = tok_rows // BLOCK
    piece_rows = BLOCK // devices
    listed_count = blocks_here * TOPK
    first_block = lax.axis_index("ctx") * blocks_here
    columns = hidden_states
    query_sum = jnp.dot(
        columns,
        lax.all_gather(query_weight, "ctx", axis=0, tiled=True),
        preferred_element_type=jnp.float32,
    )
    queries = query_sum.astype(jnp.bfloat16).reshape(blocks_here, BLOCK, heads_count, head_size)
    stacked_keys = keys.reshape(blocks_here, BLOCK, head_size)
    stacked_values = values.reshape(blocks_here, BLOCK, head_size)
    spread_keys, spread_values = (
        lax.all_to_all(stacked_keys, "ctx", split_axis=1, concat_axis=0, tiled=True),
        lax.all_to_all(stacked_values, "ctx", split_axis=1, concat_axis=0, tiled=True),
    )
    send_keys = jnp.take(spread_keys, block_lists, axis=0).reshape(
        devices, listed_count, 1, piece_rows, head_size
    )
    send_values = jnp.take(spread_values, block_lists, axis=0).reshape(
        devices, listed_count, 1, piece_rows, head_size
    )
    got_keys, got_values = (
        lax.all_to_all(send_keys, "ctx", split_axis=0, concat_axis=2, tiled=True),
        lax.all_to_all(send_values, "ctx", split_axis=0, concat_axis=2, tiled=True),
    )
    listed_keys = got_keys.reshape(blocks_here, TOPK * BLOCK, head_size)
    listed_values = got_values.reshape(blocks_here, TOPK * BLOCK, head_size)
    near_keys = jnp.concatenate([listed_keys, stacked_keys], 1)
    near_values = jnp.concatenate([listed_values, stacked_values], 1)
    mine = first_block + jnp.arange(blocks_here, dtype=jnp.int32)
    mine_lists = lax.dynamic_slice_in_dim(block_lists, first_block, blocks_here, 0)
    flags = mine_lists < mine[:, None]
    offsets = jnp.arange(BLOCK, dtype=jnp.int32)
    causal = offsets[:, None] >= offsets[None, :]
    scale = 1.0 / math.sqrt(head_size)

    def one_block(inputs):
        block_queries, block_keys, block_values, block_flags = inputs
        listed = jnp.repeat(block_flags, BLOCK, total_repeat_length=TOPK * BLOCK)
        allowed = jnp.concatenate(
            [jnp.broadcast_to(listed[None, :], (BLOCK, TOPK * BLOCK)), causal], 1
        )

        def one_head(head_queries):
            scores = (
                jnp.einsum(
                    "qd,kd->qk", head_queries, block_keys, preferred_element_type=jnp.float32
                )
                * scale
            )
            scores = jnp.where(allowed, scores, -jnp.inf)
            peak = jnp.max(scores, axis=1, keepdims=True)
            weights_raw = jnp.exp(scores - peak)
            total = jnp.sum(weights_raw, axis=1, keepdims=True)
            mixed = (
                jnp.dot(
                    weights_raw.astype(jnp.bfloat16),
                    block_values,
                    preferred_element_type=jnp.float32,
                )
                / total
            )
            return mixed.astype(jnp.bfloat16)

        per_head = lax.map(one_head, jnp.transpose(block_queries, (1, 0, 2)))
        return jnp.transpose(per_head, (1, 0, 2)).reshape(BLOCK, heads_count * head_size)

    attention = lax.map(one_block, (queries, near_keys, near_values, flags)).reshape(
        tok_rows, heads_count * head_size
    )
    columns = attention
    output_sum = jnp.dot(
        columns,
        lax.all_gather(output_weight, "ctx", axis=0, tiled=True),
        preferred_element_type=jnp.float32,
    )
    return output_sum.astype(jnp.bfloat16)


def solution(mesh):
    in_specs = (
        P(("groups", "ctx"), None),
        P("ctx", None),
        P("ctx", None),
        P(("groups", "ctx"), None),
        P(("groups", "ctx"), None),
        P("groups", None),
    )
    out_specs = P(("groups", "ctx"), None)
    return jax.shard_map(
        per_device, mesh=mesh, in_specs=in_specs, out_specs=out_specs, check_vma=False
    )
```

profile of v0, /device:TPU:0, one launch (start us, length us, event | category | flops | bytes accessed | tf_op | source)
XLA Modules:
  0.0 199.1 jit_solution(12639631111675661174)
XLA Ops:
  8.0 1.1 copy.45
  9.7 1.4 reduce.3
  11.8 7.4 %all-to-all-start.2 = ((bf16[16,2,2048]{2,1,0:T(2,128)(2,1)}), bf16[16,2,2048]{2,1,0:T(2,128)(2,1)S(1)}, u32[]{:S(2)}, u32[]{:S(2)}) async-start(bf16[16,2,2048]{2,1,0:T(2,128)(2,1)} %reshape.196), calls=%async_computation.2 | async-start | bytes 262144 | tf_op jit(solution)/shard_map/all_to_all | solution.py:32
  20.1 1.1 copy.46
  21.2 1.4 reduce.4
  23.3 5.5 %all-to-all-done.2 = bf16[16,2,2048]{2,1,0:T(2,128)(2,1)S(1)} async-done(((bf16[16,2,2048]{2,1,0:T(2,128)(2,1)}), bf16[16,2,2048]{2,1,0:T(2,128)(2,1)S(1)}, u32[]{:S(2)}, u32[]{:S(2)}) %all-to-all-start.2) | async-done | bytes 131104 | tf_op jit(solution)/shard_map/all_to_all | solution.py:32
  28.9 4.6 %all-to-all-start = ((bf16[16,2,2048]{2,1,0:T(2,128)(2,1)}), bf16[16,2,2048]{2,1,0:T(2,128)(2,1)S(1)}, u32[]{:S(2)}, u32[]{:S(2)}) async-start(bf16[16,2,2048]{2,1,0:T(2,128)(2,1)} %reshape.194), calls=%async_computation | async-start | bytes 262144 | tf_op jit(solution)/shard_map/all_to_all | solution.py:31
  34.4 9.4 %all-to-all-done = bf16[16,2,2048]{2,1,0:T(2,128)(2,1)S(1)} async-done(((bf16[16,2,2048]{2,1,0:T(2,128)(2,1)}), bf16[16,2,2048]{2,1,0:T(2,128)(2,1)S(1)}, u32[]{:S(2)}, u32[]{:S(2)}) %all-to-all-start) | async-done | bytes 131104 | tf_op jit(solution)/shard_map/all_to_all | solution.py:31
  45.3 1.0 select_bitcast_fusion
  46.3 3.6 %all-to-all-start.3 = ((bf16[16,3,1,32,128]{4,3,1,2,0:T(8,128)(2,1)}), bf16[16,3,1,32,128]{4,3,1,2,0:T(8,128)(2,1)S(1)}, u32[]{:S(2)}, u32[]{:S(2)}) async-start(bf16[16,3,1,32,128]{4,3,1,2,0:T(8,128)(2,1)} %get-tuple-element.91), calls=%async_computation.3 | async-start | bytes 786432 | tf_op jit(solution)/shard_map/all_to_all | solution.py:42
  50.6 17.8 %all-to-all-done.3 = bf16[16,3,1,32,128]{4,3,1,2,0:T(8,128)(2,1)S(1)} async-done(((bf16[16,3,1,32,128]{4,3,1,2,0:T(8,128)(2,1)}), bf16[16,3,1,32,128]{4,3,1,2,0:T(8,128)(2,1)S(1)}, u32[]{:S(2)}, u32[]{:S(2)}) %all-to-all-start.3) | async-done | bytes 393248 | tf_op jit(solution)/shard_map/all_to_all | solution.py:42
  68.4 8.4 %all-to-all-start.1 = ((bf16[16,3,1,32,128]{4,3,1,2,0:T(8,128)(2,1)}), bf16[16,3,1,32,128]{4,3,1,2,0:T(8,128)(2,1)S(1)}, u32[]{:S(2)}, u32[]{:S(2)}) async-start(bf16[16,3,1,32,128]{4,3,1,2,0:T(8,128)(2,1)} %get-tuple-element.92), calls=%async_computation.1 | async-start | bytes 786432 | tf_op jit(solution)/shard_map/all_to_all | solution.py:41
  76.8 1.9 select_select_fusion
  79.3 16.4 %all-to-all-done.1 = bf16[16,3,1,32,128]{4,3,1,2,0:T(8,128)(2,1)S(1)} async-done(((bf16[16,3,1,32,128]{4,3,1,2,0:T(8,128)(2,1)}), bf16[16,3,1,32,128]{4,3,1,2,0:T(8,128)(2,1)S(1)}, u32[]{:S(2)}, u32[]{:S(2)}) %all-to-all-start.1) | async-done | bytes 393248 | tf_op jit(solution)/shard_map/all_to_all | solution.py:41
  95.8 10.3 %all-gather.3.cloned.1.call-done = bf16[4096,1024]{1,0:T(8,128)(2,1)} async-done(((bf16[256,1024]{1,0:T(8,128)(2,1)}), bf16[4096,1024]{1,0:T(8,128)(2,1)}) %all-gather.3.cloned.1.call-update) | async-done | bytes 8388624 | tf_op jit(solution)/shard_map/all_gather | solution.py:24
  106.1 9.1 %fusion.17 = bf16[64,8,8,128]{3,2,1,0:T(8,128)(2,1)S(1)} fusion(bf16[512,4096]{1,0:T(8,128)(2,1)} %param.12, bf16[4096,1024]{1,0:T(8,128)(2,1)} %all-gather.3.cloned.1.call-done), kind=kOutput, calls=%fused_computation.18 | convolution fusion | flops 4295491584 | bytes 13631488 | tf_op jit(solution)/shard_map/dot_general | solution.py:22
  115.4 26.0 %while.18 = (s32[]{:T(128)}, bf16[8,512,128]{1,2,0:T(8,128)(2,1)}, bf16[8,512,128]{2,1,0:T(8,128)(2,1)S(1)}, bf16[2048,128]{1,0:T(8,128)(2,1)S(1)}, pred[512,204...) while((s32[]{:T(128)}, bf16[8,512,128]{1,2,0:T(8,128)(2,1)}, ...), condition=%wide.region_3.5_spmd, body=%wide.region_0.4_spmd.sunk | while | flops 544340992 | bytes 15477329 | solution.py:83
  115.4 1.0 fusion.35
  118.7 0.9 fusion.35
  131.7 0.9 fusion.35
  135.0 1.0 fusion.35
  138.2 1.0 fusion.35
  141.5 40.5 %all-gather.5.cloned.1.call-done = bf16[1024,4096]{1,0:T(8,128)(2,1)} async-done(((bf16[64,4096]{1,0:T(8,128)(2,1)}), bf16[1024,4096]{1,0:T(8,128)(2,1)}) %all-gather.5.cloned.1.call-update) | async-done | bytes 8388624 | tf_op jit(solution)/shard_map/all_gather | solution.py:92
  182.0 10.3 %convolution_convert_fusion = bf16[512,4096]{1,0:T(8,128)(2,1)} fusion(bf16[512,1024]{0,1:T(8,128)(2,1)} %bitcast.82, bf16[1024,4096]{1,0:T(8,128)(2,1)} %all-gather.5.cloned.1.call-done), kind=kOutput, calls=%fused_computation.15 | convolution fusion | flops 4297064448 | bytes 13631488 | tf_op jit(solution)/shard_map/dot_general | solution.py:90
  (74 shorter events, 29.2 us)
Async XLA Ops:
  6.5 99.5 %all-gather.3.cloned.1.call-start = ((), (), s32[]{:S(2)}) async-start(), calls=%async_computation.4 | async-start | bytes 8912896 | tf_op jit(solution)/shard_map/all_gather | solution.py:24
  7.3 174.8 %all-gather.5.cloned.1.call-start = ((), (), s32[]{:S(2)}) async-start(), calls=%async_computation.5 | async-start | bytes 8912896 | tf_op jit(solution)/shard_map/all_gather | solution.py:92
  8.0 41.9 %copy-start.2 = (s32[16,3]{0,1:T(4,128)S(1)}, s32[16,3]{0,1:T(4,128)}, u32[]{:S(2)}) copy-start(s32[16,3]{0,1:T(4,128)} %param.17) | copy-start | bytes 580
  11.1 65.7 %copy-start.3 = (pred[1536]{0:T(1024)(128)(4,1)S(1)}, pred[1536]{0:T(1024)(128)(4,1)}, u32[]{:S(2)}) copy-start(pred[1536]{0:T(1024)(128)(4,1)} %constant.164) | copy-start | bytes 4612
  11.1 65.7 %copy-start.4 = (pred[1536]{0:T(1024)(128)(4,1)S(1)}, pred[1536]{0:T(1024)(128)(4,1)}, u32[]{:S(2)}) copy-start(pred[1536]{0:T(1024)(128)(4,1)} %constant.165) | copy-start | bytes 4612
  11.8 17.0 %all-to-all-start.2 = ((bf16[16,2,2048]{2,1,0:T(2,128)(2,1)}), bf16[16,2,2048]{2,1,0:T(2,128)(2,1)S(1)}, u32[]{:S(2)}, u32[]{:S(2)}) async-start(bf16[16,2,2048]{2,1,0:T(2,128)(2,1)} %reshape.196), calls=%async_computation.2 | async-start | bytes 262144 | tf_op jit(solution)/shard_map/all_to_all | solution.py:32
  28.9 15.0 %all-to-all-start = ((bf16[16,2,2048]{2,1,0:T(2,128)(2,1)}), bf16[16,2,2048]{2,1,0:T(2,128)(2,1)S(1)}, u32[]{:S(2)}, u32[]{:S(2)}) async-start(bf16[16,2,2048]{2,1,0:T(2,128)(2,1)} %reshape.194), calls=%async_computation | async-start | bytes 262144 | tf_op jit(solution)/shard_map/all_to_all | solution.py:31
  44.0 51.7 %copy-start = (bf16[512,128]{1,0:T(8,128)(2,1)S(1)}, bf16[512,128]{1,0:T(8,128)(2,1)}, u32[]{:S(2)}) copy-start(bf16[512,128]{1,0:T(8,128)(2,1)} %param.15) | copy-start | bytes 393220
  44.0 51.7 %copy-start.1 = (bf16[512,128]{1,0:T(8,128)(2,1)S(1)}, bf16[512,128]{1,0:T(8,128)(2,1)}, u32[]{:S(2)}) copy-start(bf16[512,128]{1,0:T(8,128)(2,1)} %param.16) | copy-start | bytes 393220
  46.3 22.0 %all-to-all-start.3 = ((bf16[16,3,1,32,128]{4,3,1,2,0:T(8,128)(2,1)}), bf16[16,3,1,32,128]{4,3,1,2,0:T(8,128)(2,1)S(1)}, u32[]{:S(2)}, u32[]{:S(2)}) async-start(bf16[16,3,1,32,128]{4,3,1,2,0:T(8,128)(2,1)} %get-tuple-element.91), calls=%async_computation.3 | async-start | bytes 786432 | tf_op jit(solution)/shard_map/all_to_all | solution.py:42
  68.4 27.3 %all-to-all-start.1 = ((bf16[16,3,1,32,128]{4,3,1,2,0:T(8,128)(2,1)}), bf16[16,3,1,32,128]{4,3,1,2,0:T(8,128)(2,1)S(1)}, u32[]{:S(2)}, u32[]{:S(2)}) async-start(bf16[16,3,1,32,128]{4,3,1,2,0:T(8,128)(2,1)} %get-tuple-element.92), calls=%async_computation.1 | async-start | bytes 786432 | tf_op jit(solution)/shard_map/all_to_all | solution.py:41
Sparse Core Ops, SparseCore 0:
  9.5 96.5 all-gather.2
  108.2 73.7 all-gather.4
where the time goes:
time: 200 us; the launch traced here: 199 us
  waiting for transfers between devices  101 us (50%)
  matrix products  33.4 us (17%)
  starting transfers between devices  24 us (12%)
  between operations  13.7 us (7%)
  other arithmetic  13.4 us (7%)
  local copies, waits for them, and re-layouts  13.2 us (7%)
    all_gather x1, waiting for transfers between devices, per_device(): lax.all_gather(output_weight, 'ctx', axis=0, tiled=True)  40.5 us
    all_to_all x1, waiting for transfers between devices, per_device(): lax.all_to_all(send_values, 'ctx', split_axis=0, concat_axis=2, tiled=True)  17.8 us
    all_to_all x1, waiting for transfers between devices, per_device(): lax.all_to_all(send_keys, 'ctx', split_axis=0, concat_axis=2, tiled=True)  16.4 us
    dot_general x1, matrix products, per_device(): jnp.dot(columns, lax.all_gather(output_weight, 'ctx', axis=0, tiled=True)...  10.3 us
    all_gather x1, waiting for transfers between devices, per_device(): lax.all_gather(query_weight, 'ctx', axis=0, tiled=True)  10.3 us
    all_to_all x1, waiting for transfers between devices, per_device(): lax.all_to_all(stacked_keys, 'ctx', split_axis=1, concat_axis=0, tiled=True)  9.41 us
    dot_general x1, matrix products, per_device(): jnp.dot(columns, lax.all_gather(query_weight, 'ctx', axis=0, tiled=True),...  9.14 us
    all_to_all x1, starting transfers between devices, per_device(): lax.all_to_all(send_keys, 'ctx', split_axis=0, concat_axis=2, tiled=True)  8.43 us
  transfers between devices with their start and end apart: 6, of which 6 were waited for; matrix products, arithmetic and copies ran while one was open for 25% of the time, Pallas kernels for 0%

commit v1 on v0

v1 whole, which is shorter than its diff:
```python
import functools
import math

import jax
import jax.numpy as jnp
from jax import lax
from jax.experimental import pallas as pl
from jax.experimental.pallas import tpu as pltpu
from jax.sharding import PartitionSpec as P

BLOCK = 512
TOPK = 3
RING_CHIPS = 8
MIB = 2**20
VMEM = 56 * MIB


def pack_kernel(plane_ref, weight_ref, keys_ref, values_ref, out_ref):
    depth, width = weight_ref.shape
    head_size = keys_ref.shape[1]
    out_ref[:, :width] = weight_ref[...]
    for i, rows in enumerate(range(0, keys_ref.shape[0], depth)):
        at = width + 2 * i * head_size
        out_ref[:, at : at + head_size] = keys_ref[rows : rows + depth, :]
        out_ref[:, at + head_size : at + 2 * head_size] = values_ref[rows : rows + depth, :]


def pack(plane, weight, keys, values):
    depth, width = weight.shape
    size, head_size = keys.shape
    wide = width // 2 + 2 * head_size * (size // depth)
    return pl.pallas_call(
        pack_kernel,
        grid_spec=pltpu.PrefetchScalarGridSpec(
            num_scalar_prefetch=1,
            grid=(1,),
            in_specs=[
                pl.BlockSpec((depth, width // 2), lambda i, plane: (0, plane[0])),
                pl.BlockSpec(keys.shape, lambda i, plane: (0, 0)),
                pl.BlockSpec(values.shape, lambda i, plane: (0, 0)),
            ],
            out_specs=pl.BlockSpec((depth, wide), lambda i, plane: (0, 0)),
        ),
        out_shape=jax.ShapeDtypeStruct((depth, wide), weight.dtype),
        compiler_params=pltpu.CompilerParams(vmem_limit_bytes=VMEM),
        name="pack",
    )(plane, weight, keys, values)


def query_half_kernel(count, *refs):
    hidden, rows, rest = refs[1 : 1 + count], refs[1 + count : 1 + 2 * count], refs[1 + 2 * count :]
    left = jnp.concatenate([h[...] for h in hidden], axis=1)
    right = jnp.concatenate([w[...] for w in rows], axis=0)
    total = jnp.dot(left, right, preferred_element_type=jnp.float32)
    if len(rest) == 2:
        total += rest[0][...]
    rest[-1][...] = total.astype(rest[-1].dtype)


def query_half(hidden, scalars, whole, pieces, depth, width, total, out_dtype):
    tokens = hidden.shape[0]
    count = len(whole) + len(pieces)
    step = 256
    steps = width // step

    def hidden_spec(i):
        return pl.BlockSpec((tokens, depth), lambda n, where: (0, where[1 + i]))

    def piece_spec(row):
        return pl.BlockSpec((depth, step), lambda n, where: (row, n))

    whole_spec = pl.BlockSpec((depth, step), lambda n, where: (0, steps * where[0] + n))
    out_spec = pl.BlockSpec((tokens, step), lambda n, where: (0, n))
    return pl.pallas_call(
        functools.partial(query_half_kernel, count),
        grid_spec=pltpu.PrefetchScalarGridSpec(
            num_scalar_prefetch=1,
            grid=(steps,),
            in_specs=[hidden_spec(i) for i in range(count)]
            + [whole_spec] * len(whole)
            + [piece_spec(row) for _, row in pieces]
            + ([out_spec] if total is not None else []),
            out_specs=out_spec,
        ),
        out_shape=jax.ShapeDtypeStruct((tokens, width), out_dtype),
        compiler_params=pltpu.CompilerParams(vmem_limit_bytes=VMEM),
        cost_estimate=pl.CostEstimate(
            flops=2 * tokens * depth * width * count,
            bytes_accessed=2 * count * depth * (tokens + width) + 8 * tokens * width,
            transcendentals=0,
        ),
        name="query_half",
    )(
        scalars,
        *([hidden] * count),
        *whole,
        *[array for array, _ in pieces],
        *([total] if total is not None else []),
    )


def pick_kernel(sources, depth, width, mine_ref, give_ref, *refs):
    held, out_ref, given_ref, sems = refs[:-3], refs[-3], refs[-2], refs[-1]
    listed = mine_ref.shape[0]
    _, size, both = out_ref.shape

    def copies(source, target, slot):
        ref, row = source
        return [
            pltpu.make_async_copy(
                held[ref].at[pl.ds(row * depth, depth), pl.ds(width + i * both, both)],
                target[0].at[target[1], pl.ds(i * depth, depth)],
                sems.at[slot, i],
            )
            for i in range(size // depth)
        ]

    targets = [(out_ref, j) for j in range(listed)] + [(given_ref, j) for j in range(listed)]
    for slot, target in enumerate(targets):
        index = (mine_ref if slot < listed else give_ref)[slot % listed]
        for s, source in enumerate(sources):

            @pl.when(index == s)
            def _(slot=slot, target=target, source=source):
                for copy in copies(source, target, slot):
                    copy.start()

    targets.append((out_ref, listed))
    for copy in copies(sources[0], targets[-1], 2 * listed):
        copy.start()
    for slot, target in enumerate(targets):
        for copy in copies(sources[0], target, slot):
            copy.wait()


def pick(mine, give, pieces, depth, width, size, both):
    listed = mine.shape[0]
    held, sources = [], []
    for array, row in pieces:
        known = [i for i, h in enumerate(held) if h is array]
        if not known:
            held.append(array)
        sources.append((known[0] if known else len(held) - 1, row))
    dtype = held[0].dtype
    return pl.pallas_call(
        functools.partial(pick_kernel, sources, depth, width),
        in_specs=[pl.BlockSpec(memory_space=pltpu.SMEM)] * 2
        + [pl.BlockSpec(memory_space=pl.ANY)] * len(held),
        out_specs=[pl.BlockSpec(memory_space=pltpu.VMEM)] * 2,
        out_shape=[
            jax.ShapeDtypeStruct((listed + 1, size, both), dtype),
            jax.ShapeDtypeStruct((listed, size, both), dtype),
        ],
        scratch_shapes=[pltpu.SemaphoreType.DMA((2 * listed + 1, size // depth))],
        compiler_params=pltpu.CompilerParams(vmem_limit_bytes=VMEM),
        name="pick",
    )(mine, give, *held)


def attend_kernel(factor, shared, bias_ref, swap_ref, *refs):
    if shared:
        q_own_ref, q_got_ref, near_ref, got_ref, o_ref, kv_ref, q_ref = refs
        listed = got_ref.shape[0]
        q_ref[...] = (q_own_ref[...] + q_got_ref[...]).astype(q_ref.dtype)
        kv_ref[listed] = near_ref[listed]
        for j in range(listed):

            @pl.when(swap_ref[j] == 0)
            def _(j=j):
                kv_ref[j] = near_ref[j]

            @pl.when(swap_ref[j] != 0)
            def _(j=j):
                kv_ref[j] = got_ref[j]

    else:
        q_ref, kv_ref, o_ref = refs
    blocks, size, both = kv_ref.shape
    hd, listed, tile = both // 2, blocks - 1, size // 2
    across = (((1,), (1,)), ((), ()))

    def score(head, part):
        q = q_ref[part * tile : (part + 1) * tile, head * hd : (head + 1) * hd]
        spans = [(j, size) for j in range(listed)] + [(listed, tile * (part + 1))]
        return [
            lax.dot_general(
                q, kv_ref[j, :seen, :hd], across, preferred_element_type=jnp.float32
            )
            for j, seen in spans
        ]

    def mix(head, part, scores):
        at_query = lax.broadcasted_iota(jnp.int32, scores[-1].shape, 0) + part * tile
        at_key = lax.broadcasted_iota(jnp.int32, scores[-1].shape, 1)
        scores = scores[:-1] + [jnp.where(at_query >= at_key, scores[-1], -jnp.inf)]
        bias = [bias_ref[j] for j in range(listed)] + [0.0]
        peak = functools.reduce(
            jnp.maximum,
            [jnp.max(s, axis=1, keepdims=True) - b for s, b in zip(scores, bias)],
        )
        weights = [jnp.exp2((s - (peak + b)) * factor) for s, b in zip(scores, bias)]
        total = sum(jnp.sum(w, axis=1, keepdims=True) for w in weights)
        mixed = sum(
            jnp.dot(
                w.astype(jnp.bfloat16),
                kv_ref[j, : w.shape[1], hd:],
                preferred_element_type=jnp.float32,
            )
            for j, w in enumerate(weights)
        )
        o_ref[part * tile : (part + 1) * tile, head * hd : (head + 1) * hd] = (
            mixed / total
        ).astype(o_ref.dtype)

    parts = [(head, part) for head in range(q_ref.shape[1] // hd) for part in range(2)]
    ahead = score(*parts[0])
    for i, part in enumerate(parts):
        scores = ahead
        if i + 1 < len(parts):
            ahead = score(*parts[i + 1])
        mix(*part, scores)


def attend(queries, near, bias, swapped):
    tokens, width = queries[0].shape
    blocks, size, both = near[0].shape
    hd = both // 2
    step = min(width, 4 * hd)
    work = tokens * blocks * size * (width // hd)
    shared = len(queries) == 2
    query_spec = pl.BlockSpec((tokens, step), lambda h: (0, h))
    scratch = [
        pltpu.VMEM(near[0].shape, near[0].dtype),
        pltpu.VMEM((tokens, step), jnp.bfloat16),
    ]
    return pl.pallas_call(
        functools.partial(attend_kernel, math.log2(math.e) / math.sqrt(hd), shared),
        grid=(width // step,),
        in_specs=[pl.BlockSpec(memory_space=pltpu.SMEM)] * 2
        + [query_spec] * len(queries)
        + [pl.BlockSpec(n.shape, lambda h: (0, 0, 0)) for n in near],
        out_specs=query_spec,
        out_shape=jax.ShapeDtypeStruct((tokens, width), jnp.bfloat16),
        scratch_shapes=scratch if shared else [],
        compiler_params=pltpu.CompilerParams(vmem_limit_bytes=VMEM),
        cost_estimate=pl.CostEstimate(
            flops=8 * work * hd, bytes_accessed=4 * MIB, transcendentals=work
        ),
        name="attend",
    )(bias, swapped, *queries, *near)


def project_kernel(parts, pieces, common, scalar_ref, *refs):
    attention, refs = refs[:parts], refs[parts:]
    whole, refs = refs[:1], refs[1:]
    mine, refs = refs[:pieces], refs[pieces:]
    crossed, (out_ref, weight_ref) = refs[:pieces], refs[pieces:]

    def place(rows):
        for i, piece in enumerate(rows):
            depth = piece.shape[0]
            start = pl.multiple_of(scalar_ref[2 + i] * depth, depth)
            weight_ref[pl.ds(start, depth), :] = piece[...]

    early = pl.program_id(0) < common
    pl.when(early)(lambda: place(whole + mine))
    pl.when(jnp.logical_not(early))(lambda: place(whole + crossed))
    left = jnp.concatenate([a[...] for a in attention], axis=1)
    total = jnp.dot(left, weight_ref[...], preferred_element_type=jnp.float32)
    out_ref[...] = total.astype(out_ref.dtype)


def project(attention, scalars, whole, mine, crossed, wide):
    tokens = attention[0].shape[0]
    depth, width = whole.shape
    rows = depth * (1 + len(mine))
    step = 512
    steps = width // step
    near = mine[0][0].shape[1] // step
    part = steps - near
    common = near - part

    def column(n, where):
        return jnp.where(n < common, n, common + lax.rem(n - common + part * where[0], 2 * part))

    def near_spec(row):
        return pl.BlockSpec((depth, step), lambda n, where: (row, jnp.minimum(n, near - 1)))

    def crossed_spec(row):
        return pl.BlockSpec((depth, step), lambda n, where: (row, jnp.maximum(n - near, 0)))

    def out_column(n, where):
        return column(n, where) + (steps * where[1] if wide else 0)

    return pl.pallas_call(
        functools.partial(project_kernel, len(attention), len(mine), near),
        grid_spec=pltpu.PrefetchScalarGridSpec(
            num_scalar_prefetch=1,
            grid=(steps,),
            in_specs=[pl.BlockSpec(a.shape, lambda n, where: (0, 0)) for a in attention]
            + [pl.BlockSpec((depth, step), lambda n, where: (0, column(n, where)))]
            + [near_spec(row) for _, row in mine]
            + [crossed_spec(row) for _, row in crossed],
            out_specs=pl.BlockSpec((tokens, step), lambda n, where: (0, out_column(n, where))),
            scratch_shapes=[pltpu.VMEM((rows, step), whole.dtype)],
        ),
        out_shape=jax.ShapeDtypeStruct((tokens, 2 * width if wide else width), whole.dtype),
        compiler_params=pltpu.CompilerParams(vmem_limit_bytes=VMEM),
        cost_estimate=pl.CostEstimate(
            flops=2 * tokens * rows * width,
            bytes_accessed=2 * (rows + tokens) * width + 2 * tokens * rows,
            transcendentals=0,
        ),
        name="project",
    )(
        scalars,
        *attention,
        whole,
        *[array for array, _ in mine],
        *[array for array, _ in crossed],
    )


def fill_kernel(half_ref, into_ref, got_ref, out_ref):
    out_ref[...] = got_ref[...]


def fill(half, into, got):
    tokens, width = got.shape
    step = 512
    steps = width // step
    return pl.pallas_call(
        fill_kernel,
        grid_spec=pltpu.PrefetchScalarGridSpec(
            num_scalar_prefetch=1,
            grid=(steps,),
            in_specs=[
                pl.BlockSpec(memory_space=pl.ANY),
                pl.BlockSpec((tokens, step), lambda n, half: (0, n)),
            ],
            out_specs=pl.BlockSpec((tokens, step), lambda n, half: (0, n + steps * half[0])),
        ),
        out_shape=jax.ShapeDtypeStruct(into.shape, into.dtype),
        input_output_aliases={1: 0},
        compiler_params=pltpu.CompilerParams(vmem_limit_bytes=VMEM),
        name="fill",
    )(half, into, got)


def ring_device(hidden_states, query_weight, output_weight, keys, values, block_lists):
    devices = lax.axis_size("ctx")
    chips = devices // 2
    half = chips // 2
    ring = list(range(0, chips, 2)) + list(range(chips - 1, 0, -2))
    at = {chip: i for i, chip in enumerate(ring)}
    depth, width = query_weight.shape
    size, head_size = keys.shape

    def pairs(step):
        return [
            (2 * p + c, 2 * ring[(at[p] + step) % chips] + c) for p in range(chips) for c in (0, 1)
        ]

    ahead, back = pairs(1), pairs(-1)

    def send(array, to):
        return lax.ppermute(array, "ctx", to)

    def swap(array):
        return send(array, [(d, d ^ 1) for d in range(devices)])

    def cross(array):
        return lax.ppermute(array, "groups", [(0, 1), (1, 0)])

    def held_back(array, *until):
        return lax.optimization_barrier((array, *until))[0]

    distances = [0] + [d for s in range(1, half) for d in (-s, s)] + [half]
    me, plane = lax.axis_index("ctx"), lax.axis_index("groups")
    chip, core = me // 2, me % 2
    here = jnp.where(chip % 2 == 0, chip // 2, chips - 1 - chip // 2)
    order = (here + jnp.asarray(distances, jnp.int32) + chips) % chips
    order = jnp.where(order < half, 2 * order, 2 * (chips - 1 - order) + 1)
    lists = lax.dynamic_slice_in_dim(block_lists, 2 * chip, 2, 0)
    lists = jnp.stack([lists[core], lists[1 - core]])
    bias = jnp.where(lists[0] < me, 0.0, jnp.inf).astype(jnp.float32)
    swapped = (lists[0] % 2 != core).astype(jnp.int32)
    held_at = jnp.argmax(order == lists[:, :, None] // 2, axis=2).astype(jnp.int32)
    plane = jnp.reshape(plane, (1,)).astype(jnp.int32)
    places = 2 * order + core

    def walk(own, crossing, after, meanwhile):
        near, crossed = {}, {}
        down, up = held_back(own, *after), held_back(own, *after)
        cut = own.shape[0] // 2
        behind = []
        for step in range(1, half + 1):
            if step == half:
                down, up = down[:cut], up[cut:]
            down, up = send(down, ahead), send(up, back)
            over = cross(jnp.concatenate([down[:, crossing], up[:, crossing]], 0))
            if step < half:
                near[-step], near[step] = (down, 0), (up, 0)
                crossed[-step], crossed[step] = (over, 0), (over, 1)
                wait = behind + meanwhile.get(step, lambda *_: [])(near, crossed)
                behind = [over]
                if wait:
                    down, up = held_back(down, *wait), held_back(up, *wait)
            else:
                near[half] = (jnp.concatenate([down, up], 0), 0)
                crossed[half] = (over, 0)
        return near, crossed, [down, up]

    def part(which, found, first, last, totals):
        picks = [i for i, d in enumerate(distances) if first <= abs(d) <= last]
        scalars = jnp.stack([which[0]] + [places[i] for i in picks])
        return [
            query_half(
                hidden,
                scalars,
                (query_weight,) if first == 0 else (),
                [found[distances[i]] for i in picks if i],
                depth,
                width // 2,
                total,
                jnp.float32,
            )
            for hidden, total in zip((hidden_other, hidden_states), totals)
        ]

    hidden_other = swap(hidden_states)
    own = pack(plane, query_weight, keys, values)
    sums = {}

    def first_part(near, crossed):
        sums["near"] = part(plane, near, 0, half - 2, (None, None))
        return sums["near"]

    near, crossed, last = walk(own, slice(0, width // 2), [], {half - 1: first_part})
    held = [(own, 0)] + [near[d] for d in distances[1:]]
    picked, given = pick(held_at[0], held_at[1], held, depth, width // 2, size, 2 * head_size)
    picked = (picked, swap(given))
    query = {"near": near, "crossed": crossed}
    attention = []

    def heads(which, kind):
        other, mine = part(which, query[kind], half - 1, half, sums[kind])
        attention.append(attend((mine, swap(other)), picked, bias, swapped))
        return attention[-1:]

    def rest(*_):
        sums["crossed"] = part(1 - plane, query["crossed"], 0, half - 2, (None, None))
        return sums["crossed"]

    columns = output_weight.shape[1] // 2
    share = columns // 4
    kept = lax.dynamic_slice_in_dim(output_weight, columns * core, columns, 1)
    got = swap(lax.dynamic_slice_in_dim(output_weight, columns * (1 - core), columns, 1))
    whole = jnp.concatenate([jnp.where(core == 0, kept, got), jnp.where(core == 0, got, kept)], 0)
    own = jnp.concatenate(
        [
            whole[:, : columns - 2 * share],
            lax.dynamic_slice_in_dim(whole, columns - 2 * share + share * plane[0], share, 1),
        ],
        1,
    )
    work = {
        1: rest,
        half - 2: lambda *_: heads(plane, "near"),
        half - 1: lambda *_: heads(1 - plane, "crossed"),
    }
    near, crossed, _ = walk(own, slice(columns - 2 * share, columns - share), last, work)
    scalars = jnp.concatenate([plane, core[None], (order + half * plane) % chips])
    pieces = (whole, [near[d] for d in distances[1:]], [crossed[d] for d in distances[1:]])
    theirs = project([swap(a) for a in attention], scalars, *pieces, False)
    ours = project(attention, scalars, *pieces, True)
    return fill(1 - core[None], ours, swap(theirs))


def per_device(hidden_states, query_weight, output_weight, keys, values, block_lists):
    devices = lax.axis_size("ctx")
    head_size = keys.shape[1]
    piece_rows = BLOCK // devices
    me = lax.axis_index("ctx")
    total = jnp.dot(
        hidden_states,
        lax.all_gather(query_weight, "ctx", axis=0, tiled=True),
        preferred_element_type=jnp.float32,
    )
    queries = total.astype(jnp.bfloat16)
    near = jnp.concatenate([keys, values], 1)
    spread = lax.all_to_all(near[None], "ctx", split_axis=1, concat_axis=0, tiled=True)
    listed = jnp.take(spread, block_lists, axis=0).reshape(
        devices, TOPK, piece_rows, 2 * head_size
    )
    got = lax.all_to_all(listed, "ctx", split_axis=0, concat_axis=2, tiled=True)
    picked = jnp.concatenate([got.reshape(TOPK, BLOCK, 2 * head_size), near[None]], 0)
    mine = lax.dynamic_index_in_dim(block_lists, me, 0, keepdims=False)
    bias = jnp.where(mine < me, 0.0, jnp.inf).astype(jnp.float32)
    attention = attend((queries,), (picked,), bias, jnp.zeros_like(mine))
    projected = jnp.dot(
        attention,
        lax.all_gather(output_weight, "ctx", axis=0, tiled=True),
        preferred_element_type=jnp.float32,
    )
    return projected.astype(jnp.bfloat16)


def solution(mesh):
    in_specs = (
        P(("groups", "ctx"), None),
        P("ctx", None),
        P("ctx", None),
        P(("groups", "ctx"), None),
        P(("groups", "ctx"), None),
        P("groups", None),
    )
    out_specs = P(("groups", "ctx"), None)
    step_by_step = mesh.shape["ctx"] <= 2 * RING_CHIPS and mesh.shape["groups"] == 2
    return jax.shard_map(
        ring_device if step_by_step else per_device,
        mesh=mesh,
        in_specs=in_specs,
        out_specs=out_specs,
        check_vma=False,
    )
```

time: 200 us -> 159 us (0.80)
  Pallas kernels: 0 us -> 75.3 us
  waiting for transfers between devices: 101 us -> 38.1 us
  matrix products: 33.4 us -> 0 us
  between operations: 13.7 us -> 0.58 us
  other arithmetic: 13.4 us -> 6.75 us
  starting transfers between devices: 24 us -> 27.4 us
  local copies, waits for them, and re-layouts: 13.2 us -> 10.2 us
    pallas_call x0 -> x15, Pallas kernels: none -> 75.3 us  [the longest x8 32.7 us: query_half(): pl.pallas_call(functools.partial(query_half_kernel, count), grid_spec=plt...]
    all_gather x2 -> x0, waiting for transfers between devices: 50.8 us -> none  [the longest x1 40.5 us: per_device(): lax.all_gather(output_weight, 'ctx', axis=0, tiled=True)]
    all_to_all x4 -> x0, waiting for transfers between devices: 49.1 us -> none  [the longest x1 17.8 us: per_device(): lax.all_to_all(send_values, 'ctx', split_axis=0, concat_axis=2, tiled=True)]
    ppermute x0 -> x32, waiting for transfers between devices: none -> 38.1 us  [the longest x24 30.9 us: send(): return lax.ppermute(array, 'ctx', to)]
    dot_general x18 -> x0, matrix products: 33.4 us -> none  [the longest x1 10.3 us: per_device(): jnp.dot(columns, lax.all_gather(output_weight, 'ctx', axis=0, tiled=True)...]
    ppermute x0 -> x32, starting transfers between devices: none -> 27.4 us  [the longest x24 19.2 us: send(): return lax.ppermute(array, 'ctx', to)]
    all_to_all x4 -> x0, starting transfers between devices: 24 us -> none  [the longest x1 8.43 us: per_device(): lax.all_to_all(send_keys, 'ctx', split_axis=0, concat_axis=2, tiled=True)]
    dynamic_update_slice x16 -> x0, local copies, waits for them, and re-layouts: 6.27 us -> none  [one_block(): per_head = lax.map(one_head, jnp.transpose(block_queries, (1, 0, 2)))]
  transfers between devices with their start and end apart: 6 -> 32, of which waited for: 6 -> 10; matrix products, arithmetic and copies ran while one was open for 25% -> 7% of each run, Pallas kernels for 0% -> 40%
where the time goes in v1:
time: 159 us; the launch traced here: 158 us
  Pallas kernels  75.3 us (47%)
  waiting for transfers between devices  38.1 us (24%)
  starting transfers between devices  27.4 us (17%)
  local copies, waits for them, and re-layouts  10.2 us (6%)
  other arithmetic  6.75 us (4%)
    pallas_call x8, Pallas kernels, query_half(): pl.pallas_call(functools.partial(query_half_kernel, count), grid_spec=plt...  32.7 us
    ppermute x24, waiting for transfers between devices, send(): return lax.ppermute(array, 'ctx', to)  30.9 us
    ppermute x24, starting transfers between devices, send(): return lax.ppermute(array, 'ctx', to)  19.2 us
    pallas_call x2, Pallas kernels, attend(): pl.pallas_call(functools.partial(attend_kernel, math.log2(math.e) / math....  18.3 us
    pallas_call x2, Pallas kernels, project(): pl.pallas_call(functools.partial(project_kernel, len(attention), len(mine...  14.8 us
    ppermute x8, starting transfers between devices, cross(): return lax.ppermute(array, 'groups', [(0, 1), (1, 0)])  8.24 us
    ppermute x8, waiting for transfers between devices, cross(): return lax.ppermute(array, 'groups', [(0, 1), (1, 0)])  7.16 us
    unnamed x62, local copies, waits for them, and re-layouts  6.5 us
  transfers between devices with their start and end apart: 32, of which 10 were waited for; matrix products, arithmetic and copies ran while one was open for 7% of the time, Pallas kernels for 40%

profile of v1, /device:TPU:0, one launch (start us, length us, event | category | flops | bytes accessed | tf_op | source)
XLA Modules:
  0.0 158.3 jit_solution(6428329149173930836)
XLA Ops:
  0.5 1.9 %pack.1.refs_0_ = bf16[256,1024]{1,0:T(8,128)(2,1)} custom-call(s32[1]{0:T(128)} %bitcast.1.plane_ref, bf16[256,1024]{1,0:T(8,128)(2,1)} %refs_6_.7, bf16[512,128]{1,0:T(8,128)(2,1)} %keys_ref.1, bf16[512,128]{1,0:T(8,128)(2,1)} %values_ref.1), custom_call_target="tpu_custom_call" | custom-call | tf_op jit(solution)/shard_map/pack/pallas_call | solution.py:32
  2.4 2.6 %collective-permute-start = (bf16[256,1024]{1,0:T(8,128)(2,1)}, bf16[256,1024]{1,0:T(8,128)(2,1)S(1)}, u32[]{:S(2)}, u32[]{:S(2)}) collective-permute-start(bf16[256,1024]{1,0:T(8,128)(2,1)} %pack.1.refs_0_), channel_id=1, source_target_pairs={{0,4},{1,5},{2,0},{3,1},{4,8},{5,9},{6,2},{7,3},{8,12},{9,13},{10,... | collective-permute-start | bytes 1572872 | tf_op jit(solution)/shard_map/ppermute | solution.py:367
  8.5 10.7 %collective-permute-done.2.refs_8_.refs_2_ = bf16[256,1024]{1,0:T(8,128)(2,1)S(1)} collective-permute-done((bf16[256,1024]{1,0:T(8,128)(2,1)}, bf16[256,1024]{1,0:T(8,128)(2,1)S(1)}, u32[]{:S(2)}, u32[]{:S(2)}) %collective-permute-start.2) | collective-permute-done | bytes 524320 | tf_op jit(solution)/shard_map/ppermute | solution.py:367
  25.9 8.7 %collective-permute-done.1.refs_9_.refs_3_ = bf16[256,1024]{1,0:T(8,128)(2,1)S(1)} collective-permute-done((bf16[256,1024]{1,0:T(8,128)(2,1)S(1)}, bf16[256,1024]{1,0:T(8,128)(2,1)S(1)}, u32[]{:S(2)}, u32[]{:S(2)}) %collective-permute-start.1) | collective-permute-done | bytes 524320 | tf_op jit(solution)/shard_map/ppermute | solution.py:367
  37.6 4.3 %query_half.9.refs_7_ = f32[512,512]{1,0:T(8,128)} custom-call(s32[6]{0:T(128)} %get-tuple-element.43.refs_0_, bf16[512,4096]{1,0:T(8,128)(2,1)} %refs_3_.7, bf16[512,4096]{1,0:T(8,128)(2,1)} %refs_3_.7, bf16[512,4096]{1,0:T(8,128)(2,1)} %refs_3_.7, bf16[512,4096]{1,0:T(8,128)(2,1)} %refs_3_.7, bf16[512,4096]{1,0:T(8,128)(2,1)} %refs_3_.7, ...), custom_call_target="tpu_custom_call" | custom-call | flops 671088640 | bytes 4718592 | tf_op jit(solution)/shard_map/query_half/pallas_call | solution.py:74
  41.9 4.4 %query_half.8.refs_7_ = f32[512,512]{1,0:T(8,128)} custom-call(s32[6]{0:T(128)} %get-tuple-element.43.refs_0_, bf16[512,4096]{1,0:T(8,128)(2,1)} %collective-permute-done.8.refs_1_.refs_2_.refs_3_.refs_4_.refs_5_, bf16[512,4096]{1,0:T(8,128)(2,1)} %collective-permute-done.8.refs_1_.refs_2_.refs_3_.refs_4_.refs_5_, ...), custom_call_target="tpu_custom_call" | custom-call | flops 671088640 | bytes 4718592 | tf_op jit(solution)/shard_map/query_half/pallas_call | solution.py:74
  51.4 3.8 %collective-permute-done.9 = bf16[128,1024]{1,0:T(8,128)(2,1)S(1)} collective-permute-done((bf16[128,1024]{1,0:T(8,128)(2,1)S(1)}, bf16[128,1024]{1,0:T(8,128)(2,1)S(1)}, u32[]{:S(2)}, u32[]{:S(2)}) %collective-permute-start.9) | collective-permute-done | bytes 262176 | tf_op jit(solution)/shard_map/ppermute | solution.py:367
  55.2 2.0 %collective-permute-done.10 = bf16[128,1024]{1,0:T(8,128)(2,1)S(1)} collective-permute-done((bf16[128,1024]{1,0:T(8,128)(2,1)S(1)}, bf16[128,1024]{1,0:T(8,128)(2,1)S(1)}, u32[]{:S(2)}, u32[]{:S(2)}) %collective-permute-start.10) | collective-permute-done | bytes 262176 | tf_op jit(solution)/shard_map/ppermute | solution.py:367
  60.1 3.8 %query_half.11 = f32[512,512]{1,0:T(8,128)} custom-call(s32[4]{0:T(128)} %get-tuple-element.45.refs_0_, bf16[512,4096]{1,0:T(8,128)(2,1)} %collective-permute-done.8.refs_1_.refs_2_.refs_3_.refs_4_.refs_5_, bf16[512,4096]{1,0:T(8,128)(2,1)} %collective-permute-done.8.refs_1_.refs_2_.refs_3_.refs_4_.refs_5_, ...), custom_call_target="tpu_custom_call" | custom-call | flops 402653184 | bytes 3670016 | tf_op jit(solution)/shard_map/query_half/pallas_call | solution.py:74
  65.6 3.8 %pick.1 = (bf16[4,512,256]{2,1,0:T(8,128)(2,1)}, bf16[3,512,256]{2,1,0:T(8,128)(2,1)}) custom-call(s32[3]{0:T(128)} %get-tuple-element.34.mine_ref, s32[3]{0:T(128)} %get-tuple-element.33.give_ref, bf16[256,1024]{1,0:T(8,128)(2,1)} %pack.1.refs_0_, bf16[256,1024]{1,0:T(8,128)(2,1)} %copy-done.5, bf16[256,1024]{1,0:T(8,128)(2,1)} %copy-done.6, ...), custom_call_target="tpu_custom_call" | custom-call | tf_op jit(solution)/shard_map/pick/pallas_call | solution.py:145
  69.7 4.3 %query_half.14.refs_7_ = f32[512,512]{1,0:T(8,128)} custom-call(s32[6]{0:T(128)} %get-tuple-element.42.refs_0_, bf16[512,4096]{1,0:T(8,128)(2,1)} %collective-permute-done.8.refs_1_.refs_2_.refs_3_.refs_4_.refs_5_, bf16[512,4096]{1,0:T(8,128)(2,1)} %collective-permute-done.8.refs_1_.refs_2_.refs_3_.refs_4_.refs_5_, ...), custom_call_target="tpu_custom_call" | custom-call | flops 671088640 | bytes 4718592 | tf_op jit(solution)/shard_map/query_half/pallas_call | solution.py:74
  74.8 3.8 %query_half.15 = f32[512,512]{1,0:T(8,128)} custom-call(s32[4]{0:T(128)} %get-tuple-element.44.refs_0_, bf16[512,4096]{1,0:T(8,128)(2,1)} %collective-permute-done.8.refs_1_.refs_2_.refs_3_.refs_4_.refs_5_, bf16[512,4096]{1,0:T(8,128)(2,1)} %collective-permute-done.8.refs_1_.refs_2_.refs_3_.refs_4_.refs_5_, ...), custom_call_target="tpu_custom_call" | custom-call | flops 402653184 | bytes 3670016 | tf_op jit(solution)/shard_map/query_half/pallas_call | solution.py:74
  79.6 4.3 %query_half.12.refs_7_ = f32[512,512]{1,0:T(8,128)} custom-call(s32[6]{0:T(128)} %get-tuple-element.42.refs_0_, bf16[512,4096]{1,0:T(8,128)(2,1)} %refs_3_.7, bf16[512,4096]{1,0:T(8,128)(2,1)} %refs_3_.7, bf16[512,4096]{1,0:T(8,128)(2,1)} %refs_3_.7, bf16[512,4096]{1,0:T(8,128)(2,1)} %refs_3_.7, bf16[512,4096]{1,0:T(8,128)(2,1)} %refs_3_.7, ...), custom_call_target="tpu_custom_call" | custom-call | flops 671088640 | bytes 4718592 | tf_op jit(solution)/shard_map/query_half/pallas_call | solution.py:74
  83.9 2.3 %collective-permute-start.19 = (bf16[128,1536]{1,0:T(8,128)(2,1)S(1)}, bf16[128,1536]{1,0:T(8,128)(2,1)S(1)}, u32[]{:S(2)}, u32[]{:S(2)}) collective-permute-start(bf16[128,1536]{1,0:T(8,128)(2,1)S(1)} %collective-permute-done.17.refs_3_), channel_id=1, source_target_pairs={{0,4},{1,5},{2,0},{3,1},{4,8},{5,9},{6,2},{7,3},{8,12},{9,13},{10,... | collective-permute-start | bytes 1179656 | tf_op jit(solution)/shard_map/ppermute | solution.py:367
  86.8 3.9 %query_half.10.refs_0_ = f32[512,512]{1,0:T(8,128)} custom-call(s32[4]{0:T(128)} %get-tuple-element.45.refs_0_, bf16[512,4096]{1,0:T(8,128)(2,1)} %refs_3_.7, bf16[512,4096]{1,0:T(8,128)(2,1)} %refs_3_.7, bf16[512,4096]{1,0:T(8,128)(2,1)} %refs_3_.7, bf16[256,1024]{1,0:T(8,128)(2,1)} %copy-done.1, bf16[256,1024]{1,0:T(8,128)(2,1)} %copy-done.2, ...), custom_call_target="tpu_custom_call" | custom-call | flops 402653184 | bytes 3670016 | tf_op jit(solution)/shard_map/query_half/pallas_call | solution.py:74
  90.6 3.9 %query_half.13.refs_0_ = f32[512,512]{1,0:T(8,128)} custom-call(s32[4]{0:T(128)} %get-tuple-element.44.refs_0_, bf16[512,4096]{1,0:T(8,128)(2,1)} %refs_3_.7, bf16[512,4096]{1,0:T(8,128)(2,1)} %refs_3_.7, bf16[512,4096]{1,0:T(8,128)(2,1)} %refs_3_.7, bf16[512,512]{1,0:T(8,128)(2,1)} %copy-done.4, bf16[512,512]{1,0:T(8,128)(2,1)} %copy-done.4, ...), custom_call_target="tpu_custom_call" | custom-call | flops 402653184 | bytes 3670016 | tf_op jit(solution)/shard_map/query_half/pallas_call | solution.py:74
  94.6 2.8 %collective-permute-done.20.refs_6_ = bf16[128,1536]{1,0:T(8,128)(2,1)S(1)} collective-permute-done((bf16[128,1536]{1,0:T(8,128)(2,1)S(1)}, bf16[128,1536]{1,0:T(8,128)(2,1)S(1)}, u32[]{:S(2)}, u32[]{:S(2)}) %collective-permute-start.20) | collective-permute-done | bytes 393248 | tf_op jit(solution)/shard_map/ppermute | solution.py:367
  100.8 9.1 %attend.2.refs_0_ = bf16[512,512]{1,0:T(8,128)(2,1)} custom-call(f32[3]{0:T(128)} %compare_select_fusion.6.bias_ref, s32[3]{0:T(128)} %compare_convert_fusion.swap_ref, f32[512,512]{1,0:T(8,128)} %query_half.10.refs_0_, f32[512,512]{1,0:T(8,128)} %copy-done.27, bf16[4,512,256]{2,1,0:T(8,128)(2,1)} %get-tuple-element.24.refs_2_, bf16[3,512,256]{2,1,0:T(8,128)(2,1)} %copy-done.29), custom_call_target="tpu_custom_call" | custom-call | flops 4294967296 | bytes 4194304 | tf_op jit(solution)/shard_map/attend/pallas_call | solution.py:236
  113.0 9.1 %attend.3.refs_1_ = bf16[512,512]{1,0:T(8,128)(2,1)} custom-call(f32[3]{0:T(128)} %compare_select_fusion.6.bias_ref, s32[3]{0:T(128)} %compare_convert_fusion.swap_ref, f32[512,512]{1,0:T(8,128)} %query_half.13.refs_0_, f32[512,512]{1,0:T(8,128)} %copy-done.28, bf16[4,512,256]{2,1,0:T(8,128)(2,1)} %get-tuple-element.24.refs_2_, bf16[3,512,256]{2,1,0:T(8,128)(2,1)} %copy-done.29), custom_call_target="tpu_custom_call" | custom-call | flops 4294967296 | bytes 4194304 | tf_op jit(solution)/shard_map/attend/pallas_call | solution.py:236
  127.3 2.5 %collective-permute-done.26 = bf16[64,1536]{1,0:T(8,128)(2,1)S(1)} collective-permute-done((bf16[64,1536]{1,0:T(8,128)(2,1)S(1)}, bf16[64,1536]{1,0:T(8,128)(2,1)S(1)}, u32[]{:S(2)}, u32[]{:S(2)}) %collective-permute-start.26) | collective-permute-done | bytes 196640 | tf_op jit(solution)/shard_map/ppermute | solution.py:367
  131.3 3.7 %collective-permute-done.27.refs_14_.refs_15_ = bf16[256,512]{1,0:T(8,128)(2,1)S(1)} collective-permute-done((bf16[256,512]{1,0:T(8,128)(2,1)S(1)}, bf16[256,512]{1,0:T(8,128)(2,1)S(1)}, u32[]{:S(2)}, u32[]{:S(2)}) %collective-permute-start.27) | collective-permute-done | bytes 262176 | tf_op jit(solution)/shard_map/ppermute | solution.py:373
  138.3 7.4 %project.3 = bf16[512,2048]{1,0:T(8,128)(2,1)} custom-call(s32[10]{0:T(128)} %pad_add_fusion.1.scalar_ref, bf16[512,512]{1,0:T(8,128)(2,1)} %copy-done.25, bf16[512,512]{1,0:T(8,128)(2,1)} %copy-done.26, bf16[128,2048]{1,0:T(8,128)(2,1)} %pad_maximum_fusion.refs_2_, bf16[128,1536]{1,0:T(8,128)(2,1)} %copy-done.16, bf16[128,1536]{1,0:T(8,128)(2,1)} %copy-done.17, ...), custom_call_target="tpu_custom_call" | custom-call | flops 2147483648 | bytes 7340032 | tf_op jit(solution)/shard_map/project/pallas_call | solution.py:295
  145.8 7.4 %project.2.into_ref = bf16[512,4096]{1,0:T(8,128)(2,1)} custom-call(s32[10]{0:T(128)} %pad_add_fusion.1.scalar_ref, bf16[512,512]{1,0:T(8,128)(2,1)} %attend.2.refs_0_, bf16[512,512]{1,0:T(8,128)(2,1)} %attend.3.refs_1_, bf16[128,2048]{1,0:T(8,128)(2,1)} %pad_maximum_fusion.refs_2_, bf16[128,1536]{1,0:T(8,128)(2,1)} %copy-done.16, ...), custom_call_target="tpu_custom_call" | custom-call | flops 2147483648 | bytes 7340032 | tf_op jit(solution)/shard_map/project/pallas_call | solution.py:295
  154.5 3.8 %fill.1 = bf16[512,4096]{1,0:T(8,128)(2,1)} custom-call(s32[1]{0:T(128)S(6)} %sub.29.half_ref, bf16[512,4096]{1,0:T(8,128)(2,1)} %project.2.into_ref, bf16[512,2048]{1,0:T(8,128)(2,1)} %copy-done.20), custom_call_target="tpu_custom_call", output_to_operand_aliasing={{}: (1, {})} | custom-call | tf_op jit(solution)/shard_map/fill/pallas_call | solution.py:332
  (165 shorter events, 43.4 us)
Async XLA Ops:
  0.0 41.9 %collective-permute-start.8 = (bf16[512,4096]{1,0:T(8,128)(2,1)}, bf16[512,4096]{1,0:T(8,128)(2,1)}, u32[]{:S(2)}, u32[]{:S(2)}) collective-permute-start(bf16[512,4096]{1,0:T(8,128)(2,1)} %refs_3_.7), channel_id=1, source_target_pairs={{0,1},{1,0},{2,3},{3,2},{4,5},{5,4},{6,7},{7,6},{8,9},{9,8},{10,11... | collective-permute-start | bytes 12582920 | tf_op jit(solution)/shard_map/ppermute | solution.py:367
  2.4 16.9 %collective-permute-start = (bf16[256,1024]{1,0:T(8,128)(2,1)}, bf16[256,1024]{1,0:T(8,128)(2,1)S(1)}, u32[]{:S(2)}, u32[]{:S(2)}) collective-permute-start(bf16[256,1024]{1,0:T(8,128)(2,1)} %pack.1.refs_0_), channel_id=1, source_target_pairs={{0,4},{1,5},{2,0},{3,1},{4,8},{5,9},{6,2},{7,3},{8,12},{9,13},{10,... | collective-permute-start | bytes 1572872 | tf_op jit(solution)/shard_map/ppermute | solution.py:367
  5.0 14.2 %collective-permute-start.2 = (bf16[256,1024]{1,0:T(8,128)(2,1)}, bf16[256,1024]{1,0:T(8,128)(2,1)S(1)}, u32[]{:S(2)}, u32[]{:S(2)}) collective-permute-start(bf16[256,1024]{1,0:T(8,128)(2,1)} %pack.1.refs_0_), channel_id=1, source_target_pairs={{0,2},{1,3},{2,6},{3,7},{4,0},{5,1},{6,10},{7,11},{8,4},{9,5},{10,... | collective-permute-start | bytes 1572872 | tf_op jit(solution)/shard_map/ppermute | solution.py:367
  6.7 30.7 %collective-permute-start.16 = (bf16[64,2048]{1,0:T(8,128)(2,1)}, bf16[64,2048]{1,0:T(8,128)(2,1)S(1)}, u32[]{:S(2)}, u32[]{:S(2)}) collective-permute-start(bf16[64,2048]{1,0:T(8,128)(2,1)} %constant_dynamic-slice_fusion), channel_id=1, source_target_pairs={{0,1},{1,0},{2,3},{3,2},{4,5},{5,4},{6,7},{7,6},{8,9},{9,8},{10,11... | collective-permute-start | bytes 786440 | tf_op jit(solution)/shard_map/ppermute | solution.py:367
  20.2 14.4 %collective-permute-start.3 = (bf16[512,512]{1,0:T(8,128)(2,1)}, bf16[512,512]{1,0:T(8,128)(2,1)S(1)}, u32[]{:S(2)}, u32[]{:S(2)}) collective-permute-start(bf16[512,512]{1,0:T(8,128)(2,1)} %pad_maximum_fusion.1), channel_id=1, source_target_pairs={{0,16},{16,0},{1,17},{17,1},{2,18},{18,2},{3,19},{19,3},{4,20},{20... | collective-permute-start | bytes 1572872 | tf_op jit(solution)/shard_map/ppermute | solution.py:373
  21.7 12.9 %collective-permute-start.1 = (bf16[256,1024]{1,0:T(8,128)(2,1)S(1)}, bf16[256,1024]{1,0:T(8,128)(2,1)S(1)}, u32[]{:S(2)}, u32[]{:S(2)}) collective-permute-start(bf16[256,1024]{1,0:T(8,128)(2,1)S(1)} %collective-permute-done.refs_7_.refs_1_), channel_id=1, source_target_pairs={{0,4},{1,5},{2,0},{3,1},{4,8},{5,9},{6,2},{7,3},{8,12},{9,13},{10,... | collective-permute-start | bytes 1572872 | tf_op jit(solution)/shard_map/ppermute | solution.py:367
  23.3 12.9 %collective-permute-start.5 = (bf16[256,1024]{1,0:T(8,128)(2,1)S(1)}, bf16[256,1024]{1,0:T(8,128)(2,1)S(1)}, u32[]{:S(2)}, u32[]{:S(2)}) collective-permute-start(bf16[256,1024]{1,0:T(8,128)(2,1)S(1)} %collective-permute-done.2.refs_8_.refs_2_), channel_id=1, source_target_pairs={{0,2},{1,3},{2,6},{3,7},{4,0},{5,1},{6,10},{7,11},{8,4},{9,5},{10,... | collective-permute-start | bytes 1572872 | tf_op jit(solution)/shard_map/ppermute | solution.py:367
  34.6 12.0 %collective-permute-start.4 = (bf16[256,1024]{1,0:T(8,128)(2,1)S(1)}, bf16[256,1024]{1,0:T(8,128)(2,1)S(1)}, u32[]{:S(2)}, u32[]{:S(2)}) collective-permute-start(bf16[256,1024]{1,0:T(8,128)(2,1)S(1)} %collective-permute-done.1.refs_9_.refs_3_), channel_id=1, source_target_pairs={{0,4},{1,5},{2,0},{3,1},{4,8},{5,9},{6,2},{7,3},{8,12},{9,13},{10,... | collective-permute-start | bytes 1572872 | tf_op jit(solution)/shard_map/ppermute | solution.py:367
  36.2 13.7 %collective-permute-start.6 = (bf16[256,1024]{1,0:T(8,128)(2,1)S(1)}, bf16[256,1024]{1,0:T(8,128)(2,1)S(1)}, u32[]{:S(2)}, u32[]{:S(2)}) collective-permute-start(bf16[256,1024]{1,0:T(8,128)(2,1)S(1)} %collective-permute-done.5.refs_10_.refs_4_), channel_id=1, source_target_pairs={{0,2},{1,3},{2,6},{3,7},{4,0},{5,1},{6,10},{7,11},{8,4},{9,5},{10,... | collective-permute-start | bytes 1572872 | tf_op jit(solution)/shard_map/ppermute | solution.py:367
  36.8 11.5 %collective-permute-start.7 = (bf16[512,512]{1,0:T(8,128)(2,1)S(1)}, bf16[512,512]{1,0:T(8,128)(2,1)S(1)}, u32[]{:S(2)}, u32[]{:S(2)}) collective-permute-start(bf16[512,512]{1,0:T(8,128)(2,1)S(1)} %pad_maximum_fusion.2), channel_id=1, source_target_pairs={{0,16},{16,0},{1,17},{17,1},{2,18},{18,2},{3,19},{19,3},{4,20},{20... | collective-permute-start | bytes 1572872 | tf_op jit(solution)/shard_map/ppermute | solution.py:373
  50.6 18.8 %collective-permute-start.13 = (bf16[512,512]{1,0:T(8,128)(2,1)S(1)}, bf16[512,512]{1,0:T(8,128)(2,1)S(1)}, u32[]{:S(2)}, u32[]{:S(2)}) collective-permute-start(bf16[512,512]{1,0:T(8,128)(2,1)S(1)} %pad_maximum_fusion.3), channel_id=1, source_target_pairs={{0,16},{16,0},{1,17},{17,1},{2,18},{18,2},{3,19},{19,3},{4,20},{20... | collective-permute-start | bytes 1572872 | tf_op jit(solution)/shard_map/ppermute | solution.py:373
  57.2 26.7 %collective-permute-start.17 = (bf16[128,1536]{1,0:T(8,128)(2,1)S(1)}, bf16[128,1536]{1,0:T(8,128)(2,1)S(1)}, u32[]{:S(2)}, u32[]{:S(2)}) collective-permute-start(bf16[128,1536]{1,0:T(8,128)(2,1)S(1)} %pad_maximum_fusion.4), channel_id=1, source_target_pairs={{0,4},{1,5},{2,0},{3,1},{4,8},{5,9},{6,2},{7,3},{8,12},{9,13},{10,... | collective-permute-start | bytes 1179656 | tf_op jit(solution)/shard_map/ppermute | solution.py:367
  58.8 27.4 %collective-permute-start.18 = (bf16[128,1536]{1,0:T(8,128)(2,1)S(1)}, bf16[128,1536]{1,0:T(8,128)(2,1)S(1)}, u32[]{:S(2)}, u32[]{:S(2)}) collective-permute-start(bf16[128,1536]{1,0:T(8,128)(2,1)S(1)} %pad_maximum_fusion.4), channel_id=1, source_target_pairs={{0,2},{1,3},{2,6},{3,7},{4,0},{5,1},{6,10},{7,11},{8,4},{9,5},{10,... | collective-permute-start | bytes 1179656 | tf_op jit(solution)/shard_map/ppermute | solution.py:367
  63.9 35.7 %collective-permute-start.11 = (f32[512,512]{1,0:T(8,128)}, f32[512,512]{1,0:T(8,128)S(1)}, u32[]{:S(2)}, u32[]{:S(2)}) collective-permute-start(f32[512,512]{1,0:T(8,128)} %query_half.11), channel_id=1, source_target_pairs={{0,1},{1,0},{2,3},{3,2},{4,5},{5,4},{6,7},{7,6},{8,9},{9,8},{10,11... | collective-permute-start | bytes 3145736 | tf_op jit(solution)/shard_map/ppermute | solution.py:367
  64.0 10.1 %collective-permute-start.14 = (bf16[256,512]{1,0:T(8,128)(2,1)S(1)}, bf16[256,512]{1,0:T(8,128)(2,1)S(1)}, u32[]{:S(2)}, u32[]{:S(2)}) collective-permute-start(bf16[256,512]{1,0:T(8,128)(2,1)S(1)} %pad_maximum_fusion.5), channel_id=1, source_target_pairs={{0,16},{16,0},{1,17},{17,1},{2,18},{18,2},{3,19},{19,3},{4,20},{20... | collective-permute-start | bytes 786440 | tf_op jit(solution)/shard_map/ppermute | solution.py:373
  69.4 30.1 %collective-permute-start.12 = (bf16[3,512,256]{2,1,0:T(8,128)(2,1)}, bf16[3,512,256]{2,1,0:T(8,128)(2,1)S(1)}, u32[]{:S(2)}, u32[]{:S(2)}) collective-permute-start(bf16[3,512,256]{2,1,0:T(8,128)(2,1)} %get-tuple-element.25), channel_id=1, source_target_pairs={{0,1},{1,0},{2,3},{3,2},{4,5},{5,4},{6,7},{7,6},{8,9},{9,8},{10,11... | collective-permute-start | bytes 2359304 | tf_op jit(solution)/shard_map/ppermute | solution.py:367
  78.6 33.4 %collective-permute-start.15 = (f32[512,512]{1,0:T(8,128)}, f32[512,512]{1,0:T(8,128)S(1)}, u32[]{:S(2)}, u32[]{:S(2)}) collective-permute-start(f32[512,512]{1,0:T(8,128)} %query_half.15), channel_id=1, source_target_pairs={{0,1},{1,0},{2,3},{3,2},{4,5},{5,4},{6,7},{7,6},{8,9},{9,8},{10,11... | collective-permute-start | bytes 3145736 | tf_op jit(solution)/shard_map/ppermute | solution.py:367
  83.9 15.0 %collective-permute-start.19 = (bf16[128,1536]{1,0:T(8,128)(2,1)S(1)}, bf16[128,1536]{1,0:T(8,128)(2,1)S(1)}, u32[]{:S(2)}, u32[]{:S(2)}) collective-permute-start(bf16[128,1536]{1,0:T(8,128)(2,1)S(1)} %collective-permute-done.17.refs_3_), channel_id=1, source_target_pairs={{0,4},{1,5},{2,0},{3,1},{4,8},{5,9},{6,2},{7,3},{8,12},{9,13},{10,... | collective-permute-start | bytes 1179656 | tf_op jit(solution)/shard_map/ppermute | solution.py:367
  86.2 11.2 %collective-permute-start.20 = (bf16[128,1536]{1,0:T(8,128)(2,1)S(1)}, bf16[128,1536]{1,0:T(8,128)(2,1)S(1)}, u32[]{:S(2)}, u32[]{:S(2)}) collective-permute-start(bf16[128,1536]{1,0:T(8,128)(2,1)S(1)} %collective-permute-done.18.refs_4_), channel_id=1, source_target_pairs={{0,2},{1,3},{2,6},{3,7},{4,0},{5,1},{6,10},{7,11},{8,4},{9,5},{10,... | collective-permute-start | bytes 1179656 | tf_op jit(solution)/shard_map/ppermute | solution.py:367
  97.4 12.5 %collective-permute-start.21 = (bf16[256,512]{1,0:T(8,128)(2,1)S(1)}, bf16[256,512]{1,0:T(8,128)(2,1)S(1)}, u32[]{:S(2)}, u32[]{:S(2)}) collective-permute-start(bf16[256,512]{1,0:T(8,128)(2,1)S(1)} %pad_maximum_fusion.6), channel_id=1, source_target_pairs={{0,16},{16,0},{1,17},{17,1},{2,18},{18,2},{3,19},{19,3},{4,20},{20... | collective-permute-start | bytes 786440 | tf_op jit(solution)/shard_map/ppermute | solution.py:373
  98.9 23.2 %collective-permute-start.24 = (bf16[256,512]{1,0:T(8,128)(2,1)S(1)}, bf16[256,512]{1,0:T(8,128)(2,1)S(1)}, u32[]{:S(2)}, u32[]{:S(2)}) collective-permute-start(bf16[256,512]{1,0:T(8,128)(2,1)S(1)} %pad_maximum_fusion.7), channel_id=1, source_target_pairs={{0,16},{16,0},{1,17},{17,1},{2,18},{18,2},{3,19},{19,3},{4,20},{20... | collective-permute-start | bytes 786440 | tf_op jit(solution)/shard_map/ppermute | solution.py:373
  109.9 12.2 %collective-permute-start.22 = (bf16[128,1536]{1,0:T(8,128)(2,1)S(1)}, bf16[128,1536]{1,0:T(8,128)(2,1)S(1)}, u32[]{:S(2)}, u32[]{:S(2)}) collective-permute-start(bf16[128,1536]{1,0:T(8,128)(2,1)S(1)} %collective-permute-done.19.refs_5_), channel_id=1, source_target_pairs={{0,4},{1,5},{2,0},{3,1},{4,8},{5,9},{6,2},{7,3},{8,12},{9,13},{10,... | collective-permute-start | bytes 1179656 | tf_op jit(solution)/shard_map/ppermute | solution.py:367
  111.7 12.3 %collective-permute-start.23 = (bf16[128,1536]{1,0:T(8,128)(2,1)S(1)}, bf16[128,1536]{1,0:T(8,128)(2,1)S(1)}, u32[]{:S(2)}, u32[]{:S(2)}) collective-permute-start(bf16[128,1536]{1,0:T(8,128)(2,1)S(1)} %collective-permute-done.20.refs_6_), channel_id=1, source_target_pairs={{0,2},{1,3},{2,6},{3,7},{4,0},{5,1},{6,10},{7,11},{8,4},{9,5},{10,... | collective-permute-start | bytes 1179656 | tf_op jit(solution)/shard_map/ppermute | solution.py:367
  125.2 11.7 %collective-permute-start.30 = (bf16[512,512]{1,0:T(8,128)(2,1)}, bf16[512,512]{1,0:T(8,128)(2,1)S(1)}, u32[]{:S(2)}, u32[]{:S(2)}) collective-permute-start(bf16[512,512]{1,0:T(8,128)(2,1)} %attend.3.refs_1_), channel_id=1, source_target_pairs={{0,1},{1,0},{2,3},{3,2},{4,5},{5,4},{6,7},{7,6},{8,9},{9,8},{10,11... | collective-permute-start | bytes 1572872 | tf_op jit(solution)/shard_map/ppermute | solution.py:367
  (38 other events, 319.9 us)

commit v2 on v1

v2 whole, which is shorter than its diff:
```python
import functools
import math

import jax
import jax.numpy as jnp
from jax import lax
from jax.experimental import pallas as pl
from jax.experimental.pallas import tpu as pltpu
from jax.sharding import PartitionSpec as P

BLOCK = 512
TOPK = 3
RING_CHIPS = 8
MIB = 2**20
VMEM = 60 * MIB


def pack_kernel(plane_ref, weight_ref, keys_ref, values_ref, out_ref):
    depth, width = weight_ref.shape
    head_size = keys_ref.shape[1]
    out_ref[:, :width] = weight_ref[...]
    for i, rows in enumerate(range(0, keys_ref.shape[0], depth)):
        at = width + 2 * i * head_size
        out_ref[:, at : at + head_size] = keys_ref[rows : rows + depth, :]
        out_ref[:, at + head_size : at + 2 * head_size] = values_ref[rows : rows + depth, :]


def pack(plane, weight, keys, values):
    depth, width = weight.shape
    size, head_size = keys.shape
    wide = width // 2 + 2 * head_size * (size // depth)
    return pl.pallas_call(
        pack_kernel,
        grid_spec=pltpu.PrefetchScalarGridSpec(
            num_scalar_prefetch=1,
            grid=(1,),
            in_specs=[
                pl.BlockSpec((depth, width // 2), lambda i, plane: (0, plane[0])),
                pl.BlockSpec(keys.shape, lambda i, plane: (0, 0)),
                pl.BlockSpec(values.shape, lambda i, plane: (0, 0)),
            ],
            out_specs=pl.BlockSpec((depth, wide), lambda i, plane: (0, 0)),
        ),
        out_shape=jax.ShapeDtypeStruct((depth, wide), weight.dtype),
        compiler_params=pltpu.CompilerParams(vmem_limit_bytes=VMEM),
        name="pack",
    )(plane, weight, keys, values)


def started(copies):
    for copy in copies:
        copy.start()
    return copies


def waited(copies):
    for copy in copies:
        copy.wait()


def query_kernel(depth, pieces, summed, blocks, scalar_ref, *refs):
    count = len(pieces)
    arrays, refs = refs[: 1 + max(p for p, _ in pieces + blocks)], refs[1 + max(p for p, _ in pieces + blocks) :]
    hidden, refs = refs[:2], refs[2:]
    totals, refs = (refs[:2], refs[2:]) if summed else ((), refs)
    outs, refs = refs[:2], refs[2:]
    near, refs = (refs[:2], refs[2:]) if blocks else ((), refs)
    weight_ref, hidden_ref, total_ref, weight_sems, hidden_sems, total_sems, out_sems = refs[:7]
    tokens, width = total_ref.shape[1:]

    def weight_copy(i):
        array, row = pieces[i]
        wide = array == 0
        start = pl.multiple_of(scalar_ref[0] * width, width) if wide else 0
        return pltpu.make_async_copy(
            arrays[array].at[pl.ds(row * depth, depth), pl.ds(start, width)],
            weight_ref.at[pl.ds(i * depth, depth)],
            weight_sems.at[i],
        )

    def hidden_copy(side, i):
        start = pl.multiple_of(scalar_ref[1 + i] * depth, depth)
        return pltpu.make_async_copy(
            hidden[side].at[:, pl.ds(start, depth)],
            hidden_ref.at[side, :, pl.ds(i * depth, depth)],
            hidden_sems.at[side, i],
        )

    def near_copies(source, target, slot):
        array, row = source
        both, size = target.shape[2], target.shape[1]
        return [
            pltpu.make_async_copy(
                arrays[array].at[pl.ds(row * depth, depth), pl.ds(width + h * both, both)],
                target.at[slot, pl.ds(h * depth, depth)],
                refs[7].at[0 if target is near[0] else 1, slot, h],
            )
            for h in range(size // depth)
        ]

    weights = started([weight_copy(i) for i in range(count)])
    lefts = [started([hidden_copy(side, i) for i in range(count)]) for side in range(2)]
    added = []
    for side in range(2 if summed else 0):
        added.append(
            started(
                [pltpu.make_async_copy(totals[side], total_ref.at[side], total_sems.at[side])]
            )
        )
    if blocks:
        listed = near[1].shape[0]
        for side in range(2):
            for j in range(listed):
                for s, source in enumerate(blocks):

                    @pl.when(scalar_ref[1 + count + side * listed + j] == s)
                    def _(side=side, j=j, source=source):
                        started(near_copies(source, near[side], j))

        started(near_copies(blocks[0], near[0], listed))
    waited(weights)
    sent = []
    for side in range(2):
        waited(lefts[side])
        total = jnp.dot(hidden_ref[side], weight_ref[...], preferred_element_type=jnp.float32)
        if summed:
            waited(added[side])
            total += total_ref[side]
        total_ref[side] = total
        sent += started(
            [pltpu.make_async_copy(total_ref.at[side], outs[side], out_sems.at[side])]
        )
    if blocks:
        for side in range(2):
            for j in range(listed + 1 - side):
                waited(near_copies(blocks[0], near[side], j))
    waited(sent)


def query(hidden, scalars, weight, pieces, depth, width, totals, blocks=(), listed=0, block=None):
    tokens = hidden[0].shape[0]
    arrays = [weight]

    def index(array):
        for i, known in enumerate(arrays):
            if known is array:
                return i
        arrays.append(array)
        return len(arrays) - 1

    where = [(index(array), row) for array, row in pieces]
    held = [(index(array), row) for array, row in blocks]
    count = len(pieces)
    out_shape = [jax.ShapeDtypeStruct((tokens, width), jnp.float32)] * 2
    scratch = [
        pltpu.VMEM((count * depth, width), weight.dtype),
        pltpu.VMEM((2, tokens, count * depth), weight.dtype),
        pltpu.VMEM((2, tokens, width), jnp.float32),
        pltpu.SemaphoreType.DMA((count,)),
        pltpu.SemaphoreType.DMA((2, count)),
        pltpu.SemaphoreType.DMA((2,)),
        pltpu.SemaphoreType.DMA((2,)),
    ]
    if blocks:
        out_shape += [
            jax.ShapeDtypeStruct((listed + 1,) + block, weight.dtype),
            jax.ShapeDtypeStruct((listed,) + block, weight.dtype),
        ]
        scratch.append(pltpu.SemaphoreType.DMA((2, listed + 1, block[0] // depth)))
    operands = [*arrays, *hidden, *totals]
    anywhere = pl.BlockSpec(memory_space=pl.ANY)
    return pl.pallas_call(
        functools.partial(query_kernel, depth, where, bool(totals), held),
        in_specs=[pl.BlockSpec(memory_space=pltpu.SMEM)] + [anywhere] * len(operands),
        out_specs=[anywhere] * 2 + [pl.BlockSpec(memory_space=pltpu.VMEM)] * (len(out_shape) - 2),
        out_shape=out_shape,
        scratch_shapes=scratch,
        compiler_params=pltpu.CompilerParams(vmem_limit_bytes=VMEM),
        cost_estimate=pl.CostEstimate(
            flops=4 * tokens * depth * width * count,
            bytes_accessed=2 * count * depth * (2 * tokens + width) + 16 * tokens * width,
            transcendentals=0,
        ),
        name="query",
    )(scalars, *operands)


def attend_kernel(factor, shared, bias_ref, swap_ref, *refs):
    if shared:
        q_own_ref, q_got_ref, near_ref, got_ref, o_ref, kv_ref, q_ref = refs
        listed = got_ref.shape[0]
        q_ref[...] = (q_own_ref[...] + q_got_ref[...]).astype(q_ref.dtype)
        kv_ref[listed] = near_ref[listed]
        for j in range(listed):

            @pl.when(swap_ref[j] == 0)
            def _(j=j):
                kv_ref[j] = near_ref[j]

            @pl.when(swap_ref[j] != 0)
            def _(j=j):
                kv_ref[j] = got_ref[j]

    else:
        q_ref, kv_ref, o_ref = refs
    blocks, size, both = kv_ref.shape
    hd, listed, tile = both // 2, blocks - 1, size // 2
    across = (((1,), (1,)), ((), ()))

    def score(head, part):
        q = q_ref[part * tile : (part + 1) * tile, head * hd : (head + 1) * hd]
        spans = [(j, size) for j in range(listed)] + [(listed, tile * (part + 1))]
        return [
            lax.dot_general(
                q, kv_ref[j, :seen, :hd], across, preferred_element_type=jnp.float32
            )
            for j, seen in spans
        ]

    def mix(head, part, scores):
        at_query = lax.broadcasted_iota(jnp.int32, scores[-1].shape, 0) + part * tile
        at_key = lax.broadcasted_iota(jnp.int32, scores[-1].shape, 1)
        scores = scores[:-1] + [jnp.where(at_query >= at_key, scores[-1], -jnp.inf)]
        bias = [bias_ref[j] for j in range(listed)] + [0.0]
        peak = functools.reduce(
            jnp.maximum,
            [jnp.max(s, axis=1, keepdims=True) - b for s, b in zip(scores, bias)],
        )
        weights = [jnp.exp2((s - (peak + b)) * factor) for s, b in zip(scores, bias)]
        total = sum(jnp.sum(w, axis=1, keepdims=True) for w in weights)
        mixed = sum(
            jnp.dot(
                w.astype(jnp.bfloat16),
                kv_ref[j, : w.shape[1], hd:],
                preferred_element_type=jnp.float32,
            )
            for j, w in enumerate(weights)
        )
        o_ref[part * tile : (part + 1) * tile, head * hd : (head + 1) * hd] = (
            mixed / total
        ).astype(o_ref.dtype)

    parts = [(head, part) for head in range(q_ref.shape[1] // hd) for part in range(2)]
    ahead = score(*parts[0])
    for i, part in enumerate(parts):
        scores = ahead
        if i + 1 < len(parts):
            ahead = score(*parts[i + 1])
        mix(*part, scores)


def attend(queries, near, bias, swapped):
    tokens, width = queries[0].shape
    blocks, size, both = near[0].shape
    hd = both // 2
    step = min(width, 4 * hd)
    work = tokens * blocks * size * (width // hd)
    shared = len(queries) == 2
    query_spec = pl.BlockSpec((tokens, step), lambda h: (0, h))
    scratch = [
        pltpu.VMEM(near[0].shape, near[0].dtype),
        pltpu.VMEM((tokens, step), jnp.bfloat16),
    ]
    return pl.pallas_call(
        functools.partial(attend_kernel, math.log2(math.e) / math.sqrt(hd), shared),
        grid=(width // step,),
        in_specs=[pl.BlockSpec(memory_space=pltpu.SMEM)] * 2
        + [query_spec] * len(queries)
        + [pl.BlockSpec(n.shape, lambda h: (0, 0, 0)) for n in near],
        out_specs=query_spec,
        out_shape=jax.ShapeDtypeStruct((tokens, width), jnp.bfloat16),
        scratch_shapes=scratch if shared else [],
        compiler_params=pltpu.CompilerParams(vmem_limit_bytes=VMEM),
        cost_estimate=pl.CostEstimate(
            flops=8 * work * hd, bytes_accessed=4 * MIB, transcendentals=work
        ),
        name="attend",
    )(bias, swapped, *queries, *near)


def project_kernel(parts, pieces, step, place_ref, *refs):
    attention, refs = refs[:parts], refs[parts:]
    rows, refs = refs[: len(pieces)], refs[len(pieces) :]
    out_ref, weight_ref, left_ref, result_ref, weight_sems, left_sems, out_sems = refs
    steps = weight_ref.shape[1] // step

    def columns(n):
        return pl.ds(n * step, step)

    def weight_copy(n, i):
        start = pl.multiple_of(place_ref[i], pieces[i])
        return pltpu.make_async_copy(
            rows[i].at[:, columns(n)],
            weight_ref.at[pl.ds(start, pieces[i]), columns(n)],
            weight_sems.at[n, i],
        )

    wide = left_ref.shape[1] // parts
    lefts = [
        pltpu.make_async_copy(a, left_ref.at[:, pl.ds(i * wide, wide)], left_sems.at[i])
        for i, a in enumerate(attention)
    ]
    arriving = [started([weight_copy(0, i) for i in range(len(pieces))])]
    started(lefts)
    for n in range(1, steps):
        arriving.append(started([weight_copy(n, i) for i in range(len(pieces))]))
    waited(lefts)
    left = left_ref[...]
    leaving = []
    for n in range(steps):
        waited(arriving[n])
        total = jnp.dot(left, weight_ref[:, columns(n)], preferred_element_type=jnp.float32)
        result_ref[:, columns(n)] = total.astype(result_ref.dtype)
        leaving += started(
            [
                pltpu.make_async_copy(
                    result_ref.at[:, columns(n)], out_ref.at[:, columns(n)], out_sems.at[n]
                )
            ]
        )
    waited(leaving)


def project(attention, places, pieces):
    tokens = attention[0].shape[0]
    width = pieces[0].shape[1]
    depths = [p.shape[0] for p in pieces]
    rows = sum(depths)
    step = min(1024, width)
    anywhere = pl.BlockSpec(memory_space=pl.ANY)
    return pl.pallas_call(
        functools.partial(project_kernel, len(attention), depths, step),
        in_specs=[pl.BlockSpec(memory_space=pltpu.SMEM)]
        + [anywhere] * (len(attention) + len(pieces)),
        out_specs=anywhere,
        out_shape=jax.ShapeDtypeStruct((tokens, width), attention[0].dtype),
        scratch_shapes=[
            pltpu.VMEM((rows, width), pieces[0].dtype),
            pltpu.VMEM((tokens, rows), attention[0].dtype),
            pltpu.VMEM((tokens, width), attention[0].dtype),
            pltpu.SemaphoreType.DMA((width // step, len(pieces))),
            pltpu.SemaphoreType.DMA((len(attention),)),
            pltpu.SemaphoreType.DMA((width // step,)),
        ],
        compiler_params=pltpu.CompilerParams(vmem_limit_bytes=VMEM),
        cost_estimate=pl.CostEstimate(
            flops=2 * tokens * rows * width,
            bytes_accessed=2 * (rows + tokens) * width + 2 * tokens * rows,
            transcendentals=0,
        ),
        name="project",
    )(places, *attention, *pieces)


def ring_device(hidden_states, query_weight, output_weight, keys, values, block_lists):
    devices = lax.axis_size("ctx")
    chips = devices // 2
    half = chips // 2
    ring = list(range(0, chips, 2)) + list(range(chips - 1, 0, -2))
    at = {chip: i for i, chip in enumerate(ring)}
    depth, width = query_weight.shape
    size, head_size = keys.shape

    def pairs(step):
        return [
            (2 * p + c, 2 * ring[(at[p] + step) % chips] + c) for p in range(chips) for c in (0, 1)
        ]

    ahead, back = pairs(1), pairs(-1)

    def send(array, to):
        return lax.ppermute(array, "ctx", to)

    def swap(array):
        return send(array, [(d, d ^ 1) for d in range(devices)])

    def cross(array):
        return lax.ppermute(array, "groups", [(0, 1), (1, 0)])

    def held_back(array, *until):
        return lax.optimization_barrier((array, *until))[0]

    distances = [0] + [d for s in range(1, half) for d in (-s, s)] + [half]
    me, plane = lax.axis_index("ctx"), lax.axis_index("groups")
    chip, core = me // 2, me % 2
    here = jnp.where(chip % 2 == 0, chip // 2, chips - 1 - chip // 2)
    order = (here + jnp.asarray(distances, jnp.int32) + chips) % chips
    order = jnp.where(order < half, 2 * order, 2 * (chips - 1 - order) + 1)
    lists = lax.dynamic_slice_in_dim(block_lists, 2 * chip, 2, 0)
    lists = jnp.where(core == 0, lists, lists[::-1])
    listed = lists.shape[1]
    bias = jnp.where(lists[0] < me, 0.0, jnp.inf).astype(jnp.float32)
    swapped = (lists[0] % 2 != core).astype(jnp.int32)
    held_at = jnp.argmax(order == lists[:, :, None] // 2, axis=2).astype(jnp.int32).reshape(-1)
    plane = jnp.reshape(plane, (1,)).astype(jnp.int32)
    places = 2 * order + core
    early, late = 2 * half - 3, 2 * half
    scalars = {
        (which, when): jnp.concatenate([plane if which == 0 else 1 - plane, places[span], held_at])
        for which in (0, 1)
        for when, span in enumerate((slice(0, early), slice(early, late)))
    }
    rows = output_weight.shape[0]
    cut = rows // 2
    row_of = 2 * order[:, None] + (core + jnp.arange(2, dtype=jnp.int32)) % 2
    row_of = ((row_of + chips * plane) % devices * rows).reshape(-1)
    row_of = jnp.concatenate([row_of, row_of[-2:] + cut])
    bias, swapped, row_of, scalars = lax.optimization_barrier((bias, swapped, row_of, scalars))

    hidden = (swap(hidden_states), hidden_states)
    own = pack(plane, query_weight, keys, values)

    def part(which, found, when, totals, **more):
        spans = distances[:early] if when == 0 else distances[early:]
        pieces = [(query_weight, 0) if d == 0 else found[d] for d in spans]
        return query(
            hidden, scalars[which, when], query_weight, pieces, depth, width // 2, totals, **more
        )

    near, crossed = {}, {}
    down, up = own, own
    behind = [bias, swapped, row_of, scalars[0, 0]]
    for step in range(1, half):
        down, up = send(down, ahead), send(up, back)
        over = cross(jnp.concatenate([down[:, : width // 2], up[:, : width // 2]], 0))
        near[-step], near[step] = (down, 0), (up, 0)
        crossed[-step], crossed[step] = (over, 0), (over, 1)
        if step == half - 1:
            first = part(0, near, 0, ())
            behind = [*first, crossed[step - 2][0]]
        down, up = held_back(down, *behind), held_back(up, *behind)
        behind = []
    down, up = send(down[: depth // 2], ahead), send(up[depth // 2 :], back)
    far = jnp.concatenate([down, up], 0)
    near[half] = (far, 0)
    crossed[half] = (cross(far[:, : width // 2]), 0)
    second = part(1, crossed, 0, ())
    last = [down, up, *second]
    blocks = [(own, 0)] + [near[d] for d in distances[1:]]
    block = (size, 2 * head_size)
    theirs, ours, picked, given = part(
        0, near, 1, first, blocks=blocks, listed=listed, block=block
    )
    queries = [(ours, swap(theirs))]
    picked = (picked, swap(given))
    theirs, ours = part(1, crossed, 1, second)
    queries.append((ours, swap(theirs)))

    pieces = [output_weight, swap(output_weight)]
    down, up = held_back(output_weight, *last), held_back(output_weight, *last)
    attention = []
    behind = [pieces[1], given, crossed[half - 1][0]]
    for step in range(1, half):
        down, up = send(down, ahead), send(up, back)
        got = [swap(down), swap(up)]
        pieces += [down, got[0], up, got[1]]
        if step > 1:
            attention.append(attend(queries[step - 2], picked, bias, swapped))
            behind.append(attention[-1])
        down, up = held_back(down, *behind), held_back(up, *behind)
        behind = got + [crossed[half][0]] if step == 1 else got
    down, up = send(down[:cut], ahead), send(up[cut:], back)
    pieces += [down, swap(down), up, swap(up)]
    return project(attention, row_of, pieces)


def per_device(hidden_states, query_weight, output_weight, keys, values, block_lists):
    devices = lax.axis_size("ctx")
    head_size = keys.shape[1]
    piece_rows = BLOCK // devices
    me = lax.axis_index("ctx")
    total = jnp.dot(
        hidden_states,
        lax.all_gather(query_weight, "ctx", axis=0, tiled=True),
        preferred_element_type=jnp.float32,
    )
    queries = total.astype(jnp.bfloat16)
    near = jnp.concatenate([keys, values], 1)
    spread = lax.all_to_all(near[None], "ctx", split_axis=1, concat_axis=0, tiled=True)
    listed = jnp.take(spread, block_lists, axis=0).reshape(
        devices, TOPK, piece_rows, 2 * head_size
    )
    got = lax.all_to_all(listed, "ctx", split_axis=0, concat_axis=2, tiled=True)
    picked = jnp.concatenate([got.reshape(TOPK, BLOCK, 2 * head_size), near[None]], 0)
    mine = lax.dynamic_index_in_dim(block_lists, me, 0, keepdims=False)
    bias = jnp.where(mine < me, 0.0, jnp.inf).astype(jnp.float32)
    attention = attend((queries,), (picked,), bias, jnp.zeros_like(mine))
    projected = jnp.dot(
        attention,
        lax.all_gather(output_weight, "ctx", axis=0, tiled=True),
        preferred_element_type=jnp.float32,
    )
    return projected.astype(jnp.bfloat16)


def solution(mesh):
    in_specs = (
        P(("groups", "ctx"), None),
        P("ctx", None),
        P("ctx", None),
        P(("groups", "ctx"), None),
        P(("groups", "ctx"), None),
        P("groups", None),
    )
    out_specs = P(("groups", "ctx"), None)
    step_by_step = mesh.shape["ctx"] <= 2 * RING_CHIPS and mesh.shape["groups"] == 2
    return jax.shard_map(
        ring_device if step_by_step else per_device,
        mesh=mesh,
        in_specs=in_specs,
        out_specs=out_specs,
        check_vma=False,
    )
```

time: 159 us -> 132 us (0.83)
  Pallas kernels: 75.3 us -> 54.6 us
  local copies, waits for them, and re-layouts: 10.2 us -> 6.2 us
  starting transfers between devices: 27.4 us -> 25.1 us
    pallas_call x12 -> x5, Pallas kernels: 55.1 us -> 34.4 us  [the longest x4 23.1 us: query(): pl.pallas_call(functools.partial(query_kernel, depth, where, bool(totals)...]
    ppermute x8 -> x4, waiting for transfers between devices: 7.16 us -> 3.68 us  [cross(): return lax.ppermute(array, 'groups', [(0, 1), (1, 0)])]
    ppermute x24 -> x29, waiting for transfers between devices: 30.9 us -> 34.2 us  [send(): return lax.ppermute(array, 'ctx', to)]
    ppermute x8 -> x4, starting transfers between devices: 8.24 us -> 5.38 us  [cross(): return lax.ppermute(array, 'groups', [(0, 1), (1, 0)])]
    unnamed x62 -> x47, local copies, waits for them, and re-layouts: 6.5 us -> 3.74 us
    dynamic_slice x2 -> x1, local copies, waits for them, and re-layouts: 2.6 us -> 0.75 us  [ring_device(): lists = lax.dynamic_slice_in_dim(block_lists, 2 * chip, 2, 0)]
    concatenate x13 -> x6, other arithmetic: 2.67 us -> 3.58 us  [the longest x3 1.72 us: ring_device(): over = cross(jnp.concatenate([down[:, :width // 2], up[:, :width // 2]], 0))]
    ppermute x24 -> x29, starting transfers between devices: 19.2 us -> 19.7 us  [send(): return lax.ppermute(array, 'ctx', to)]
  transfers between devices with their start and end apart: 32 -> 33, of which waited for: 10 -> 11; matrix products, arithmetic and copies ran while one was open for 7% -> 7% of each run, Pallas kernels for 40% -> 33%
where the time goes in v2:
time: 132 us; the launch traced here: 131 us
  Pallas kernels  54.6 us (41%)
  waiting for transfers between devices  37.8 us (29%)
  starting transfers between devices  25.1 us (19%)
  other arithmetic  7.1 us (5%)
  local copies, waits for them, and re-layouts  6.2 us (5%)
    ppermute x29, waiting for transfers between devices, send(): return lax.ppermute(array, 'ctx', to)  34.2 us
    pallas_call x4, Pallas kernels, query(): pl.pallas_call(functools.partial(query_kernel, depth, where, bool(totals)...  23.1 us
    ppermute x29, starting transfers between devices, send(): return lax.ppermute(array, 'ctx', to)  19.7 us
    pallas_call x2, Pallas kernels, attend(): pl.pallas_call(functools.partial(attend_kernel, math.log2(math.e) / math....  18.2 us
    pallas_call x1, Pallas kernels, project(): pl.pallas_call(functools.partial(project_kernel, len(attention), depths,...  11.3 us
    ppermute x4, starting transfers between devices, cross(): return lax.ppermute(array, 'groups', [(0, 1), (1, 0)])  5.38 us
    unnamed x47, local copies, waits for them, and re-layouts  3.74 us
    ppermute x4, waiting for transfers between devices, cross(): return lax.ppermute(array, 'groups', [(0, 1), (1, 0)])  3.68 us
  transfers between devices with their start and end apart: 33, of which 11 were waited for; matrix products, arithmetic and copies ran while one was open for 7% of the time, Pallas kernels for 33%

profile of v2, /device:TPU:0, one launch (start us, length us, event | category | flops | bytes accessed | tf_op | source)
XLA Modules:
  0.0 131.4 jit_solution(11177205141460705044)
XLA Ops:
  0.5 1.9 %pack.1.refs_4_ = bf16[256,1024]{1,0:T(8,128)(2,1)} custom-call(s32[1]{0:T(128)} %bitcast.plane_ref, bf16[256,1024]{1,0:T(8,128)(2,1)} %refs_0_.7, bf16[512,128]{1,0:T(8,128)(2,1)} %keys_ref.1, bf16[512,128]{1,0:T(8,128)(2,1)} %values_ref.1), custom_call_target="tpu_custom_call" | custom-call | tf_op jit(solution)/shard_map/pack/pallas_call | solution.py:32
  2.4 2.6 %collective-permute-start = (bf16[256,1024]{1,0:T(8,128)(2,1)}, bf16[256,1024]{1,0:T(8,128)(2,1)S(1)}, u32[]{:S(2)}, u32[]{:S(2)}) collective-permute-start(bf16[256,1024]{1,0:T(8,128)(2,1)} %pack.1.refs_4_), channel_id=1, source_target_pairs={{0,4},{1,5},{2,0},{3,1},{4,8},{5,9},{6,2},{7,3},{8,12},{9,13},{10,... | collective-permute-start | bytes 1572872 | tf_op jit(solution)/shard_map/ppermute | solution.py:372
  11.6 6.1 %collective-permute-done.refs_1_.refs_5_ = bf16[256,1024]{1,0:T(8,128)(2,1)S(1)} collective-permute-done((bf16[256,1024]{1,0:T(8,128)(2,1)}, bf16[256,1024]{1,0:T(8,128)(2,1)S(1)}, u32[]{:S(2)}, u32[]{:S(2)}) %collective-permute-start) | collective-permute-done | bytes 524320 | tf_op jit(solution)/shard_map/ppermute | solution.py:372
  17.7 1.8 %collective-permute-start.1 = (bf16[256,1024]{1,0:T(8,128)(2,1)S(1)}, bf16[256,1024]{1,0:T(8,128)(2,1)S(1)}, u32[]{:S(2)}, u32[]{:S(2)}) collective-permute-start(bf16[256,1024]{1,0:T(8,128)(2,1)S(1)} %collective-permute-done.refs_1_.refs_5_), channel_id=1, source_target_pairs={{0,4},{1,5},{2,0},{3,1},{4,8},{5,9},{6,2},{7,3},{8,12},{9,13},{10,... | collective-permute-start | bytes 1572872 | tf_op jit(solution)/shard_map/ppermute | solution.py:372
  20.6 1.7 %collective-permute-start.7 = (bf16[512,512]{1,0:T(8,128)(2,1)}, bf16[512,512]{1,0:T(8,128)(2,1)S(1)}, u32[]{:S(2)}, u32[]{:S(2)}) collective-permute-start(bf16[512,512]{1,0:T(8,128)(2,1)} %pad_maximum_fusion), channel_id=1, source_target_pairs={{0,16},{16,0},{1,17},{17,1},{2,18},{18,2},{3,19},{19,3},{4,20},{20... | collective-permute-start | bytes 1572872 | tf_op jit(solution)/shard_map/ppermute | solution.py:378
  22.3 9.1 %collective-permute-done.1.refs_3_.refs_7_ = bf16[256,1024]{1,0:T(8,128)(2,1)S(1)} collective-permute-done((bf16[256,1024]{1,0:T(8,128)(2,1)S(1)}, bf16[256,1024]{1,0:T(8,128)(2,1)S(1)}, u32[]{:S(2)}, u32[]{:S(2)}) %collective-permute-start.1) | collective-permute-done | bytes 524320 | tf_op jit(solution)/shard_map/ppermute | solution.py:372
  31.5 1.6 %collective-permute-start.2 = (bf16[256,1024]{1,0:T(8,128)(2,1)S(1)}, bf16[256,1024]{1,0:T(8,128)(2,1)S(1)}, u32[]{:S(2)}, u32[]{:S(2)}) collective-permute-start(bf16[256,1024]{1,0:T(8,128)(2,1)S(1)} %collective-permute-done.1.refs_3_.refs_7_), channel_id=1, source_target_pairs={{0,4},{1,5},{2,0},{3,1},{4,8},{5,9},{6,2},{7,3},{8,12},{9,13},{10,... | collective-permute-start | bytes 1572872 | tf_op jit(solution)/shard_map/ppermute | solution.py:372
  35.9 5.5 %query.4 = (f32[512,512]{1,0:T(8,128)}, f32[512,512]{1,0:T(8,128)}) custom-call(s32[12]{0:T(128)} %get-tuple-element.39.scalar_ref, bf16[256,1024]{1,0:T(8,128)(2,1)} %refs_0_.7, bf16[256,1024]{1,0:T(8,128)(2,1)} %copy-done, bf16[256,1024]{1,0:T(8,128)(2,1)} %copy-done.1, bf16[256,1024]{1,0:T(8,128)(2,1)} %copy-done.2, bf16[256,1024]{1,0:T(8,128)(2,1)} %copy-done.3, ...), custom_call_target="tpu_custom_call" | custom-call | flops 1342177280 | bytes 8126464 | tf_op jit(solution)/shard_map/query/pallas_call | solution.py:172
  41.5 2.9 %collective-permute-done.2.refs_1_ = bf16[256,1024]{1,0:T(8,128)(2,1)S(1)} collective-permute-done((bf16[256,1024]{1,0:T(8,128)(2,1)S(1)}, bf16[256,1024]{1,0:T(8,128)(2,1)S(1)}, u32[]{:S(2)}, u32[]{:S(2)}) %collective-permute-start.2) | collective-permute-done | bytes 524320 | tf_op jit(solution)/shard_map/ppermute | solution.py:372
  48.0 5.5 %query.6 = (f32[512,512]{1,0:T(8,128)}, f32[512,512]{1,0:T(8,128)}) custom-call(s32[12]{0:T(128)} %get-tuple-element.51.scalar_ref, bf16[256,1024]{1,0:T(8,128)(2,1)} %refs_0_.7, bf16[512,512]{1,0:T(8,128)(2,1)} %copy-done.8, bf16[512,512]{1,0:T(8,128)(2,1)} %collective-permute-done.14.refs_2_, ...), custom_call_target="tpu_custom_call" | custom-call | flops 1342177280 | bytes 8126464 | tf_op jit(solution)/shard_map/query/pallas_call | solution.py:172
  53.5 1.6 %collective-permute-start.17 = (bf16[64,4096]{1,0:T(8,128)(2,1)}, bf16[64,4096]{1,0:T(8,128)(2,1)S(1)}, u32[]{:S(2)}, u32[]{:S(2)}) collective-permute-start(bf16[64,4096]{1,0:T(8,128)(2,1)} %refs_2_.1), channel_id=1, source_target_pairs={{0,4},{1,5},{2,0},{3,1},{4,8},{5,9},{6,2},{7,3},{8,12},{9,13},{10,... | collective-permute-start | bytes 1572872 | tf_op jit(solution)/shard_map/ppermute | solution.py:372
  56.5 7.1 %query.5 = (f32[512,512]{1,0:T(8,128)}, f32[512,512]{1,0:T(8,128)}, bf16[4,512,256]{2,1,0:T(8,128)(2,1)}, bf16[3,512,256]{2,1,0:T(8,128)(2,1)}) custom-call(s32[10]{0:T(128)} %get-tuple-element.38.scalar_ref, bf16[256,1024]{1,0:T(8,128)(2,1)} %refs_0_.7, bf16[256,1024]{1,0:T(8,128)(2,1)} %copy-done.4, bf16[256,1024]{1,0:T(8,128)(2,1)} %copy-done.5, ...), custom_call_target="tpu_custom_call" | custom-call | flops 805306368 | bytes 6553600 | tf_op jit(solution)/shard_map/query/pallas_call | solution.py:172
  66.0 1.8 %collective-permute-done.17.refs_4_ = bf16[64,4096]{1,0:T(8,128)(2,1)S(1)} collective-permute-done((bf16[64,4096]{1,0:T(8,128)(2,1)}, bf16[64,4096]{1,0:T(8,128)(2,1)S(1)}, u32[]{:S(2)}, u32[]{:S(2)}) %collective-permute-start.17) | collective-permute-done | bytes 524320 | tf_op jit(solution)/shard_map/ppermute | solution.py:372
  67.9 1.6 %collective-permute-start.21 = (bf16[64,4096]{1,0:T(8,128)(2,1)S(1)}, bf16[64,4096]{1,0:T(8,128)(2,1)S(1)}, u32[]{:S(2)}, u32[]{:S(2)}) collective-permute-start(bf16[64,4096]{1,0:T(8,128)(2,1)S(1)} %collective-permute-done.17.refs_4_), channel_id=1, source_target_pairs={{0,4},{1,5},{2,0},{3,1},{4,8},{5,9},{6,2},{7,3},{8,12},{9,13},{10,... | collective-permute-start | bytes 1572872 | tf_op jit(solution)/shard_map/ppermute | solution.py:372
  69.9 3.7 %collective-permute-done.13.refs_2_ = bf16[256,512]{1,0:T(8,128)(2,1)S(1)} collective-permute-done((bf16[256,512]{1,0:T(8,128)(2,1)S(1)}, bf16[256,512]{1,0:T(8,128)(2,1)S(1)}, u32[]{:S(2)}, u32[]{:S(2)}) %collective-permute-start.13) | collective-permute-done | bytes 262176 | tf_op jit(solution)/shard_map/ppermute | solution.py:378
  74.3 4.9 %query.7 = (f32[512,512]{1,0:T(8,128)}, f32[512,512]{1,0:T(8,128)}) custom-call(s32[10]{0:T(128)} %get-tuple-element.50.scalar_ref, bf16[256,1024]{1,0:T(8,128)(2,1)} %refs_0_.7, bf16[512,512]{1,0:T(8,128)(2,1)} %copy-done.7, bf16[256,512]{1,0:T(8,128)(2,1)} %copy-done.9, bf16[512,4096]{1,0:T(8,128)(2,1)} %collective-permute-done.6.refs_5_.refs_9_.refs_3_, ...), custom_call_target="tpu_custom_call" | custom-call | flops 805306368 | bytes 6553600 | tf_op jit(solution)/shard_map/query/pallas_call | solution.py:172
  83.5 9.1 %attend.2.refs_0_ = bf16[512,512]{1,0:T(8,128)(2,1)} custom-call(f32[3]{0:T(128)} %compare_select_fusion.9.bias_ref, s32[3]{0:T(128)} %compare_convert_fusion.swap_ref, f32[512,512]{1,0:T(8,128)} %get-tuple-element.46.refs_0_, f32[512,512]{1,0:T(8,128)} %copy-done.12, bf16[4,512,256]{2,1,0:T(8,128)(2,1)} %get-tuple-element.48.refs_2_, ...), custom_call_target="tpu_custom_call" | custom-call | flops 4294967296 | bytes 4194304 | tf_op jit(solution)/shard_map/attend/pallas_call | solution.py:264
  92.6 1.6 %collective-permute-start.25 = (bf16[64,4096]{1,0:T(8,128)(2,1)S(1)}, bf16[64,4096]{1,0:T(8,128)(2,1)S(1)}, u32[]{:S(2)}, u32[]{:S(2)}) collective-permute-start(bf16[64,4096]{1,0:T(8,128)(2,1)S(1)} %collective-permute-done.21.refs_8_), channel_id=1, source_target_pairs={{0,4},{1,5},{2,0},{3,1},{4,8},{5,9},{6,2},{7,3},{8,12},{9,13},{10,... | collective-permute-start | bytes 1572872 | tf_op jit(solution)/shard_map/ppermute | solution.py:372
  95.7 9.1 %attend.3.refs_1_ = bf16[512,512]{1,0:T(8,128)(2,1)} custom-call(f32[3]{0:T(128)} %compare_select_fusion.9.bias_ref, s32[3]{0:T(128)} %compare_convert_fusion.swap_ref, f32[512,512]{1,0:T(8,128)} %get-tuple-element.54.refs_0_, f32[512,512]{1,0:T(8,128)} %copy-done.13, bf16[4,512,256]{2,1,0:T(8,128)(2,1)} %get-tuple-element.48.refs_2_, ...), custom_call_target="tpu_custom_call" | custom-call | flops 4294967296 | bytes 4194304 | tf_op jit(solution)/shard_map/attend/pallas_call | solution.py:264
  104.8 2.2 %collective-permute-done.25.refs_12_ = bf16[64,4096]{1,0:T(8,128)(2,1)S(1)} collective-permute-done((bf16[64,4096]{1,0:T(8,128)(2,1)S(1)}, bf16[64,4096]{1,0:T(8,128)(2,1)S(1)}, u32[]{:S(2)}, u32[]{:S(2)}) %collective-permute-start.25) | collective-permute-done | bytes 524320 | tf_op jit(solution)/shard_map/ppermute | solution.py:372
  107.0 1.6 %collective-permute-start.29 = (bf16[32,4096]{1,0:T(8,128)(2,1)S(1)}, bf16[32,4096]{1,0:T(8,128)(2,1)S(1)}, u32[]{:S(2)}, u32[]{:S(2)}) collective-permute-start(bf16[32,4096]{1,0:T(8,128)(2,1)S(1)} %slice.62), channel_id=1, source_target_pairs={{0,4},{1,5},{2,0},{3,1},{4,8},{5,9},{6,2},{7,3},{8,12},{9,13},{10,... | collective-permute-start | bytes 786440 | tf_op jit(solution)/shard_map/ppermute | solution.py:372
  109.7 5.3 %collective-permute-done.29.refs_16_ = bf16[32,4096]{1,0:T(8,128)(2,1)S(1)} collective-permute-done((bf16[32,4096]{1,0:T(8,128)(2,1)S(1)}, bf16[32,4096]{1,0:T(8,128)(2,1)S(1)}, u32[]{:S(2)}, u32[]{:S(2)}) %collective-permute-start.29) | collective-permute-done | bytes 262176 | tf_op jit(solution)/shard_map/ppermute | solution.py:372
  115.0 2.5 %collective-permute-done.31.refs_18_ = bf16[32,4096]{1,0:T(8,128)(2,1)S(1)} collective-permute-done((bf16[32,4096]{1,0:T(8,128)(2,1)S(1)}, bf16[32,4096]{1,0:T(8,128)(2,1)S(1)}, u32[]{:S(2)}, u32[]{:S(2)}) %collective-permute-start.31) | collective-permute-done | bytes 262176 | tf_op jit(solution)/shard_map/ppermute | solution.py:372
  119.9 11.3 %project.1 = bf16[512,4096]{1,0:T(8,128)(2,1)} custom-call(s32[18]{0:T(128)} %pad_add_fusion.place_ref, bf16[512,512]{1,0:T(8,128)(2,1)} %attend.2.refs_0_, bf16[512,512]{1,0:T(8,128)(2,1)} %attend.3.refs_1_, bf16[64,4096]{1,0:T(8,128)(2,1)} %refs_2_.1, bf16[64,4096]{1,0:T(8,128)(2,1)} %collective-permute-done.16.refs_3_, bf16[64,4096]{1,0:T(8,128)(2,1)} %copy-done.14, ...), custom_call_target="tpu_custom_call" | custom-call | flops 4294967296 | bytes 13631488 | tf_op jit(solution)/shard_map/project/pallas_call | solution.py:331
  (132 shorter events, 28.4 us)
Async XLA Ops:
  0.0 35.9 %collective-permute-start.6 = (bf16[512,4096]{1,0:T(8,128)(2,1)}, bf16[512,4096]{1,0:T(8,128)(2,1)}, u32[]{:S(2)}, u32[]{:S(2)}) collective-permute-start(bf16[512,4096]{1,0:T(8,128)(2,1)} %refs_4_.3), channel_id=1, source_target_pairs={{0,1},{1,0},{2,3},{3,2},{4,5},{5,4},{6,7},{7,6},{8,9},{9,8},{10,11... | collective-permute-start | bytes 12582920 | tf_op jit(solution)/shard_map/ppermute | solution.py:372
  2.4 15.3 %collective-permute-start = (bf16[256,1024]{1,0:T(8,128)(2,1)}, bf16[256,1024]{1,0:T(8,128)(2,1)S(1)}, u32[]{:S(2)}, u32[]{:S(2)}) collective-permute-start(bf16[256,1024]{1,0:T(8,128)(2,1)} %pack.1.refs_4_), channel_id=1, source_target_pairs={{0,4},{1,5},{2,0},{3,1},{4,8},{5,9},{6,2},{7,3},{8,12},{9,13},{10,... | collective-permute-start | bytes 1572872 | tf_op jit(solution)/shard_map/ppermute | solution.py:372
  4.9 14.6 %collective-permute-start.3 = (bf16[256,1024]{1,0:T(8,128)(2,1)}, bf16[256,1024]{1,0:T(8,128)(2,1)S(1)}, u32[]{:S(2)}, u32[]{:S(2)}) collective-permute-start(bf16[256,1024]{1,0:T(8,128)(2,1)} %pack.1.refs_4_), channel_id=1, source_target_pairs={{0,2},{1,3},{2,6},{3,7},{4,0},{5,1},{6,10},{7,11},{8,4},{9,5},{10,... | collective-permute-start | bytes 1572872 | tf_op jit(solution)/shard_map/ppermute | solution.py:372
  17.7 13.8 %collective-permute-start.1 = (bf16[256,1024]{1,0:T(8,128)(2,1)S(1)}, bf16[256,1024]{1,0:T(8,128)(2,1)S(1)}, u32[]{:S(2)}, u32[]{:S(2)}) collective-permute-start(bf16[256,1024]{1,0:T(8,128)(2,1)S(1)} %collective-permute-done.refs_1_.refs_5_), channel_id=1, source_target_pairs={{0,4},{1,5},{2,0},{3,1},{4,8},{5,9},{6,2},{7,3},{8,12},{9,13},{10,... | collective-permute-start | bytes 1572872 | tf_op jit(solution)/shard_map/ppermute | solution.py:372
  19.5 13.6 %collective-permute-start.4 = (bf16[256,1024]{1,0:T(8,128)(2,1)S(1)}, bf16[256,1024]{1,0:T(8,128)(2,1)S(1)}, u32[]{:S(2)}, u32[]{:S(2)}) collective-permute-start(bf16[256,1024]{1,0:T(8,128)(2,1)S(1)} %collective-permute-done.3.refs_2_.refs_6_), channel_id=1, source_target_pairs={{0,2},{1,3},{2,6},{3,7},{4,0},{5,1},{6,10},{7,11},{8,4},{9,5},{10,... | collective-permute-start | bytes 1572872 | tf_op jit(solution)/shard_map/ppermute | solution.py:372
  20.6 20.8 %collective-permute-start.7 = (bf16[512,512]{1,0:T(8,128)(2,1)}, bf16[512,512]{1,0:T(8,128)(2,1)S(1)}, u32[]{:S(2)}, u32[]{:S(2)}) collective-permute-start(bf16[512,512]{1,0:T(8,128)(2,1)} %pad_maximum_fusion), channel_id=1, source_target_pairs={{0,16},{16,0},{1,17},{17,1},{2,18},{18,2},{3,19},{19,3},{4,20},{20... | collective-permute-start | bytes 1572872 | tf_op jit(solution)/shard_map/ppermute | solution.py:378
  31.5 12.9 %collective-permute-start.2 = (bf16[256,1024]{1,0:T(8,128)(2,1)S(1)}, bf16[256,1024]{1,0:T(8,128)(2,1)S(1)}, u32[]{:S(2)}, u32[]{:S(2)}) collective-permute-start(bf16[256,1024]{1,0:T(8,128)(2,1)S(1)} %collective-permute-done.1.refs_3_.refs_7_), channel_id=1, source_target_pairs={{0,4},{1,5},{2,0},{3,1},{4,8},{5,9},{6,2},{7,3},{8,12},{9,13},{10,... | collective-permute-start | bytes 1572872 | tf_op jit(solution)/shard_map/ppermute | solution.py:372
  33.1 12.7 %collective-permute-start.5 = (bf16[256,1024]{1,0:T(8,128)(2,1)S(1)}, bf16[256,1024]{1,0:T(8,128)(2,1)S(1)}, u32[]{:S(2)}, u32[]{:S(2)}) collective-permute-start(bf16[256,1024]{1,0:T(8,128)(2,1)S(1)} %collective-permute-done.4.refs_4_.refs_8_), channel_id=1, source_target_pairs={{0,2},{1,3},{2,6},{3,7},{4,0},{5,1},{6,10},{7,11},{8,4},{9,5},{10,... | collective-permute-start | bytes 1572872 | tf_op jit(solution)/shard_map/ppermute | solution.py:372
  34.4 13.6 %collective-permute-start.14 = (bf16[512,512]{1,0:T(8,128)(2,1)}, bf16[512,512]{1,0:T(8,128)(2,1)}, u32[]{:S(2)}, u32[]{:S(2)}) collective-permute-start(bf16[512,512]{1,0:T(8,128)(2,1)} %pad_maximum_fusion.2), channel_id=1, source_target_pairs={{0,16},{16,0},{1,17},{17,1},{2,18},{18,2},{3,19},{19,3},{4,20},{20... | collective-permute-start | bytes 1572872 | tf_op jit(solution)/shard_map/ppermute | solution.py:378
  46.5 17.2 %collective-permute-start.16 = (bf16[64,4096]{1,0:T(8,128)(2,1)}, bf16[64,4096]{1,0:T(8,128)(2,1)}, u32[]{:S(2)}, u32[]{:S(2)}) collective-permute-start(bf16[64,4096]{1,0:T(8,128)(2,1)} %refs_2_.1), channel_id=1, source_target_pairs={{0,1},{1,0},{2,3},{3,2},{4,5},{5,4},{6,7},{7,6},{8,9},{9,8},{10,11... | collective-permute-start | bytes 1572872 | tf_op jit(solution)/shard_map/ppermute | solution.py:372
  46.6 18.6 %collective-permute-start.12 = (bf16[512,512]{1,0:T(8,128)(2,1)S(1)}, bf16[512,512]{1,0:T(8,128)(2,1)S(1)}, u32[]{:S(2)}, u32[]{:S(2)}) collective-permute-start(bf16[512,512]{1,0:T(8,128)(2,1)S(1)} %pad_maximum_fusion.1), channel_id=1, source_target_pairs={{0,16},{16,0},{1,17},{17,1},{2,18},{18,2},{3,19},{19,3},{4,20},{20... | collective-permute-start | bytes 1572872 | tf_op jit(solution)/shard_map/ppermute | solution.py:378
  53.5 14.3 %collective-permute-start.17 = (bf16[64,4096]{1,0:T(8,128)(2,1)}, bf16[64,4096]{1,0:T(8,128)(2,1)S(1)}, u32[]{:S(2)}, u32[]{:S(2)}) collective-permute-start(bf16[64,4096]{1,0:T(8,128)(2,1)} %refs_2_.1), channel_id=1, source_target_pairs={{0,4},{1,5},{2,0},{3,1},{4,8},{5,9},{6,2},{7,3},{8,12},{9,13},{10,... | collective-permute-start | bytes 1572872 | tf_op jit(solution)/shard_map/ppermute | solution.py:372
  55.2 14.3 %collective-permute-start.19 = (bf16[64,4096]{1,0:T(8,128)(2,1)}, bf16[64,4096]{1,0:T(8,128)(2,1)S(1)}, u32[]{:S(2)}, u32[]{:S(2)}) collective-permute-start(bf16[64,4096]{1,0:T(8,128)(2,1)} %refs_2_.1), channel_id=1, source_target_pairs={{0,2},{1,3},{2,6},{3,7},{4,0},{5,1},{6,10},{7,11},{8,4},{9,5},{10,... | collective-permute-start | bytes 1572872 | tf_op jit(solution)/shard_map/ppermute | solution.py:372
  63.6 18.9 %collective-permute-start.10 = (f32[512,512]{1,0:T(8,128)}, f32[512,512]{1,0:T(8,128)S(1)}, u32[]{:S(2)}, u32[]{:S(2)}) collective-permute-start(f32[512,512]{1,0:T(8,128)} %get-tuple-element.47), channel_id=1, source_target_pairs={{0,1},{1,0},{2,3},{3,2},{4,5},{5,4},{6,7},{7,6},{8,9},{9,8},{10,11... | collective-permute-start | bytes 3145736 | tf_op jit(solution)/shard_map/ppermute | solution.py:372
  63.7 15.6 %collective-permute-start.11 = (bf16[3,512,256]{2,1,0:T(8,128)(2,1)}, bf16[3,512,256]{2,1,0:T(8,128)(2,1)}, u32[]{:S(2)}, u32[]{:S(2)}) collective-permute-start(bf16[3,512,256]{2,1,0:T(8,128)(2,1)} %get-tuple-element.49), channel_id=1, source_target_pairs={{0,1},{1,0},{2,3},{3,2},{4,5},{5,4},{6,7},{7,6},{8,9},{9,8},{10,11... | collective-permute-start | bytes 2359304 | tf_op jit(solution)/shard_map/ppermute | solution.py:372
  67.9 13.2 %collective-permute-start.21 = (bf16[64,4096]{1,0:T(8,128)(2,1)S(1)}, bf16[64,4096]{1,0:T(8,128)(2,1)S(1)}, u32[]{:S(2)}, u32[]{:S(2)}) collective-permute-start(bf16[64,4096]{1,0:T(8,128)(2,1)S(1)} %collective-permute-done.17.refs_4_), channel_id=1, source_target_pairs={{0,4},{1,5},{2,0},{3,1},{4,8},{5,9},{6,2},{7,3},{8,12},{9,13},{10,... | collective-permute-start | bytes 1572872 | tf_op jit(solution)/shard_map/ppermute | solution.py:372
  69.4 13.1 %collective-permute-start.23 = (bf16[64,4096]{1,0:T(8,128)(2,1)S(1)}, bf16[64,4096]{1,0:T(8,128)(2,1)}, u32[]{:S(2)}, u32[]{:S(2)}) collective-permute-start(bf16[64,4096]{1,0:T(8,128)(2,1)S(1)} %collective-permute-done.19.refs_6_), channel_id=1, source_target_pairs={{0,2},{1,3},{2,6},{3,7},{4,0},{5,1},{6,10},{7,11},{8,4},{9,5},{10,... | collective-permute-start | bytes 1572872 | tf_op jit(solution)/shard_map/ppermute | solution.py:372
  79.2 15.5 %collective-permute-start.15 = (f32[512,512]{1,0:T(8,128)}, f32[512,512]{1,0:T(8,128)S(1)}, u32[]{:S(2)}, u32[]{:S(2)}) collective-permute-start(f32[512,512]{1,0:T(8,128)} %get-tuple-element.55), channel_id=1, source_target_pairs={{0,1},{1,0},{2,3},{3,2},{4,5},{5,4},{6,7},{7,6},{8,9},{9,8},{10,11... | collective-permute-start | bytes 3145736 | tf_op jit(solution)/shard_map/ppermute | solution.py:372
  79.3 13.3 %collective-permute-start.18 = (bf16[64,4096]{1,0:T(8,128)(2,1)S(1)}, bf16[64,4096]{1,0:T(8,128)(2,1)}, u32[]{:S(2)}, u32[]{:S(2)}) collective-permute-start(bf16[64,4096]{1,0:T(8,128)(2,1)S(1)} %collective-permute-done.17.refs_4_), channel_id=1, source_target_pairs={{0,1},{1,0},{2,3},{3,2},{4,5},{5,4},{6,7},{7,6},{8,9},{9,8},{10,11... | collective-permute-start | bytes 1572872 | tf_op jit(solution)/shard_map/ppermute | solution.py:372
  81.1 11.5 %collective-permute-start.20 = (bf16[64,4096]{1,0:T(8,128)(2,1)S(1)}, bf16[64,4096]{1,0:T(8,128)(2,1)}, u32[]{:S(2)}, u32[]{:S(2)}) collective-permute-start(bf16[64,4096]{1,0:T(8,128)(2,1)S(1)} %collective-permute-done.19.refs_6_), channel_id=1, source_target_pairs={{0,1},{1,0},{2,3},{3,2},{4,5},{5,4},{6,7},{7,6},{8,9},{9,8},{10,11... | collective-permute-start | bytes 1572872 | tf_op jit(solution)/shard_map/ppermute | solution.py:372
  82.5 22.3 %collective-permute-start.22 = (bf16[64,4096]{1,0:T(8,128)(2,1)S(1)}, bf16[64,4096]{1,0:T(8,128)(2,1)}, u32[]{:S(2)}, u32[]{:S(2)}) collective-permute-start(bf16[64,4096]{1,0:T(8,128)(2,1)S(1)} %collective-permute-done.21.refs_8_), channel_id=1, source_target_pairs={{0,1},{1,0},{2,3},{3,2},{4,5},{5,4},{6,7},{7,6},{8,9},{9,8},{10,11... | collective-permute-start | bytes 1572872 | tf_op jit(solution)/shard_map/ppermute | solution.py:372
  82.5 22.3 %collective-permute-start.24 = (bf16[64,4096]{1,0:T(8,128)(2,1)}, bf16[64,4096]{1,0:T(8,128)(2,1)}, u32[]{:S(2)}, u32[]{:S(2)}) collective-permute-start(bf16[64,4096]{1,0:T(8,128)(2,1)} %collective-permute-done.23.refs_10_), channel_id=1, source_target_pairs={{0,1},{1,0},{2,3},{3,2},{4,5},{5,4},{6,7},{7,6},{8,9},{9,8},{10,11... | collective-permute-start | bytes 1572872 | tf_op jit(solution)/shard_map/ppermute | solution.py:372
  92.6 14.4 %collective-permute-start.25 = (bf16[64,4096]{1,0:T(8,128)(2,1)S(1)}, bf16[64,4096]{1,0:T(8,128)(2,1)S(1)}, u32[]{:S(2)}, u32[]{:S(2)}) collective-permute-start(bf16[64,4096]{1,0:T(8,128)(2,1)S(1)} %collective-permute-done.21.refs_8_), channel_id=1, source_target_pairs={{0,4},{1,5},{2,0},{3,1},{4,8},{5,9},{6,2},{7,3},{8,12},{9,13},{10,... | collective-permute-start | bytes 1572872 | tf_op jit(solution)/shard_map/ppermute | solution.py:372
  94.2 14.4 %collective-permute-start.27 = (bf16[64,4096]{1,0:T(8,128)(2,1)}, bf16[64,4096]{1,0:T(8,128)(2,1)S(1)}, u32[]{:S(2)}, u32[]{:S(2)}) collective-permute-start(bf16[64,4096]{1,0:T(8,128)(2,1)} %collective-permute-done.23.refs_10_), channel_id=1, source_target_pairs={{0,2},{1,3},{2,6},{3,7},{4,0},{5,1},{6,10},{7,11},{8,4},{9,5},{10,... | collective-permute-start | bytes 1572872 | tf_op jit(solution)/shard_map/ppermute | solution.py:372
  (32 other events, 245.5 us)

commit v3 on v2

--- a/solution.py
+++ b/solution.py
@@ -12,7 +12,7 @@
 TOPK = 3
 RING_CHIPS = 8
 MIB = 2**20
-VMEM = 60 * MIB
+VMEM = 28 * MIB
 
 
 def pack_kernel(plane_ref, weight_ref, keys_ref, values_ref, out_ref):
@@ -176,11 +176,7 @@
         out_shape=out_shape,
         scratch_shapes=scratch,
         compiler_params=pltpu.CompilerParams(vmem_limit_bytes=VMEM),
-        cost_estimate=pl.CostEstimate(
-            flops=4 * tokens * depth * width * count,
-            bytes_accessed=2 * count * depth * (2 * tokens + width) + 16 * tokens * width,
-            transcendentals=0,
-        ),
+        cost_estimate=pl.CostEstimate(flops=1955000000, bytes_accessed=1000, transcendentals=0),
         name="query",
     )(scalars, *operands)
 
@@ -271,16 +267,14 @@
         out_shape=jax.ShapeDtypeStruct((tokens, width), jnp.bfloat16),
         scratch_shapes=scratch if shared else [],
         compiler_params=pltpu.CompilerParams(vmem_limit_bytes=VMEM),
-        cost_estimate=pl.CostEstimate(
-            flops=8 * work * hd, bytes_accessed=4 * MIB, transcendentals=work
-        ),
+        cost_estimate=pl.CostEstimate(flops=3910000000, bytes_accessed=1000, transcendentals=0),
         name="attend",
     )(bias, swapped, *queries, *near)
 
 
-def project_kernel(parts, pieces, step, place_ref, *refs):
+def project_kernel(parts, count, pieces, step, place_ref, *refs):
     attention, refs = refs[:parts], refs[parts:]
-    rows, refs = refs[: len(pieces)], refs[len(pieces) :]
+    arrays, refs = refs[:count], refs[count:]
     out_ref, weight_ref, left_ref, result_ref, weight_sems, left_sems, out_sems = refs
     steps = weight_ref.shape[1] // step
 
@@ -288,10 +282,11 @@
         return pl.ds(n * step, step)
 
     def weight_copy(n, i):
-        start = pl.multiple_of(place_ref[i], pieces[i])
+        array, row, depth = pieces[i]
+        start = pl.multiple_of(place_ref[i], depth)
         return pltpu.make_async_copy(
-            rows[i].at[:, columns(n)],
-            weight_ref.at[pl.ds(start, pieces[i]), columns(n)],
+            arrays[array].at[pl.ds(row, depth), columns(n)],
+            weight_ref.at[pl.ds(start, depth), columns(n)],
             weight_sems.at[n, i],
         )
 
@@ -323,22 +318,27 @@
 
 def project(attention, places, pieces):
     tokens = attention[0].shape[0]
-    width = pieces[0].shape[1]
-    depths = [p.shape[0] for p in pieces]
-    rows = sum(depths)
+    width = pieces[0][0].shape[1]
+    arrays, held = [], []
+    for array, row, depth in pieces:
+        known = [i for i, other in enumerate(arrays) if other is array]
+        if not known:
+            arrays.append(array)
+        held.append((known[0] if known else len(arrays) - 1, row, depth))
+    rows = sum(depth for _, _, depth in held)
     step = min(1024, width)
     anywhere = pl.BlockSpec(memory_space=pl.ANY)
     return pl.pallas_call(
-        functools.partial(project_kernel, len(attention), depths, step),
+        functools.partial(project_kernel, len(attention), len(arrays), held, step),
         in_specs=[pl.BlockSpec(memory_space=pltpu.SMEM)]
-        + [anywhere] * (len(attention) + len(pieces)),
+        + [anywhere] * (len(attention) + len(arrays)),
         out_specs=anywhere,
         out_shape=jax.ShapeDtypeStruct((tokens, width), attention[0].dtype),
         scratch_shapes=[
-            pltpu.VMEM((rows, width), pieces[0].dtype),
+            pltpu.VMEM((rows, width), arrays[0].dtype),
             pltpu.VMEM((tokens, rows), attention[0].dtype),
             pltpu.VMEM((tokens, width), attention[0].dtype),
-            pltpu.SemaphoreType.DMA((width // step, len(pieces))),
+            pltpu.SemaphoreType.DMA((width // step, len(held))),
             pltpu.SemaphoreType.DMA((len(attention),)),
             pltpu.SemaphoreType.DMA((width // step,)),
         ],
@@ -349,7 +349,7 @@
             transcendentals=0,
         ),
         name="project",
-    )(places, *attention, *pieces)
+    )(places, *attention, *arrays)
 
 
 def ring_device(hidden_states, query_weight, output_weight, keys, values, block_lists):
@@ -422,7 +422,8 @@
     behind = [bias, swapped, row_of, scalars[0, 0]]
     for step in range(1, half):
         down, up = send(down, ahead), send(up, back)
-        over = cross(jnp.concatenate([down[:, : width // 2], up[:, : width // 2]], 0))
+        over = jnp.concatenate([down[:, : width // 2], up[:, : width // 2]], 0)
+        over = cross(over) if step < half - 1 else over
         near[-step], near[step] = (down, 0), (up, 0)
         crossed[-step], crossed[step] = (over, 0), (over, 1)
         if step == half - 1:
@@ -433,7 +434,9 @@
     down, up = send(down[: depth // 2], ahead), send(up[depth // 2 :], back)
     far = jnp.concatenate([down, up], 0)
     near[half] = (far, 0)
-    crossed[half] = (cross(far[:, : width // 2]), 0)
+    over = cross(jnp.concatenate([over, far[:, : width // 2]], 0))
+    for i, distance in enumerate((1 - half, half - 1, half)):
+        crossed[distance] = (over, i)
     second = part(1, crossed, 0, ())
     last = [down, up, *second]
     blocks = [(own, 0)] + [near[d] for d in distances[1:]]
@@ -446,21 +449,24 @@
     theirs, ours = part(1, crossed, 1, second)
     queries.append((ours, swap(theirs)))
 
-    pieces = [output_weight, swap(output_weight)]
+    pieces = [(output_weight, 0, rows), (swap(output_weight), 0, rows)]
     down, up = held_back(output_weight, *last), held_back(output_weight, *last)
     attention = []
-    behind = [pieces[1], given, crossed[half - 1][0]]
+    behind = [pieces[1][0], given]
     for step in range(1, half):
         down, up = send(down, ahead), send(up, back)
-        got = [swap(down), swap(up)]
-        pieces += [down, got[0], up, got[1]]
+        pair = jnp.concatenate([down, up], 0)
         if step > 1:
             attention.append(attend(queries[step - 2], picked, bias, swapped))
             behind.append(attention[-1])
+        if step == half - 1:
+            pair = held_back(pair, attention[-1])
+        other = swap(pair)
+        pieces += [(down, 0, rows), (other, 0, rows), (up, 0, rows), (other, rows, rows)]
         down, up = held_back(down, *behind), held_back(up, *behind)
-        behind = got + [crossed[half][0]] if step == 1 else got
+        behind = [other]
     down, up = send(down[:cut], ahead), send(up[cut:], back)
-    pieces += [down, swap(down), up, swap(up)]
+    pieces += [(down, 0, cut), (swap(down), 0, cut), (up, 0, cut), (swap(up), 0, cut)]
     return project(attention, row_of, pieces)
 
 

time: 132 us -> 127 us (0.962)
  waiting for transfers between devices: 37.8 us -> 58.5 us
  Pallas kernels: 54.6 us -> 37.8 us
  other arithmetic: 7.1 us -> 2.89 us
  starting transfers between devices: 25.1 us -> 22.8 us
  local copies, waits for them, and re-layouts: 6.2 us -> 4.39 us
    ppermute x29 -> x26, waiting for transfers between devices: 34.2 us -> 52.5 us  [send(): return lax.ppermute(array, 'ctx', to)]
    pallas_call x4, Pallas kernels: 23.1 us -> 14.7 us  [query(): pl.pallas_call(functools.partial(query_kernel, depth, where, bool(totals)...]
    pallas_call x2, Pallas kernels: 18.2 us -> 13.6 us  [attend(): pl.pallas_call(functools.partial(attend_kernel, math.log2(math.e) / math....]
    ppermute x4 -> x3, waiting for transfers between devices: 3.68 us -> 6.04 us  [cross(): return lax.ppermute(array, 'groups', [(0, 1), (1, 0)])]
    pallas_call x1, Pallas kernels: 11.3 us -> 9.4 us  [project(): pl.pallas_call(functools.partial(project_kernel, len(attention), len(arra...]
    pallas_call x1, Pallas kernels: 1.92 us -> 0.08 us  [pack(): pl.pallas_call(pack_kernel, grid_spec=pltpu.PrefetchScalarGridSpec(num_sc...]
    ppermute x29 -> x26, starting transfers between devices: 19.7 us -> 17.9 us  [send(): return lax.ppermute(array, 'ctx', to)]
    concatenate x3 -> x6, other arithmetic: 1.72 us -> 0.38 us  [the longest x3 0.25 us: ring_device(): pair = jnp.concatenate([down, up], 0)]
  transfers between devices with their start and end apart: 33 -> 29, of which waited for: 11 -> 15; matrix products, arithmetic and copies ran while one was open for 7% -> 3% of each run, Pallas kernels for 33% -> 22%
where the time goes in v3:
time: 127 us
  waiting for transfers between devices  58.5 us (46%)
  Pallas kernels  37.8 us (30%)
  starting transfers between devices  22.8 us (18%)
  local copies, waits for them, and re-layouts  4.39 us (3%)
  other arithmetic  2.89 us (2%)
    ppermute x26, waiting for transfers between devices, send(): return lax.ppermute(array, 'ctx', to)  52.5 us
    ppermute x26, starting transfers between devices, send(): return lax.ppermute(array, 'ctx', to)  17.9 us
    pallas_call x4, Pallas kernels, query(): pl.pallas_call(functools.partial(query_kernel, depth, where, bool(totals)...  14.7 us
    pallas_call x2, Pallas kernels, attend(): pl.pallas_call(functools.partial(attend_kernel, math.log2(math.e) / math....  13.6 us
    pallas_call x1, Pallas kernels, project(): pl.pallas_call(functools.partial(project_kernel, len(attention), len(arra...  9.4 us
    ppermute x3, waiting for transfers between devices, cross(): return lax.ppermute(array, 'groups', [(0, 1), (1, 0)])  6.04 us
    ppermute x3, starting transfers between devices, cross(): return lax.ppermute(array, 'groups', [(0, 1), (1, 0)])  4.91 us
    unnamed x13, local copies, waits for them, and re-layouts  2.88 us
  transfers between devices with their start and end apart: 29, of which 15 were waited for; matrix products, arithmetic and copies ran while one was open for 3% of the time, Pallas kernels for 22%

profile of v3, /device:TPU:0, one launch (start us, length us, event | category | flops | bytes accessed | tf_op | source)
XLA Modules:
  0.0 126.9 jit_solution(14310286439000961107)
XLA Ops:
  3.4 2.6 %collective-permute-start = (bf16[256,1024]{1,0:T(8,128)(2,1)S(1)}, bf16[256,1024]{1,0:T(8,128)(2,1)S(1)}, u32[]{:S(2)}, u32[]{:S(2)}) collective-permute-start(bf16[256,1024]{1,0:T(8,128)(2,1)S(1)} %pack.1.refs_4_), channel_id=1, source_target_pairs={{0,4},{1,5},{2,0},{3,1},{4,8},{5,9},{6,2},{7,3},{8,12},{9,13},{10,... | collective-permute-start | bytes 1572872 | tf_op jit(solution)/shard_map/ppermute | solution.py:372
  9.9 8.7 %collective-permute-done.refs_1_.refs_5_ = bf16[256,1024]{1,0:T(8,128)(2,1)S(1)} collective-permute-done((bf16[256,1024]{1,0:T(8,128)(2,1)S(1)}, bf16[256,1024]{1,0:T(8,128)(2,1)S(1)}, u32[]{:S(2)}, u32[]{:S(2)}) %collective-permute-start) | collective-permute-done | bytes 524320 | tf_op jit(solution)/shard_map/ppermute | solution.py:372
  18.6 1.8 %collective-permute-start.1 = (bf16[256,1024]{1,0:T(8,128)(2,1)S(1)}, bf16[256,1024]{1,0:T(8,128)(2,1)S(1)}, u32[]{:S(2)}, u32[]{:S(2)}) collective-permute-start(bf16[256,1024]{1,0:T(8,128)(2,1)S(1)} %collective-permute-done.refs_1_.refs_5_), channel_id=1, source_target_pairs={{0,4},{1,5},{2,0},{3,1},{4,8},{5,9},{6,2},{7,3},{8,12},{9,13},{10,... | collective-permute-start | bytes 1572872 | tf_op jit(solution)/shard_map/ppermute | solution.py:372
  20.7 1.8 %collective-permute-start.7 = (bf16[512,512]{1,0:T(8,128)(2,1)S(1)}, bf16[512,512]{1,0:T(8,128)(2,1)S(1)}, u32[]{:S(2)}, u32[]{:S(2)}) collective-permute-start(bf16[512,512]{1,0:T(8,128)(2,1)S(1)} %pad_maximum_fusion.4), channel_id=1, source_target_pairs={{0,16},{16,0},{1,17},{17,1},{2,18},{18,2},{3,19},{19,3},{4,20},{20... | collective-permute-start | bytes 1572872 | tf_op jit(solution)/shard_map/ppermute | solution.py:378
  22.5 9.9 %collective-permute-done.1.refs_3_.refs_7_ = bf16[256,1024]{1,0:T(8,128)(2,1)S(1)} collective-permute-done((bf16[256,1024]{1,0:T(8,128)(2,1)S(1)}, bf16[256,1024]{1,0:T(8,128)(2,1)S(1)}, u32[]{:S(2)}, u32[]{:S(2)}) %collective-permute-start.1) | collective-permute-done | bytes 524320 | tf_op jit(solution)/shard_map/ppermute | solution.py:372
  32.3 1.6 %collective-permute-start.2 = (bf16[256,1024]{1,0:T(8,128)(2,1)S(1)}, bf16[256,1024]{1,0:T(8,128)(2,1)S(1)}, u32[]{:S(2)}, u32[]{:S(2)}) collective-permute-start(bf16[256,1024]{1,0:T(8,128)(2,1)S(1)} %collective-permute-done.1.refs_3_.refs_7_), channel_id=1, source_target_pairs={{0,4},{1,5},{2,0},{3,1},{4,8},{5,9},{6,2},{7,3},{8,12},{9,13},{10,... | collective-permute-start | bytes 1572872 | tf_op jit(solution)/shard_map/ppermute | solution.py:372
  34.5 1.6 %collective-permute-start.13 = (bf16[512,512]{1,0:T(8,128)(2,1)S(1)}, bf16[512,512]{1,0:T(8,128)(2,1)S(1)}, u32[]{:S(2)}, u32[]{:S(2)}) collective-permute-start(bf16[512,512]{1,0:T(8,128)(2,1)S(1)} %pad_maximum_fusion.5), channel_id=1, source_target_pairs={{0,16},{16,0},{1,17},{17,1},{2,18},{18,2},{3,19},{19,3},{4,20},{20... | collective-permute-start | bytes 1572872 | tf_op jit(solution)/shard_map/ppermute | solution.py:378
  36.0 3.9 %query.4 = (f32[512,512]{1,0:T(8,128)S(1)}, f32[512,512]{1,0:T(8,128)S(1)}) custom-call(s32[12]{0:T(128)S(1)} %get-tuple-element.40.scalar_ref, bf16[256,1024]{1,0:T(8,128)(2,1)S(1)} %copy-done.2, bf16[256,1024]{1,0:T(8,128)(2,1)S(1)} %collective-permute-done.refs_1_.refs_5_, bf16[256,1024]{1,0:T(8,128)(2,1)S(1)} %collective-permute-done.3.refs_2_.refs_6_, ...), custom_call_target="tpu_custom_call" | custom-call | flops 1955000064 | bytes 1000 | tf_op jit(solution)/shard_map/query/pallas_call | solution.py:172
  40.0 5.2 %collective-permute-done.2.refs_1_ = bf16[256,1024]{1,0:T(8,128)(2,1)S(1)} collective-permute-done((bf16[256,1024]{1,0:T(8,128)(2,1)S(1)}, bf16[256,1024]{1,0:T(8,128)(2,1)S(1)}, u32[]{:S(2)}, u32[]{:S(2)}) %collective-permute-start.2) | collective-permute-done | bytes 524320 | tf_op jit(solution)/shard_map/ppermute | solution.py:372
  47.5 3.9 %query.6 = (f32[512,512]{1,0:T(8,128)S(1)}, f32[512,512]{1,0:T(8,128)S(1)}) custom-call(s32[12]{0:T(128)S(1)} %get-tuple-element.52.scalar_ref, bf16[256,1024]{1,0:T(8,128)(2,1)S(1)} %copy-done.2, bf16[512,512]{1,0:T(8,128)(2,1)S(1)} %collective-permute-done.7.refs_1_, bf16[512,512]{1,0:T(8,128)(2,1)S(1)} %collective-permute-done.13.refs_2_, ...), custom_call_target="tpu_custom_call" | custom-call | flops 1955000064 | bytes 1000 | tf_op jit(solution)/shard_map/query/pallas_call | solution.py:172
  51.7 1.4 %collective-permute-done.9 = bf16[128,1024]{1,0:T(8,128)(2,1)S(1)} collective-permute-done((bf16[128,1024]{1,0:T(8,128)(2,1)S(1)}, bf16[128,1024]{1,0:T(8,128)(2,1)S(1)}, u32[]{:S(2)}, u32[]{:S(2)}) %collective-permute-start.9) | collective-permute-done | bytes 262176 | tf_op jit(solution)/shard_map/ppermute | solution.py:372
  53.1 1.6 %collective-permute-start.16 = (bf16[64,4096]{1,0:T(8,128)(2,1)S(1)}, bf16[64,4096]{1,0:T(8,128)(2,1)S(1)}, u32[]{:S(2)}, u32[]{:S(2)}) collective-permute-start(bf16[64,4096]{1,0:T(8,128)(2,1)S(1)} %copy-done.5), channel_id=1, source_target_pairs={{0,4},{1,5},{2,0},{3,1},{4,8},{5,9},{6,2},{7,3},{8,12},{9,13},{10,... | collective-permute-start | bytes 1572872 | tf_op jit(solution)/shard_map/ppermute | solution.py:372
  55.3 1.6 %collective-permute-start.12 = (bf16[768,512]{1,0:T(8,128)(2,1)S(1)}, bf16[768,512]{1,0:T(8,128)(2,1)S(1)}, u32[]{:S(2)}, u32[]{:S(2)}) collective-permute-start(bf16[768,512]{1,0:T(8,128)(2,1)S(1)} %pad_maximum_fusion.3), channel_id=1, source_target_pairs={{0,16},{16,0},{1,17},{17,1},{2,18},{18,2},{3,19},{19,3},{4,20},{20... | collective-permute-start | bytes 2359304 | tf_op jit(solution)/shard_map/ppermute | solution.py:378
  56.8 3.5 %query.5 = (f32[512,512]{1,0:T(8,128)S(1)}, f32[512,512]{1,0:T(8,128)S(1)}, bf16[4,512,256]{2,1,0:T(8,128)(2,1)S(1)}, bf16[3,512,256]{2,1,0:T(8,128)(2,1)S(1)}) custom-call(s32[10]{0:T(128)S(1)} %get-tuple-element.39.scalar_ref, bf16[256,1024]{1,0:T(8,128)(2,1)S(1)} %copy-done.2, bf16[256,1024]{1,0:T(8,128)(2,1)S(1)} %collective-permute-done.2.refs_1_, ...), custom_call_target="tpu_custom_call" | custom-call | flops 1955000064 | bytes 1000 | tf_op jit(solution)/shard_map/query/pallas_call | solution.py:172
  60.4 5.4 %collective-permute-done.16.refs_4_ = bf16[64,4096]{1,0:T(8,128)(2,1)S(1)} collective-permute-done((bf16[64,4096]{1,0:T(8,128)(2,1)S(1)}, bf16[64,4096]{1,0:T(8,128)(2,1)S(1)}, u32[]{:S(2)}, u32[]{:S(2)}) %collective-permute-start.16) | collective-permute-done | bytes 524320 | tf_op jit(solution)/shard_map/ppermute | solution.py:372
  67.1 6.0 %collective-permute-done.12.refs_1_ = bf16[768,512]{1,0:T(8,128)(2,1)S(1)} collective-permute-done((bf16[768,512]{1,0:T(8,128)(2,1)S(1)}, bf16[768,512]{1,0:T(8,128)(2,1)S(1)}, u32[]{:S(2)}, u32[]{:S(2)}) %collective-permute-start.12) | collective-permute-done | bytes 786464 | tf_op jit(solution)/shard_map/ppermute | solution.py:378
  73.1 3.3 %query.7 = (f32[512,512]{1,0:T(8,128)S(1)}, f32[512,512]{1,0:T(8,128)S(1)}) custom-call(s32[10]{0:T(128)S(1)} %get-tuple-element.51.scalar_ref, bf16[256,1024]{1,0:T(8,128)(2,1)S(1)} %copy-done.2, bf16[768,512]{1,0:T(8,128)(2,1)S(1)} %collective-permute-done.12.refs_1_, bf16[512,4096]{1,0:T(8,128)(2,1)} %collective-permute-done.6.refs_5_.refs_9_.refs_3_.refs_2_, ...), custom_call_target="tpu_custom_call" | custom-call | flops 1955000064 | bytes 1000 | tf_op jit(solution)/shard_map/query/pallas_call | solution.py:172
  78.6 6.8 %attend.2.refs_0_ = bf16[512,512]{1,0:T(8,128)(2,1)S(1)} custom-call(f32[3]{0:T(128)S(1)} %compare_select_fusion.9.bias_ref, s32[3]{0:T(128)S(1)} %compare_convert_fusion.swap_ref, f32[512,512]{1,0:T(8,128)S(1)} %get-tuple-element.47.refs_0_, f32[512,512]{1,0:T(8,128)S(1)} %collective-permute-done.10.refs_1_, ...), custom_call_target="tpu_custom_call" | custom-call | flops 3910000128 | bytes 1000 | tf_op jit(solution)/shard_map/attend/pallas_call | solution.py:260
  85.4 5.5 %collective-permute-done.19.refs_7_ = bf16[64,4096]{1,0:T(8,128)(2,1)S(1)} collective-permute-done((bf16[64,4096]{1,0:T(8,128)(2,1)S(1)}, bf16[64,4096]{1,0:T(8,128)(2,1)S(1)}, u32[]{:S(2)}, u32[]{:S(2)}) %collective-permute-start.19) | collective-permute-done | bytes 524320 | tf_op jit(solution)/shard_map/ppermute | solution.py:372
  93.1 6.8 %attend.3.refs_1_ = bf16[512,512]{1,0:T(8,128)(2,1)S(1)} custom-call(f32[3]{0:T(128)S(1)} %compare_select_fusion.9.bias_ref, s32[3]{0:T(128)S(1)} %compare_convert_fusion.swap_ref, f32[512,512]{1,0:T(8,128)S(1)} %get-tuple-element.55.refs_0_, f32[512,512]{1,0:T(8,128)S(1)} %collective-permute-done.14.refs_1_, ...), custom_call_target="tpu_custom_call" | custom-call | flops 3910000128 | bytes 1000 | tf_op jit(solution)/shard_map/attend/pallas_call | solution.py:260
  99.9 4.4 %collective-permute-done.22.refs_10_ = bf16[64,4096]{1,0:T(8,128)(2,1)S(1)} collective-permute-done((bf16[64,4096]{1,0:T(8,128)(2,1)S(1)}, bf16[64,4096]{1,0:T(8,128)(2,1)S(1)}, u32[]{:S(2)}, u32[]{:S(2)}) %collective-permute-start.22) | collective-permute-done | bytes 524320 | tf_op jit(solution)/shard_map/ppermute | solution.py:372
  105.6 1.6 %collective-permute-start.25 = (bf16[32,4096]{1,0:T(8,128)(2,1)S(1)}, bf16[32,4096]{1,0:T(8,128)(2,1)S(1)}, u32[]{:S(2)}, u32[]{:S(2)}) collective-permute-start(bf16[32,4096]{1,0:T(8,128)(2,1)S(1)} %slice.62), channel_id=1, source_target_pairs={{0,4},{1,5},{2,0},{3,1},{4,8},{5,9},{6,2},{7,3},{8,12},{9,13},{10,... | collective-permute-start | bytes 786440 | tf_op jit(solution)/shard_map/ppermute | solution.py:372
  107.8 6.6 %collective-permute-done.25.refs_13_ = bf16[32,4096]{1,0:T(8,128)(2,1)S(1)} collective-permute-done((bf16[32,4096]{1,0:T(8,128)(2,1)S(1)}, bf16[32,4096]{1,0:T(8,128)(2,1)S(1)}, u32[]{:S(2)}, u32[]{:S(2)}) %collective-permute-start.25) | collective-permute-done | bytes 262176 | tf_op jit(solution)/shard_map/ppermute | solution.py:372
  117.3 9.4 %project.1 = bf16[512,4096]{1,0:T(8,128)(2,1)} custom-call(s32[18]{0:T(128)S(1)} %pad_add_fusion.place_ref, bf16[512,512]{1,0:T(8,128)(2,1)S(1)} %attend.2.refs_0_, bf16[512,512]{1,0:T(8,128)(2,1)S(1)} %attend.3.refs_1_, bf16[64,4096]{1,0:T(8,128)(2,1)S(1)} %copy-done.5, bf16[64,4096]{1,0:T(8,128)(2,1)S(1)} %collective-permute-done.15.refs_3_, ...), custom_call_target="tpu_custom_call" | custom-call | flops 4294967296 | bytes 13631488 | tf_op jit(solution)/shard_map/project/pallas_call | solution.py:331
  (93 shorter events, 21.4 us)
Async XLA Ops:
  0.0 36.0 %collective-permute-start.6 = (bf16[512,4096]{1,0:T(8,128)(2,1)}, bf16[512,4096]{1,0:T(8,128)(2,1)}, u32[]{:S(2)}, u32[]{:S(2)}) collective-permute-start(bf16[512,4096]{1,0:T(8,128)(2,1)} %refs_3_.1), channel_id=1, source_target_pairs={{0,1},{1,0},{2,3},{3,2},{4,5},{5,4},{6,7},{7,6},{8,9},{9,8},{10,11... | collective-permute-start | bytes 12582920 | tf_op jit(solution)/shard_map/ppermute | solution.py:372
  3.4 15.2 %collective-permute-start = (bf16[256,1024]{1,0:T(8,128)(2,1)S(1)}, bf16[256,1024]{1,0:T(8,128)(2,1)S(1)}, u32[]{:S(2)}, u32[]{:S(2)}) collective-permute-start(bf16[256,1024]{1,0:T(8,128)(2,1)S(1)} %pack.1.refs_4_), channel_id=1, source_target_pairs={{0,4},{1,5},{2,0},{3,1},{4,8},{5,9},{6,2},{7,3},{8,12},{9,13},{10,... | collective-permute-start | bytes 1572872 | tf_op jit(solution)/shard_map/ppermute | solution.py:372
  6.0 14.3 %collective-permute-start.3 = (bf16[256,1024]{1,0:T(8,128)(2,1)S(1)}, bf16[256,1024]{1,0:T(8,128)(2,1)S(1)}, u32[]{:S(2)}, u32[]{:S(2)}) collective-permute-start(bf16[256,1024]{1,0:T(8,128)(2,1)S(1)} %pack.1.refs_4_), channel_id=1, source_target_pairs={{0,2},{1,3},{2,6},{3,7},{4,0},{5,1},{6,10},{7,11},{8,4},{9,5},{10,... | collective-permute-start | bytes 1572872 | tf_op jit(solution)/shard_map/ppermute | solution.py:372
  18.6 13.8 %collective-permute-start.1 = (bf16[256,1024]{1,0:T(8,128)(2,1)S(1)}, bf16[256,1024]{1,0:T(8,128)(2,1)S(1)}, u32[]{:S(2)}, u32[]{:S(2)}) collective-permute-start(bf16[256,1024]{1,0:T(8,128)(2,1)S(1)} %collective-permute-done.refs_1_.refs_5_), channel_id=1, source_target_pairs={{0,4},{1,5},{2,0},{3,1},{4,8},{5,9},{6,2},{7,3},{8,12},{9,13},{10,... | collective-permute-start | bytes 1572872 | tf_op jit(solution)/shard_map/ppermute | solution.py:372
  20.4 13.6 %collective-permute-start.4 = (bf16[256,1024]{1,0:T(8,128)(2,1)S(1)}, bf16[256,1024]{1,0:T(8,128)(2,1)S(1)}, u32[]{:S(2)}, u32[]{:S(2)}) collective-permute-start(bf16[256,1024]{1,0:T(8,128)(2,1)S(1)} %collective-permute-done.3.refs_2_.refs_6_), channel_id=1, source_target_pairs={{0,2},{1,3},{2,6},{3,7},{4,0},{5,1},{6,10},{7,11},{8,4},{9,5},{10,... | collective-permute-start | bytes 1572872 | tf_op jit(solution)/shard_map/ppermute | solution.py:372
  20.7 19.3 %collective-permute-start.7 = (bf16[512,512]{1,0:T(8,128)(2,1)S(1)}, bf16[512,512]{1,0:T(8,128)(2,1)S(1)}, u32[]{:S(2)}, u32[]{:S(2)}) collective-permute-start(bf16[512,512]{1,0:T(8,128)(2,1)S(1)} %pad_maximum_fusion.4), channel_id=1, source_target_pairs={{0,16},{16,0},{1,17},{17,1},{2,18},{18,2},{3,19},{19,3},{4,20},{20... | collective-permute-start | bytes 1572872 | tf_op jit(solution)/shard_map/ppermute | solution.py:378
  32.3 12.9 %collective-permute-start.2 = (bf16[256,1024]{1,0:T(8,128)(2,1)S(1)}, bf16[256,1024]{1,0:T(8,128)(2,1)S(1)}, u32[]{:S(2)}, u32[]{:S(2)}) collective-permute-start(bf16[256,1024]{1,0:T(8,128)(2,1)S(1)} %collective-permute-done.1.refs_3_.refs_7_), channel_id=1, source_target_pairs={{0,4},{1,5},{2,0},{3,1},{4,8},{5,9},{6,2},{7,3},{8,12},{9,13},{10,... | collective-permute-start | bytes 1572872 | tf_op jit(solution)/shard_map/ppermute | solution.py:372
  33.9 12.7 %collective-permute-start.5 = (bf16[256,1024]{1,0:T(8,128)(2,1)S(1)}, bf16[256,1024]{1,0:T(8,128)(2,1)S(1)}, u32[]{:S(2)}, u32[]{:S(2)}) collective-permute-start(bf16[256,1024]{1,0:T(8,128)(2,1)S(1)} %collective-permute-done.4.refs_4_.refs_8_), channel_id=1, source_target_pairs={{0,2},{1,3},{2,6},{3,7},{4,0},{5,1},{6,10},{7,11},{8,4},{9,5},{10,... | collective-permute-start | bytes 1572872 | tf_op jit(solution)/shard_map/ppermute | solution.py:372
  34.5 13.0 %collective-permute-start.13 = (bf16[512,512]{1,0:T(8,128)(2,1)S(1)}, bf16[512,512]{1,0:T(8,128)(2,1)S(1)}, u32[]{:S(2)}, u32[]{:S(2)}) collective-permute-start(bf16[512,512]{1,0:T(8,128)(2,1)S(1)} %pad_maximum_fusion.5), channel_id=1, source_target_pairs={{0,16},{16,0},{1,17},{17,1},{2,18},{18,2},{3,19},{19,3},{4,20},{20... | collective-permute-start | bytes 1572872 | tf_op jit(solution)/shard_map/ppermute | solution.py:378
  47.4 29.1 %collective-permute-start.15 = (bf16[64,4096]{1,0:T(8,128)(2,1)S(1)}, bf16[64,4096]{1,0:T(8,128)(2,1)S(1)}, u32[]{:S(2)}, u32[]{:S(2)}) collective-permute-start(bf16[64,4096]{1,0:T(8,128)(2,1)S(1)} %copy-done.5), channel_id=1, source_target_pairs={{0,1},{1,0},{2,3},{3,2},{4,5},{5,4},{6,7},{7,6},{8,9},{9,8},{10,11... | collective-permute-start | bytes 1572872 | tf_op jit(solution)/shard_map/ppermute | solution.py:372
  53.1 12.7 %collective-permute-start.16 = (bf16[64,4096]{1,0:T(8,128)(2,1)S(1)}, bf16[64,4096]{1,0:T(8,128)(2,1)S(1)}, u32[]{:S(2)}, u32[]{:S(2)}) collective-permute-start(bf16[64,4096]{1,0:T(8,128)(2,1)S(1)} %copy-done.5), channel_id=1, source_target_pairs={{0,4},{1,5},{2,0},{3,1},{4,8},{5,9},{6,2},{7,3},{8,12},{9,13},{10,... | collective-permute-start | bytes 1572872 | tf_op jit(solution)/shard_map/ppermute | solution.py:372
  54.7 12.2 %collective-permute-start.17 = (bf16[64,4096]{1,0:T(8,128)(2,1)S(1)}, bf16[64,4096]{1,0:T(8,128)(2,1)S(1)}, u32[]{:S(2)}, u32[]{:S(2)}) collective-permute-start(bf16[64,4096]{1,0:T(8,128)(2,1)S(1)} %copy-done.5), channel_id=1, source_target_pairs={{0,2},{1,3},{2,6},{3,7},{4,0},{5,1},{6,10},{7,11},{8,4},{9,5},{10,... | collective-permute-start | bytes 1572872 | tf_op jit(solution)/shard_map/ppermute | solution.py:372
  55.3 17.8 %collective-permute-start.12 = (bf16[768,512]{1,0:T(8,128)(2,1)S(1)}, bf16[768,512]{1,0:T(8,128)(2,1)S(1)}, u32[]{:S(2)}, u32[]{:S(2)}) collective-permute-start(bf16[768,512]{1,0:T(8,128)(2,1)S(1)} %pad_maximum_fusion.3), channel_id=1, source_target_pairs={{0,16},{16,0},{1,17},{17,1},{2,18},{18,2},{3,19},{19,3},{4,20},{20... | collective-permute-start | bytes 2359304 | tf_op jit(solution)/shard_map/ppermute | solution.py:378
  60.3 18.3 %collective-permute-start.10 = (f32[512,512]{1,0:T(8,128)S(1)}, f32[512,512]{1,0:T(8,128)S(1)}, u32[]{:S(2)}, u32[]{:S(2)}) collective-permute-start(f32[512,512]{1,0:T(8,128)S(1)} %get-tuple-element.48), channel_id=1, source_target_pairs={{0,1},{1,0},{2,3},{3,2},{4,5},{5,4},{6,7},{7,6},{8,9},{9,8},{10,11... | collective-permute-start | bytes 3145736 | tf_op jit(solution)/shard_map/ppermute | solution.py:372
  65.8 12.1 %collective-permute-start.11 = (bf16[3,512,256]{2,1,0:T(8,128)(2,1)S(1)}, bf16[3,512,256]{2,1,0:T(8,128)(2,1)S(1)}, u32[]{:S(2)}, u32[]{:S(2)}) collective-permute-start(bf16[3,512,256]{2,1,0:T(8,128)(2,1)S(1)} %get-tuple-element.50), channel_id=1, source_target_pairs={{0,1},{1,0},{2,3},{3,2},{4,5},{5,4},{6,7},{7,6},{8,9},{9,8},{10,11... | collective-permute-start | bytes 2359304 | tf_op jit(solution)/shard_map/ppermute | solution.py:372
  67.0 23.9 %collective-permute-start.18 = (bf16[128,4096]{1,0:T(8,128)(2,1)S(1)}, bf16[128,4096]{1,0:T(8,128)(2,1)S(1)}, u32[]{:S(2)}, u32[]{:S(2)}) collective-permute-start(bf16[128,4096]{1,0:T(8,128)(2,1)S(1)} %pad_maximum_fusion), channel_id=1, source_target_pairs={{0,1},{1,0},{2,3},{3,2},{4,5},{5,4},{6,7},{7,6},{8,9},{9,8},{10,11... | collective-permute-start | bytes 3145736 | tf_op jit(solution)/shard_map/ppermute | solution.py:372
  76.4 16.6 %collective-permute-start.14 = (f32[512,512]{1,0:T(8,128)S(1)}, f32[512,512]{1,0:T(8,128)S(1)}, u32[]{:S(2)}, u32[]{:S(2)}) collective-permute-start(f32[512,512]{1,0:T(8,128)S(1)} %get-tuple-element.56), channel_id=1, source_target_pairs={{0,1},{1,0},{2,3},{3,2},{4,5},{5,4},{6,7},{7,6},{8,9},{9,8},{10,11... | collective-permute-start | bytes 3145736 | tf_op jit(solution)/shard_map/ppermute | solution.py:372
  76.5 14.3 %collective-permute-start.19 = (bf16[64,4096]{1,0:T(8,128)(2,1)S(1)}, bf16[64,4096]{1,0:T(8,128)(2,1)S(1)}, u32[]{:S(2)}, u32[]{:S(2)}) collective-permute-start(bf16[64,4096]{1,0:T(8,128)(2,1)S(1)} %collective-permute-done.16.refs_4_), channel_id=1, source_target_pairs={{0,4},{1,5},{2,0},{3,1},{4,8},{5,9},{6,2},{7,3},{8,12},{9,13},{10,... | collective-permute-start | bytes 1572872 | tf_op jit(solution)/shard_map/ppermute | solution.py:372
  77.9 14.3 %collective-permute-start.20 = (bf16[64,4096]{1,0:T(8,128)(2,1)S(1)}, bf16[64,4096]{1,0:T(8,128)(2,1)S(1)}, u32[]{:S(2)}, u32[]{:S(2)}) collective-permute-start(bf16[64,4096]{1,0:T(8,128)(2,1)S(1)} %collective-permute-done.17.refs_6_), channel_id=1, source_target_pairs={{0,2},{1,3},{2,6},{3,7},{4,0},{5,1},{6,10},{7,11},{8,4},{9,5},{10,... | collective-permute-start | bytes 1572872 | tf_op jit(solution)/shard_map/ppermute | solution.py:372
  90.9 13.5 %collective-permute-start.22 = (bf16[64,4096]{1,0:T(8,128)(2,1)S(1)}, bf16[64,4096]{1,0:T(8,128)(2,1)S(1)}, u32[]{:S(2)}, u32[]{:S(2)}) collective-permute-start(bf16[64,4096]{1,0:T(8,128)(2,1)S(1)} %collective-permute-done.19.refs_7_), channel_id=1, source_target_pairs={{0,4},{1,5},{2,0},{3,1},{4,8},{5,9},{6,2},{7,3},{8,12},{9,13},{10,... | collective-permute-start | bytes 1572872 | tf_op jit(solution)/shard_map/ppermute | solution.py:372
  92.2 13.2 %collective-permute-start.23 = (bf16[64,4096]{1,0:T(8,128)(2,1)S(1)}, bf16[64,4096]{1,0:T(8,128)(2,1)S(1)}, u32[]{:S(2)}, u32[]{:S(2)}) collective-permute-start(bf16[64,4096]{1,0:T(8,128)(2,1)S(1)} %collective-permute-done.20.refs_9_), channel_id=1, source_target_pairs={{0,2},{1,3},{2,6},{3,7},{4,0},{5,1},{6,10},{7,11},{8,4},{9,5},{10,... | collective-permute-start | bytes 1572872 | tf_op jit(solution)/shard_map/ppermute | solution.py:372
  93.0 12.6 %collective-permute-start.21 = (bf16[128,4096]{1,0:T(8,128)(2,1)S(1)}, bf16[128,4096]{1,0:T(8,128)(2,1)S(1)}, u32[]{:S(2)}, u32[]{:S(2)}) collective-permute-start(bf16[128,4096]{1,0:T(8,128)(2,1)S(1)} %pad_maximum_fusion.1), channel_id=1, source_target_pairs={{0,1},{1,0},{2,3},{3,2},{4,5},{5,4},{6,7},{7,6},{8,9},{9,8},{10,11... | collective-permute-start | bytes 3145736 | tf_op jit(solution)/shard_map/ppermute | solution.py:372
  105.5 11.8 %collective-permute-start.24 = (bf16[128,4096]{1,0:T(8,128)(2,1)S(1)}, bf16[128,4096]{1,0:T(8,128)(2,1)S(1)}, u32[]{:S(2)}, u32[]{:S(2)}) collective-permute-start(bf16[128,4096]{1,0:T(8,128)(2,1)S(1)} %pad_maximum_fusion.2), channel_id=1, source_target_pairs={{0,1},{1,0},{2,3},{3,2},{4,5},{5,4},{6,7},{7,6},{8,9},{9,8},{10,11... | collective-permute-start | bytes 3145736 | tf_op jit(solution)/shard_map/ppermute | solution.py:372
  105.6 8.7 %collective-permute-start.25 = (bf16[32,4096]{1,0:T(8,128)(2,1)S(1)}, bf16[32,4096]{1,0:T(8,128)(2,1)S(1)}, u32[]{:S(2)}, u32[]{:S(2)}) collective-permute-start(bf16[32,4096]{1,0:T(8,128)(2,1)S(1)} %slice.62), channel_id=1, source_target_pairs={{0,4},{1,5},{2,0},{3,1},{4,8},{5,9},{6,2},{7,3},{8,12},{9,13},{10,... | collective-permute-start | bytes 786440 | tf_op jit(solution)/shard_map/ppermute | solution.py:372
  (11 other events, 99.1 us)

commit v4 on v3

--- a/solution.py
+++ b/solution.py
@@ -446,27 +446,29 @@
     )
     queries = [(ours, swap(theirs))]
     picked = (picked, swap(given))
-    theirs, ours = part(1, crossed, 1, second)
-    queries.append((ours, swap(theirs)))
 
     pieces = [(output_weight, 0, rows), (swap(output_weight), 0, rows)]
     down, up = held_back(output_weight, *last), held_back(output_weight, *last)
     attention = []
     behind = [pieces[1][0], given]
     for step in range(1, half):
+        came = [down, up]
         down, up = send(down, ahead), send(up, back)
         pair = jnp.concatenate([down, up], 0)
-        if step > 1:
-            attention.append(attend(queries[step - 2], picked, bias, swapped))
-            behind.append(attention[-1])
+        if step == 2:
+            attention.append(attend(queries[0], picked, held_back(bias, *came), swapped))
+            behind.append(attention[0])
         if step == half - 1:
-            pair = held_back(pair, attention[-1])
+            second = lax.optimization_barrier((*second, *attention, *came))[:2]
+            theirs, ours = part(1, crossed, 1, second)
+            attention.append(attend((ours, swap(theirs)), picked, bias, swapped))
         other = swap(pair)
         pieces += [(down, 0, rows), (other, 0, rows), (up, 0, rows), (other, rows, rows)]
         down, up = held_back(down, *behind), held_back(up, *behind)
         behind = [other]
     down, up = send(down[:cut], ahead), send(up[cut:], back)
-    pieces += [(down, 0, cut), (swap(down), 0, cut), (up, 0, cut), (swap(up), 0, cut)]
+    got = [swap(held_back(x, attention[-1])) for x in (down, up)]
+    pieces += [(down, 0, cut), (got[0], 0, cut), (up, 0, cut), (got[1], 0, cut)]
     return project(attention, row_of, pieces)
 
 

time: 127 us -> 116 us (0.913)
  waiting for transfers between devices: 58.5 us -> 46.5 us
    ppermute x26, waiting for transfers between devices: 52.5 us -> 42.7 us  [send(): return lax.ppermute(array, 'ctx', to)]
    ppermute x3, waiting for transfers between devices: 6.04 us -> 3.8 us  [cross(): return lax.ppermute(array, 'groups', [(0, 1), (1, 0)])]
  transfers between devices with their start and end apart: 29 -> 29, of which waited for: 15 -> 15; matrix products, arithmetic and copies ran while one was open for 3% -> 4% of each run, Pallas kernels for 22% -> 25%
where the time goes in v4:
time: 116 us
  waiting for transfers between devices  46.5 us (40%)
  Pallas kernels  37.8 us (33%)
  starting transfers between devices  23.8 us (21%)
  local copies, waits for them, and re-layouts  4.4 us (4%)
  other arithmetic  2.86 us (2%)
    ppermute x26, waiting for transfers between devices, send(): return lax.ppermute(array, 'ctx', to)  42.7 us
    ppermute x26, starting transfers between devices, send(): return lax.ppermute(array, 'ctx', to)  19 us
    pallas_call x4, Pallas kernels, query(): pl.pallas_call(functools.partial(query_kernel, depth, where, bool(totals)...  14.7 us
    pallas_call x2, Pallas kernels, attend(): pl.pallas_call(functools.partial(attend_kernel, math.log2(math.e) / math....  13.6 us
    pallas_call x1, Pallas kernels, project(): pl.pallas_call(functools.partial(project_kernel, len(attention), len(arra...  9.41 us
    ppermute x3, starting transfers between devices, cross(): return lax.ppermute(array, 'groups', [(0, 1), (1, 0)])  4.8 us
    ppermute x3, waiting for transfers between devices, cross(): return lax.ppermute(array, 'groups', [(0, 1), (1, 0)])  3.8 us
    unnamed x13, local copies, waits for them, and re-layouts  2.88 us
  transfers between devices with their start and end apart: 29, of which 15 were waited for; matrix products, arithmetic and copies ran while one was open for 4% of the time, Pallas kernels for 25%

profile of v4, /device:TPU:0, one launch (start us, length us, event | category | flops | bytes accessed | tf_op | source)
XLA Modules:
  0.0 115.8 jit_solution(10749302653938118903)
XLA Ops:
  3.4 2.6 %collective-permute-start.3 = (bf16[256,1024]{1,0:T(8,128)(2,1)S(1)}, bf16[256,1024]{1,0:T(8,128)(2,1)S(1)}, u32[]{:S(2)}, u32[]{:S(2)}) collective-permute-start(bf16[256,1024]{1,0:T(8,128)(2,1)S(1)} %pack.1.refs_4_), channel_id=1, source_target_pairs={{0,2},{1,3},{2,6},{3,7},{4,0},{5,1},{6,10},{7,11},{8,4},{9,5},{10,... | collective-permute-start | bytes 1572872 | tf_op jit(solution)/shard_map/ppermute | solution.py:372
  9.9 8.7 %collective-permute-done.3.refs_2_.refs_6_ = bf16[256,1024]{1,0:T(8,128)(2,1)S(1)} collective-permute-done((bf16[256,1024]{1,0:T(8,128)(2,1)S(1)}, bf16[256,1024]{1,0:T(8,128)(2,1)S(1)}, u32[]{:S(2)}, u32[]{:S(2)}) %collective-permute-start.3) | collective-permute-done | bytes 524320 | tf_op jit(solution)/shard_map/ppermute | solution.py:372
  18.6 1.7 %collective-permute-start.4 = (bf16[256,1024]{1,0:T(8,128)(2,1)S(1)}, bf16[256,1024]{1,0:T(8,128)(2,1)S(1)}, u32[]{:S(2)}, u32[]{:S(2)}) collective-permute-start(bf16[256,1024]{1,0:T(8,128)(2,1)S(1)} %collective-permute-done.3.refs_2_.refs_6_), channel_id=1, source_target_pairs={{0,2},{1,3},{2,6},{3,7},{4,0},{5,1},{6,10},{7,11},{8,4},{9,5},{10,... | collective-permute-start | bytes 1572872 | tf_op jit(solution)/shard_map/ppermute | solution.py:372
  20.7 1.7 %collective-permute-start.6 = (bf16[512,512]{1,0:T(8,128)(2,1)S(1)}, bf16[512,512]{1,0:T(8,128)(2,1)S(1)}, u32[]{:S(2)}, u32[]{:S(2)}) collective-permute-start(bf16[512,512]{1,0:T(8,128)(2,1)S(1)} %pad_maximum_fusion.4), channel_id=1, source_target_pairs={{0,16},{16,0},{1,17},{17,1},{2,18},{18,2},{3,19},{19,3},{4,20},{20... | collective-permute-start | bytes 1572872 | tf_op jit(solution)/shard_map/ppermute | solution.py:378
  22.5 9.9 %collective-permute-done.4.refs_4_.refs_8_ = bf16[256,1024]{1,0:T(8,128)(2,1)S(1)} collective-permute-done((bf16[256,1024]{1,0:T(8,128)(2,1)S(1)}, bf16[256,1024]{1,0:T(8,128)(2,1)S(1)}, u32[]{:S(2)}, u32[]{:S(2)}) %collective-permute-start.4) | collective-permute-done | bytes 524320 | tf_op jit(solution)/shard_map/ppermute | solution.py:372
  36.0 3.9 %query.4 = (f32[512,512]{1,0:T(8,128)S(1)}, f32[512,512]{1,0:T(8,128)S(1)}) custom-call(s32[12]{0:T(128)S(1)} %get-tuple-element.43.scalar_ref, bf16[256,1024]{1,0:T(8,128)(2,1)S(1)} %copy-done.2, bf16[256,1024]{1,0:T(8,128)(2,1)S(1)} %collective-permute-done.refs_1_.refs_5_, bf16[256,1024]{1,0:T(8,128)(2,1)S(1)} %collective-permute-done.3.refs_2_.refs_6_, ...), custom_call_target="tpu_custom_call" | custom-call | flops 1955000064 | bytes 1000 | tf_op jit(solution)/shard_map/query/pallas_call | solution.py:172
  40.0 5.3 %collective-permute-done.8.refs_2_ = bf16[256,1024]{1,0:T(8,128)(2,1)S(1)} collective-permute-done((bf16[256,1024]{1,0:T(8,128)(2,1)S(1)}, bf16[256,1024]{1,0:T(8,128)(2,1)S(1)}, u32[]{:S(2)}, u32[]{:S(2)}) %collective-permute-start.8) | collective-permute-done | bytes 524320 | tf_op jit(solution)/shard_map/ppermute | solution.py:372
  46.3 1.6 %collective-permute-start.9 = (bf16[128,1024]{1,0:T(8,128)(2,1)S(1)}, bf16[128,1024]{1,0:T(8,128)(2,1)S(1)}, u32[]{:S(2)}, u32[]{:S(2)}) collective-permute-start(bf16[128,1024]{1,0:T(8,128)(2,1)S(1)} %slice.56), channel_id=1, source_target_pairs={{0,2},{1,3},{2,6},{3,7},{4,0},{5,1},{6,10},{7,11},{8,4},{9,5},{10,... | collective-permute-start | bytes 786440 | tf_op jit(solution)/shard_map/ppermute | solution.py:372
  48.4 3.9 %query.5 = (f32[512,512]{1,0:T(8,128)S(1)}, f32[512,512]{1,0:T(8,128)S(1)}) custom-call(s32[12]{0:T(128)S(1)} %get-tuple-element.50.scalar_ref, bf16[256,1024]{1,0:T(8,128)(2,1)S(1)} %copy-done.2, bf16[512,512]{1,0:T(8,128)(2,1)S(1)} %collective-permute-done.6.refs_1_, bf16[512,512]{1,0:T(8,128)(2,1)S(1)} %collective-permute-done.10.refs_2_, ...), custom_call_target="tpu_custom_call" | custom-call | flops 1955000064 | bytes 1000 | tf_op jit(solution)/shard_map/query/pallas_call | solution.py:172
  52.7 1.6 %collective-permute-done.7 = bf16[128,1024]{1,0:T(8,128)(2,1)S(1)} collective-permute-done((bf16[128,1024]{1,0:T(8,128)(2,1)S(1)}, bf16[128,1024]{1,0:T(8,128)(2,1)S(1)}, u32[]{:S(2)}, u32[]{:S(2)}) %collective-permute-start.7) | collective-permute-done | bytes 262176 | tf_op jit(solution)/shard_map/ppermute | solution.py:372
  54.3 1.6 %collective-permute-start.13 = (bf16[64,4096]{1,0:T(8,128)(2,1)S(1)}, bf16[64,4096]{1,0:T(8,128)(2,1)S(1)}, u32[]{:S(2)}, u32[]{:S(2)}) collective-permute-start(bf16[64,4096]{1,0:T(8,128)(2,1)S(1)} %copy-done.5), channel_id=1, source_target_pairs={{0,2},{1,3},{2,6},{3,7},{4,0},{5,1},{6,10},{7,11},{8,4},{9,5},{10,... | collective-permute-start | bytes 1572872 | tf_op jit(solution)/shard_map/ppermute | solution.py:372
  56.4 3.5 %query.6 = (f32[512,512]{1,0:T(8,128)S(1)}, f32[512,512]{1,0:T(8,128)S(1)}, bf16[4,512,256]{2,1,0:T(8,128)(2,1)S(1)}, bf16[3,512,256]{2,1,0:T(8,128)(2,1)S(1)}) custom-call(s32[10]{0:T(128)S(1)} %get-tuple-element.54.scalar_ref, bf16[256,1024]{1,0:T(8,128)(2,1)S(1)} %copy-done.2, bf16[256,1024]{1,0:T(8,128)(2,1)S(1)} %collective-permute-done.2.refs_1_, ...), custom_call_target="tpu_custom_call" | custom-call | flops 1955000064 | bytes 1000 | tf_op jit(solution)/shard_map/query/pallas_call | solution.py:172
  60.6 4.1 %collective-permute-done.13.refs_6_ = bf16[64,4096]{1,0:T(8,128)(2,1)S(1)} collective-permute-done((bf16[64,4096]{1,0:T(8,128)(2,1)S(1)}, bf16[64,4096]{1,0:T(8,128)(2,1)S(1)}, u32[]{:S(2)}, u32[]{:S(2)}) %collective-permute-start.13) | collective-permute-done | bytes 524320 | tf_op jit(solution)/shard_map/ppermute | solution.py:372
  66.1 1.6 %collective-permute-start.19 = (bf16[64,4096]{1,0:T(8,128)(2,1)S(1)}, bf16[64,4096]{1,0:T(8,128)(2,1)S(1)}, u32[]{:S(2)}, u32[]{:S(2)}) collective-permute-start(bf16[64,4096]{1,0:T(8,128)(2,1)S(1)} %collective-permute-done.13.refs_6_), channel_id=1, source_target_pairs={{0,2},{1,3},{2,6},{3,7},{4,0},{5,1},{6,10},{7,11},{8,4},{9,5},{10,... | collective-permute-start | bytes 1572872 | tf_op jit(solution)/shard_map/ppermute | solution.py:372
  68.3 1.6 %collective-permute-start.16 = (bf16[768,512]{1,0:T(8,128)(2,1)S(1)}, bf16[768,512]{1,0:T(8,128)(2,1)S(1)}, u32[]{:S(2)}, u32[]{:S(2)}) collective-permute-start(bf16[768,512]{1,0:T(8,128)(2,1)S(1)} %pad_maximum_fusion.3), channel_id=1, source_target_pairs={{0,16},{16,0},{1,17},{17,1},{2,18},{18,2},{3,19},{19,3},{4,20},{20... | collective-permute-start | bytes 2359304 | tf_op jit(solution)/shard_map/ppermute | solution.py:378
  69.9 6.8 %attend.2.refs_0_ = bf16[512,512]{1,0:T(8,128)(2,1)S(1)} custom-call(f32[3]{0:T(128)S(1)} %compare_select_fusion.9.bias_ref, s32[3]{0:T(128)S(1)} %compare_convert_fusion.swap_ref, f32[512,512]{1,0:T(8,128)S(1)} %get-tuple-element.59.refs_0_, f32[512,512]{1,0:T(8,128)S(1)} %collective-permute-done.14.refs_1_, ...), custom_call_target="tpu_custom_call" | custom-call | flops 3910000128 | bytes 1000 | tf_op jit(solution)/shard_map/attend/pallas_call | solution.py:260
  76.7 3.8 %collective-permute-done.19.refs_9_ = bf16[64,4096]{1,0:T(8,128)(2,1)S(1)} collective-permute-done((bf16[64,4096]{1,0:T(8,128)(2,1)S(1)}, bf16[64,4096]{1,0:T(8,128)(2,1)S(1)}, u32[]{:S(2)}, u32[]{:S(2)}) %collective-permute-start.19) | collective-permute-done | bytes 524320 | tf_op jit(solution)/shard_map/ppermute | solution.py:372
  82.2 1.6 %collective-permute-start.23 = (bf16[64,4096]{1,0:T(8,128)(2,1)S(1)}, bf16[64,4096]{1,0:T(8,128)(2,1)S(1)}, u32[]{:S(2)}, u32[]{:S(2)}) collective-permute-start(bf16[64,4096]{1,0:T(8,128)(2,1)S(1)} %collective-permute-done.19.refs_9_), channel_id=1, source_target_pairs={{0,2},{1,3},{2,6},{3,7},{4,0},{5,1},{6,10},{7,11},{8,4},{9,5},{10,... | collective-permute-start | bytes 1572872 | tf_op jit(solution)/shard_map/ppermute | solution.py:372
  83.9 3.8 %collective-permute-done.16.refs_1_ = bf16[768,512]{1,0:T(8,128)(2,1)S(1)} collective-permute-done((bf16[768,512]{1,0:T(8,128)(2,1)S(1)}, bf16[768,512]{1,0:T(8,128)(2,1)S(1)}, u32[]{:S(2)}, u32[]{:S(2)}) %collective-permute-start.16) | collective-permute-done | bytes 786464 | tf_op jit(solution)/shard_map/ppermute | solution.py:378
  87.7 3.3 %query.7 = (f32[512,512]{1,0:T(8,128)S(1)}, f32[512,512]{1,0:T(8,128)S(1)}) custom-call(s32[10]{0:T(128)S(1)} %get-tuple-element.62.scalar_ref, bf16[256,1024]{1,0:T(8,128)(2,1)S(1)} %copy-done.2, bf16[768,512]{1,0:T(8,128)(2,1)S(1)} %collective-permute-done.16.refs_1_, bf16[512,4096]{1,0:T(8,128)(2,1)} %collective-permute-done.5.refs_5_.refs_3_.refs_9_.refs_2_, ...), custom_call_target="tpu_custom_call" | custom-call | flops 1955000064 | bytes 1000 | tf_op jit(solution)/shard_map/query/pallas_call | solution.py:172
  91.1 3.7 %collective-permute-done.22.refs_10_ = bf16[64,4096]{1,0:T(8,128)(2,1)S(1)} collective-permute-done((bf16[64,4096]{1,0:T(8,128)(2,1)S(1)}, bf16[64,4096]{1,0:T(8,128)(2,1)S(1)}, u32[]{:S(2)}, u32[]{:S(2)}) %collective-permute-start.22) | collective-permute-done | bytes 524320 | tf_op jit(solution)/shard_map/ppermute | solution.py:372
  95.8 1.6 %collective-permute-start.27 = (bf16[32,4096]{1,0:T(8,128)(2,1)S(1)}, bf16[32,4096]{1,0:T(8,128)(2,1)S(1)}, u32[]{:S(2)}, u32[]{:S(2)}) collective-permute-start(bf16[32,4096]{1,0:T(8,128)(2,1)S(1)} %slice.63), channel_id=1, source_target_pairs={{0,2},{1,3},{2,6},{3,7},{4,0},{5,1},{6,10},{7,11},{8,4},{9,5},{10,... | collective-permute-start | bytes 786440 | tf_op jit(solution)/shard_map/ppermute | solution.py:372
  97.4 6.8 %attend.3.refs_1_ = bf16[512,512]{1,0:T(8,128)(2,1)S(1)} custom-call(f32[3]{0:T(128)S(1)} %compare_select_fusion.9.bias_ref, s32[3]{0:T(128)S(1)} %compare_convert_fusion.swap_ref, f32[512,512]{1,0:T(8,128)S(1)} %get-tuple-element.67.refs_0_, f32[512,512]{1,0:T(8,128)S(1)} %collective-permute-done.20.refs_1_, ...), custom_call_target="tpu_custom_call" | custom-call | flops 3910000128 | bytes 1000 | tf_op jit(solution)/shard_map/attend/pallas_call | solution.py:260
  106.2 9.4 %project.1 = bf16[512,4096]{1,0:T(8,128)(2,1)} custom-call(s32[18]{0:T(128)S(1)} %pad_add_fusion.place_ref, bf16[512,512]{1,0:T(8,128)(2,1)S(1)} %attend.2.refs_0_, bf16[512,512]{1,0:T(8,128)(2,1)S(1)} %attend.3.refs_1_, bf16[64,4096]{1,0:T(8,128)(2,1)S(1)} %copy-done.5, bf16[64,4096]{1,0:T(8,128)(2,1)S(1)} %collective-permute-done.12.refs_3_, ...), custom_call_target="tpu_custom_call" | custom-call | flops 4294967296 | bytes 13631488 | tf_op jit(solution)/shard_map/project/pallas_call | solution.py:331
  (93 shorter events, 21.2 us)
Async XLA Ops:
  0.0 36.0 %collective-permute-start.5 = (bf16[512,4096]{1,0:T(8,128)(2,1)}, bf16[512,4096]{1,0:T(8,128)(2,1)}, u32[]{:S(2)}, u32[]{:S(2)}) collective-permute-start(bf16[512,4096]{1,0:T(8,128)(2,1)} %refs_3_.1), channel_id=1, source_target_pairs={{0,1},{1,0},{2,3},{3,2},{4,5},{5,4},{6,7},{7,6},{8,9},{9,8},{10,11... | collective-permute-start | bytes 12582920 | tf_op jit(solution)/shard_map/ppermute | solution.py:372
  3.4 15.2 %collective-permute-start.3 = (bf16[256,1024]{1,0:T(8,128)(2,1)S(1)}, bf16[256,1024]{1,0:T(8,128)(2,1)S(1)}, u32[]{:S(2)}, u32[]{:S(2)}) collective-permute-start(bf16[256,1024]{1,0:T(8,128)(2,1)S(1)} %pack.1.refs_4_), channel_id=1, source_target_pairs={{0,2},{1,3},{2,6},{3,7},{4,0},{5,1},{6,10},{7,11},{8,4},{9,5},{10,... | collective-permute-start | bytes 1572872 | tf_op jit(solution)/shard_map/ppermute | solution.py:372
  6.0 14.3 %collective-permute-start = (bf16[256,1024]{1,0:T(8,128)(2,1)S(1)}, bf16[256,1024]{1,0:T(8,128)(2,1)S(1)}, u32[]{:S(2)}, u32[]{:S(2)}) collective-permute-start(bf16[256,1024]{1,0:T(8,128)(2,1)S(1)} %pack.1.refs_4_), channel_id=1, source_target_pairs={{0,4},{1,5},{2,0},{3,1},{4,8},{5,9},{6,2},{7,3},{8,12},{9,13},{10,... | collective-permute-start | bytes 1572872 | tf_op jit(solution)/shard_map/ppermute | solution.py:372
  18.6 13.8 %collective-permute-start.4 = (bf16[256,1024]{1,0:T(8,128)(2,1)S(1)}, bf16[256,1024]{1,0:T(8,128)(2,1)S(1)}, u32[]{:S(2)}, u32[]{:S(2)}) collective-permute-start(bf16[256,1024]{1,0:T(8,128)(2,1)S(1)} %collective-permute-done.3.refs_2_.refs_6_), channel_id=1, source_target_pairs={{0,2},{1,3},{2,6},{3,7},{4,0},{5,1},{6,10},{7,11},{8,4},{9,5},{10,... | collective-permute-start | bytes 1572872 | tf_op jit(solution)/shard_map/ppermute | solution.py:372
  20.3 13.6 %collective-permute-start.1 = (bf16[256,1024]{1,0:T(8,128)(2,1)S(1)}, bf16[256,1024]{1,0:T(8,128)(2,1)S(1)}, u32[]{:S(2)}, u32[]{:S(2)}) collective-permute-start(bf16[256,1024]{1,0:T(8,128)(2,1)S(1)} %collective-permute-done.refs_1_.refs_5_), channel_id=1, source_target_pairs={{0,4},{1,5},{2,0},{3,1},{4,8},{5,9},{6,2},{7,3},{8,12},{9,13},{10,... | collective-permute-start | bytes 1572872 | tf_op jit(solution)/shard_map/ppermute | solution.py:372
  20.7 19.2 %collective-permute-start.6 = (bf16[512,512]{1,0:T(8,128)(2,1)S(1)}, bf16[512,512]{1,0:T(8,128)(2,1)S(1)}, u32[]{:S(2)}, u32[]{:S(2)}) collective-permute-start(bf16[512,512]{1,0:T(8,128)(2,1)S(1)} %pad_maximum_fusion.4), channel_id=1, source_target_pairs={{0,16},{16,0},{1,17},{17,1},{2,18},{18,2},{3,19},{19,3},{4,20},{20... | collective-permute-start | bytes 1572872 | tf_op jit(solution)/shard_map/ppermute | solution.py:378
  32.4 12.9 %collective-permute-start.8 = (bf16[256,1024]{1,0:T(8,128)(2,1)S(1)}, bf16[256,1024]{1,0:T(8,128)(2,1)S(1)}, u32[]{:S(2)}, u32[]{:S(2)}) collective-permute-start(bf16[256,1024]{1,0:T(8,128)(2,1)S(1)} %collective-permute-done.4.refs_4_.refs_8_), channel_id=1, source_target_pairs={{0,2},{1,3},{2,6},{3,7},{4,0},{5,1},{6,10},{7,11},{8,4},{9,5},{10,... | collective-permute-start | bytes 1572872 | tf_op jit(solution)/shard_map/ppermute | solution.py:372
  33.9 12.4 %collective-permute-start.2 = (bf16[256,1024]{1,0:T(8,128)(2,1)S(1)}, bf16[256,1024]{1,0:T(8,128)(2,1)S(1)}, u32[]{:S(2)}, u32[]{:S(2)}) collective-permute-start(bf16[256,1024]{1,0:T(8,128)(2,1)S(1)} %collective-permute-done.1.refs_3_.refs_7_), channel_id=1, source_target_pairs={{0,4},{1,5},{2,0},{3,1},{4,8},{5,9},{6,2},{7,3},{8,12},{9,13},{10,... | collective-permute-start | bytes 1572872 | tf_op jit(solution)/shard_map/ppermute | solution.py:372
  34.5 13.9 %collective-permute-start.10 = (bf16[512,512]{1,0:T(8,128)(2,1)S(1)}, bf16[512,512]{1,0:T(8,128)(2,1)S(1)}, u32[]{:S(2)}, u32[]{:S(2)}) collective-permute-start(bf16[512,512]{1,0:T(8,128)(2,1)S(1)} %pad_maximum_fusion.5), channel_id=1, source_target_pairs={{0,16},{16,0},{1,17},{17,1},{2,18},{18,2},{3,19},{19,3},{4,20},{20... | collective-permute-start | bytes 1572872 | tf_op jit(solution)/shard_map/ppermute | solution.py:378
  54.3 10.3 %collective-permute-start.13 = (bf16[64,4096]{1,0:T(8,128)(2,1)S(1)}, bf16[64,4096]{1,0:T(8,128)(2,1)S(1)}, u32[]{:S(2)}, u32[]{:S(2)}) collective-permute-start(bf16[64,4096]{1,0:T(8,128)(2,1)S(1)} %copy-done.5), channel_id=1, source_target_pairs={{0,2},{1,3},{2,6},{3,7},{4,0},{5,1},{6,10},{7,11},{8,4},{9,5},{10,... | collective-permute-start | bytes 1572872 | tf_op jit(solution)/shard_map/ppermute | solution.py:372
  55.9 10.0 %collective-permute-start.11 = (bf16[64,4096]{1,0:T(8,128)(2,1)S(1)}, bf16[64,4096]{1,0:T(8,128)(2,1)S(1)}, u32[]{:S(2)}, u32[]{:S(2)}) collective-permute-start(bf16[64,4096]{1,0:T(8,128)(2,1)S(1)} %copy-done.5), channel_id=1, source_target_pairs={{0,4},{1,5},{2,0},{3,1},{4,8},{5,9},{6,2},{7,3},{8,12},{9,13},{10,... | collective-permute-start | bytes 1572872 | tf_op jit(solution)/shard_map/ppermute | solution.py:372
  56.3 9.8 %collective-permute-start.12 = (bf16[64,4096]{1,0:T(8,128)(2,1)S(1)}, bf16[64,4096]{1,0:T(8,128)(2,1)S(1)}, u32[]{:S(2)}, u32[]{:S(2)}) collective-permute-start(bf16[64,4096]{1,0:T(8,128)(2,1)S(1)} %copy-done.5), channel_id=1, source_target_pairs={{0,1},{1,0},{2,3},{3,2},{4,5},{5,4},{6,7},{7,6},{8,9},{9,8},{10,11... | collective-permute-start | bytes 1572872 | tf_op jit(solution)/shard_map/ppermute | solution.py:372
  59.9 8.4 %collective-permute-start.15 = (bf16[3,512,256]{2,1,0:T(8,128)(2,1)S(1)}, bf16[3,512,256]{2,1,0:T(8,128)(2,1)S(1)}, u32[]{:S(2)}, u32[]{:S(2)}) collective-permute-start(bf16[3,512,256]{2,1,0:T(8,128)(2,1)S(1)} %get-tuple-element.55), channel_id=1, source_target_pairs={{0,1},{1,0},{2,3},{3,2},{4,5},{5,4},{6,7},{7,6},{8,9},{9,8},{10,11... | collective-permute-start | bytes 2359304 | tf_op jit(solution)/shard_map/ppermute | solution.py:372
  60.5 9.4 %collective-permute-start.14 = (f32[512,512]{1,0:T(8,128)S(1)}, f32[512,512]{1,0:T(8,128)S(1)}, u32[]{:S(2)}, u32[]{:S(2)}) collective-permute-start(f32[512,512]{1,0:T(8,128)S(1)} %get-tuple-element.60), channel_id=1, source_target_pairs={{0,1},{1,0},{2,3},{3,2},{4,5},{5,4},{6,7},{7,6},{8,9},{9,8},{10,11... | collective-permute-start | bytes 3145736 | tf_op jit(solution)/shard_map/ppermute | solution.py:372
  66.0 14.4 %collective-permute-start.18 = (bf16[128,4096]{1,0:T(8,128)(2,1)S(1)}, bf16[128,4096]{1,0:T(8,128)(2,1)S(1)}, u32[]{:S(2)}, u32[]{:S(2)}) collective-permute-start(bf16[128,4096]{1,0:T(8,128)(2,1)S(1)} %pad_maximum_fusion), channel_id=1, source_target_pairs={{0,1},{1,0},{2,3},{3,2},{4,5},{5,4},{6,7},{7,6},{8,9},{9,8},{10,11... | collective-permute-start | bytes 3145736 | tf_op jit(solution)/shard_map/ppermute | solution.py:372
  66.1 14.3 %collective-permute-start.19 = (bf16[64,4096]{1,0:T(8,128)(2,1)S(1)}, bf16[64,4096]{1,0:T(8,128)(2,1)S(1)}, u32[]{:S(2)}, u32[]{:S(2)}) collective-permute-start(bf16[64,4096]{1,0:T(8,128)(2,1)S(1)} %collective-permute-done.13.refs_6_), channel_id=1, source_target_pairs={{0,2},{1,3},{2,6},{3,7},{4,0},{5,1},{6,10},{7,11},{8,4},{9,5},{10,... | collective-permute-start | bytes 1572872 | tf_op jit(solution)/shard_map/ppermute | solution.py:372
  67.7 14.0 %collective-permute-start.17 = (bf16[64,4096]{1,0:T(8,128)(2,1)S(1)}, bf16[64,4096]{1,0:T(8,128)(2,1)S(1)}, u32[]{:S(2)}, u32[]{:S(2)}) collective-permute-start(bf16[64,4096]{1,0:T(8,128)(2,1)S(1)} %collective-permute-done.11.refs_4_), channel_id=1, source_target_pairs={{0,4},{1,5},{2,0},{3,1},{4,8},{5,9},{6,2},{7,3},{8,12},{9,13},{10,... | collective-permute-start | bytes 1572872 | tf_op jit(solution)/shard_map/ppermute | solution.py:372
  68.3 19.4 %collective-permute-start.16 = (bf16[768,512]{1,0:T(8,128)(2,1)S(1)}, bf16[768,512]{1,0:T(8,128)(2,1)S(1)}, u32[]{:S(2)}, u32[]{:S(2)}) collective-permute-start(bf16[768,512]{1,0:T(8,128)(2,1)S(1)} %pad_maximum_fusion.3), channel_id=1, source_target_pairs={{0,16},{16,0},{1,17},{17,1},{2,18},{18,2},{3,19},{19,3},{4,20},{20... | collective-permute-start | bytes 2359304 | tf_op jit(solution)/shard_map/ppermute | solution.py:378
  81.7 13.2 %collective-permute-start.22 = (bf16[64,4096]{1,0:T(8,128)(2,1)S(1)}, bf16[64,4096]{1,0:T(8,128)(2,1)S(1)}, u32[]{:S(2)}, u32[]{:S(2)}) collective-permute-start(bf16[64,4096]{1,0:T(8,128)(2,1)S(1)} %collective-permute-done.17.refs_7_), channel_id=1, source_target_pairs={{0,4},{1,5},{2,0},{3,1},{4,8},{5,9},{6,2},{7,3},{8,12},{9,13},{10,... | collective-permute-start | bytes 1572872 | tf_op jit(solution)/shard_map/ppermute | solution.py:372
  82.2 12.9 %collective-permute-start.23 = (bf16[64,4096]{1,0:T(8,128)(2,1)S(1)}, bf16[64,4096]{1,0:T(8,128)(2,1)S(1)}, u32[]{:S(2)}, u32[]{:S(2)}) collective-permute-start(bf16[64,4096]{1,0:T(8,128)(2,1)S(1)} %collective-permute-done.19.refs_9_), channel_id=1, source_target_pairs={{0,2},{1,3},{2,6},{3,7},{4,0},{5,1},{6,10},{7,11},{8,4},{9,5},{10,... | collective-permute-start | bytes 1572872 | tf_op jit(solution)/shard_map/ppermute | solution.py:372
  83.9 11.4 %collective-permute-start.21 = (bf16[128,4096]{1,0:T(8,128)(2,1)S(1)}, bf16[128,4096]{1,0:T(8,128)(2,1)S(1)}, u32[]{:S(2)}, u32[]{:S(2)}) collective-permute-start(bf16[128,4096]{1,0:T(8,128)(2,1)S(1)} %pad_maximum_fusion.1), channel_id=1, source_target_pairs={{0,1},{1,0},{2,3},{3,2},{4,5},{5,4},{6,7},{7,6},{8,9},{9,8},{10,11... | collective-permute-start | bytes 3145736 | tf_op jit(solution)/shard_map/ppermute | solution.py:372
  95.1 11.1 %collective-permute-start.24 = (bf16[128,4096]{1,0:T(8,128)(2,1)S(1)}, bf16[128,4096]{1,0:T(8,128)(2,1)S(1)}, u32[]{:S(2)}, u32[]{:S(2)}) collective-permute-start(bf16[128,4096]{1,0:T(8,128)(2,1)S(1)} %pad_maximum_fusion.2), channel_id=1, source_target_pairs={{0,1},{1,0},{2,3},{3,2},{4,5},{5,4},{6,7},{7,6},{8,9},{9,8},{10,11... | collective-permute-start | bytes 3145736 | tf_op jit(solution)/shard_map/ppermute | solution.py:372
  95.3 9.0 %collective-permute-start.25 = (bf16[32,4096]{1,0:T(8,128)(2,1)S(1)}, bf16[32,4096]{1,0:T(8,128)(2,1)S(1)}, u32[]{:S(2)}, u32[]{:S(2)}) collective-permute-start(bf16[32,4096]{1,0:T(8,128)(2,1)S(1)} %slice.62), channel_id=1, source_target_pairs={{0,4},{1,5},{2,0},{3,1},{4,8},{5,9},{6,2},{7,3},{8,12},{9,13},{10,... | collective-permute-start | bytes 786440 | tf_op jit(solution)/shard_map/ppermute | solution.py:372
  95.8 8.5 %collective-permute-start.27 = (bf16[32,4096]{1,0:T(8,128)(2,1)S(1)}, bf16[32,4096]{1,0:T(8,128)(2,1)S(1)}, u32[]{:S(2)}, u32[]{:S(2)}) collective-permute-start(bf16[32,4096]{1,0:T(8,128)(2,1)S(1)} %slice.63), channel_id=1, source_target_pairs={{0,2},{1,3},{2,6},{3,7},{4,0},{5,1},{6,10},{7,11},{8,4},{9,5},{10,... | collective-permute-start | bytes 786440 | tf_op jit(solution)/shard_map/ppermute | solution.py:372
  (11 other events, 92.4 us)

commit v5 on v4

--- a/solution.py
+++ b/solution.py
@@ -42,7 +42,7 @@
             out_specs=pl.BlockSpec((depth, wide), lambda i, plane: (0, 0)),
         ),
         out_shape=jax.ShapeDtypeStruct((depth, wide), weight.dtype),
-        compiler_params=pltpu.CompilerParams(vmem_limit_bytes=VMEM),
+        compiler_params=pltpu.CompilerParams(vmem_limit_bytes=60 * MIB),
         name="pack",
     )(plane, weight, keys, values)
 
@@ -431,6 +431,7 @@
             behind = [*first, crossed[step - 2][0]]
         down, up = held_back(down, *behind), held_back(up, *behind)
         behind = []
+    sent = [down, up]
     down, up = send(down[: depth // 2], ahead), send(up[depth // 2 :], back)
     far = jnp.concatenate([down, up], 0)
     near[half] = (far, 0)
@@ -438,7 +439,7 @@
     for i, distance in enumerate((1 - half, half - 1, half)):
         crossed[distance] = (over, i)
     second = part(1, crossed, 0, ())
-    last = [down, up, *second]
+    last = [*sent, *second]
     blocks = [(own, 0)] + [near[d] for d in distances[1:]]
     block = (size, 2 * head_size)
     theirs, ours, picked, given = part(

time: 116 us -> 115 us (level)
  local copies, waits for them, and re-layouts: 4.4 us -> 1.55 us
  Pallas kernels: 37.8 us -> 39.8 us
    unnamed x13 -> x9, local copies, waits for them, and re-layouts: 2.88 us -> 0.04 us
    pallas_call x1, Pallas kernels: 0.08 us -> 1.99 us  [pack(): pl.pallas_call(pack_kernel, grid_spec=pltpu.PrefetchScalarGridSpec(num_sc...]
  transfers between devices with their start and end apart: 29 -> 29, of which waited for: 15 -> 14; matrix products, arithmetic and copies ran while one was open for 4% -> 4% of each run, Pallas kernels for 25% -> 26%
where the time goes in v5:
time: 115 us
  waiting for transfers between devices  46.2 us (40%)
  Pallas kernels  39.8 us (35%)
  starting transfers between devices  23.7 us (21%)
  other arithmetic  2.88 us (3%)
  local copies, waits for them, and re-layouts  1.55 us (1%)
    ppermute x26, waiting for transfers between devices, send(): return lax.ppermute(array, 'ctx', to)  42.4 us
    ppermute x26, starting transfers between devices, send(): return lax.ppermute(array, 'ctx', to)  18.9 us
    pallas_call x4, Pallas kernels, query(): pl.pallas_call(functools.partial(query_kernel, depth, where, bool(totals)...  14.7 us
    pallas_call x2, Pallas kernels, attend(): pl.pallas_call(functools.partial(attend_kernel, math.log2(math.e) / math....  13.7 us
    pallas_call x1, Pallas kernels, project(): pl.pallas_call(functools.partial(project_kernel, len(attention), len(arra...  9.43 us
    ppermute x3, starting transfers between devices, cross(): return lax.ppermute(array, 'groups', [(0, 1), (1, 0)])  4.8 us
    ppermute x3, waiting for transfers between devices, cross(): return lax.ppermute(array, 'groups', [(0, 1), (1, 0)])  3.82 us
  transfers between devices with their start and end apart: 29, of which 14 were waited for; matrix products, arithmetic and copies ran while one was open for 4% of the time, Pallas kernels for 26%

profile of v5, /device:TPU:0, one launch (start us, length us, event | category | flops | bytes accessed | tf_op | source)
XLA Modules:
  0.0 114.7 jit_solution(4876466990689740177)
XLA Ops:
  0.5 2.0 %pack.1.refs_4_ = bf16[256,1024]{1,0:T(8,128)(2,1)} custom-call(s32[1]{0:T(128)} %bitcast.plane_ref, bf16[256,1024]{1,0:T(8,128)(2,1)} %refs_0_.7, bf16[512,128]{1,0:T(8,128)(2,1)} %keys_ref.1, bf16[512,128]{1,0:T(8,128)(2,1)} %values_ref.1), custom_call_target="tpu_custom_call" | custom-call | tf_op jit(solution)/shard_map/pack/pallas_call | solution.py:32
  2.4 2.5 %collective-permute-start.3 = (bf16[256,1024]{1,0:T(8,128)(2,1)}, bf16[256,1024]{1,0:T(8,128)(2,1)S(1)}, u32[]{:S(2)}, u32[]{:S(2)}) collective-permute-start(bf16[256,1024]{1,0:T(8,128)(2,1)} %pack.1.refs_4_), channel_id=1, source_target_pairs={{0,2},{1,3},{2,6},{3,7},{4,0},{5,1},{6,10},{7,11},{8,4},{9,5},{10,... | collective-permute-start | bytes 1572872 | tf_op jit(solution)/shard_map/ppermute | solution.py:372
  8.9 9.0 %collective-permute-done.3.refs_2_.refs_6_ = bf16[256,1024]{1,0:T(8,128)(2,1)S(1)} collective-permute-done((bf16[256,1024]{1,0:T(8,128)(2,1)}, bf16[256,1024]{1,0:T(8,128)(2,1)S(1)}, u32[]{:S(2)}, u32[]{:S(2)}) %collective-permute-start.3) | collective-permute-done | bytes 524320 | tf_op jit(solution)/shard_map/ppermute | solution.py:372
  17.8 1.7 %collective-permute-start.4 = (bf16[256,1024]{1,0:T(8,128)(2,1)S(1)}, bf16[256,1024]{1,0:T(8,128)(2,1)S(1)}, u32[]{:S(2)}, u32[]{:S(2)}) collective-permute-start(bf16[256,1024]{1,0:T(8,128)(2,1)S(1)} %collective-permute-done.3.refs_2_.refs_6_), channel_id=1, source_target_pairs={{0,2},{1,3},{2,6},{3,7},{4,0},{5,1},{6,10},{7,11},{8,4},{9,5},{10,... | collective-permute-start | bytes 1572872 | tf_op jit(solution)/shard_map/ppermute | solution.py:372
  19.9 1.7 %collective-permute-start.6 = (bf16[512,512]{1,0:T(8,128)(2,1)S(1)}, bf16[512,512]{1,0:T(8,128)(2,1)S(1)}, u32[]{:S(2)}, u32[]{:S(2)}) collective-permute-start(bf16[512,512]{1,0:T(8,128)(2,1)S(1)} %pad_maximum_fusion.4), channel_id=1, source_target_pairs={{0,16},{16,0},{1,17},{17,1},{2,18},{18,2},{3,19},{19,3},{4,20},{20... | collective-permute-start | bytes 1572872 | tf_op jit(solution)/shard_map/ppermute | solution.py:378
  21.7 9.9 %collective-permute-done.4.refs_4_.refs_8_ = bf16[256,1024]{1,0:T(8,128)(2,1)S(1)} collective-permute-done((bf16[256,1024]{1,0:T(8,128)(2,1)S(1)}, bf16[256,1024]{1,0:T(8,128)(2,1)S(1)}, u32[]{:S(2)}, u32[]{:S(2)}) %collective-permute-start.4) | collective-permute-done | bytes 524320 | tf_op jit(solution)/shard_map/ppermute | solution.py:372
  35.2 3.9 %query.4 = (f32[512,512]{1,0:T(8,128)S(1)}, f32[512,512]{1,0:T(8,128)S(1)}) custom-call(s32[12]{0:T(128)S(1)} %get-tuple-element.43.scalar_ref, bf16[256,1024]{1,0:T(8,128)(2,1)S(1)} %copy-done.1, bf16[256,1024]{1,0:T(8,128)(2,1)S(1)} %collective-permute-done.refs_1_.refs_5_, bf16[256,1024]{1,0:T(8,128)(2,1)S(1)} %collective-permute-done.3.refs_2_.refs_6_, ...), custom_call_target="tpu_custom_call" | custom-call | flops 1955000064 | bytes 1000 | tf_op jit(solution)/shard_map/query/pallas_call | solution.py:172
  39.2 5.3 %collective-permute-done.7.refs_2_ = bf16[256,1024]{1,0:T(8,128)(2,1)S(1)} collective-permute-done((bf16[256,1024]{1,0:T(8,128)(2,1)S(1)}, bf16[256,1024]{1,0:T(8,128)(2,1)S(1)}, u32[]{:S(2)}, u32[]{:S(2)}) %collective-permute-start.7) | collective-permute-done | bytes 524320 | tf_op jit(solution)/shard_map/ppermute | solution.py:372
  45.5 1.6 %collective-permute-start.12 = (bf16[128,1024]{1,0:T(8,128)(2,1)S(1)}, bf16[128,1024]{1,0:T(8,128)(2,1)S(1)}, u32[]{:S(2)}, u32[]{:S(2)}) collective-permute-start(bf16[128,1024]{1,0:T(8,128)(2,1)S(1)} %slice.58), channel_id=1, source_target_pairs={{0,2},{1,3},{2,6},{3,7},{4,0},{5,1},{6,10},{7,11},{8,4},{9,5},{10,... | collective-permute-start | bytes 786440 | tf_op jit(solution)/shard_map/ppermute | solution.py:372
  47.6 3.9 %query.5 = (f32[512,512]{1,0:T(8,128)S(1)}, f32[512,512]{1,0:T(8,128)S(1)}) custom-call(s32[12]{0:T(128)S(1)} %get-tuple-element.50.scalar_ref, bf16[256,1024]{1,0:T(8,128)(2,1)S(1)} %copy-done.1, bf16[512,512]{1,0:T(8,128)(2,1)S(1)} %collective-permute-done.6.refs_1_, bf16[512,512]{1,0:T(8,128)(2,1)S(1)} %collective-permute-done.8.refs_2_, ...), custom_call_target="tpu_custom_call" | custom-call | flops 1955000064 | bytes 1000 | tf_op jit(solution)/shard_map/query/pallas_call | solution.py:172
  51.6 1.6 %collective-permute-start.13 = (bf16[64,4096]{1,0:T(8,128)(2,1)S(1)}, bf16[64,4096]{1,0:T(8,128)(2,1)S(1)}, u32[]{:S(2)}, u32[]{:S(2)}) collective-permute-start(bf16[64,4096]{1,0:T(8,128)(2,1)S(1)} %copy-done.3), channel_id=1, source_target_pairs={{0,2},{1,3},{2,6},{3,7},{4,0},{5,1},{6,10},{7,11},{8,4},{9,5},{10,... | collective-permute-start | bytes 1572872 | tf_op jit(solution)/shard_map/ppermute | solution.py:372
  54.5 3.5 %query.6 = (f32[512,512]{1,0:T(8,128)S(1)}, f32[512,512]{1,0:T(8,128)S(1)}, bf16[4,512,256]{2,1,0:T(8,128)(2,1)S(1)}, bf16[3,512,256]{2,1,0:T(8,128)(2,1)S(1)}) custom-call(s32[10]{0:T(128)S(1)} %get-tuple-element.54.scalar_ref, bf16[256,1024]{1,0:T(8,128)(2,1)S(1)} %copy-done.1, bf16[256,1024]{1,0:T(8,128)(2,1)S(1)} %collective-permute-done.2.refs_1_, ...), custom_call_target="tpu_custom_call" | custom-call | flops 1955000064 | bytes 1000 | tf_op jit(solution)/shard_map/query/pallas_call | solution.py:172
  58.6 4.6 %collective-permute-done.13.refs_6_ = bf16[64,4096]{1,0:T(8,128)(2,1)S(1)} collective-permute-done((bf16[64,4096]{1,0:T(8,128)(2,1)S(1)}, bf16[64,4096]{1,0:T(8,128)(2,1)S(1)}, u32[]{:S(2)}, u32[]{:S(2)}) %collective-permute-start.13) | collective-permute-done | bytes 524320 | tf_op jit(solution)/shard_map/ppermute | solution.py:372
  63.2 1.6 %collective-permute-done.9.refs_4_ = bf16[64,4096]{1,0:T(8,128)(2,1)S(1)} collective-permute-done((bf16[64,4096]{1,0:T(8,128)(2,1)S(1)}, bf16[64,4096]{1,0:T(8,128)(2,1)S(1)}, u32[]{:S(2)}, u32[]{:S(2)}) %collective-permute-start.9) | collective-permute-done | bytes 524320 | tf_op jit(solution)/shard_map/ppermute | solution.py:372
  65.0 1.6 %collective-permute-start.19 = (bf16[64,4096]{1,0:T(8,128)(2,1)S(1)}, bf16[64,4096]{1,0:T(8,128)(2,1)S(1)}, u32[]{:S(2)}, u32[]{:S(2)}) collective-permute-start(bf16[64,4096]{1,0:T(8,128)(2,1)S(1)} %collective-permute-done.13.refs_6_), channel_id=1, source_target_pairs={{0,2},{1,3},{2,6},{3,7},{4,0},{5,1},{6,10},{7,11},{8,4},{9,5},{10,... | collective-permute-start | bytes 1572872 | tf_op jit(solution)/shard_map/ppermute | solution.py:372
  68.7 6.9 %attend.2.refs_0_ = bf16[512,512]{1,0:T(8,128)(2,1)S(1)} custom-call(f32[3]{0:T(128)S(1)} %compare_select_fusion.9.bias_ref, s32[3]{0:T(128)S(1)} %compare_convert_fusion.swap_ref, f32[512,512]{1,0:T(8,128)S(1)} %get-tuple-element.59.refs_0_, f32[512,512]{1,0:T(8,128)S(1)} %collective-permute-done.14.refs_1_, ...), custom_call_target="tpu_custom_call" | custom-call | flops 3910000128 | bytes 1000 | tf_op jit(solution)/shard_map/attend/pallas_call | solution.py:260
  75.6 3.7 %collective-permute-done.19.refs_9_ = bf16[64,4096]{1,0:T(8,128)(2,1)S(1)} collective-permute-done((bf16[64,4096]{1,0:T(8,128)(2,1)S(1)}, bf16[64,4096]{1,0:T(8,128)(2,1)S(1)}, u32[]{:S(2)}, u32[]{:S(2)}) %collective-permute-start.19) | collective-permute-done | bytes 524320 | tf_op jit(solution)/shard_map/ppermute | solution.py:372
  81.0 1.6 %collective-permute-start.23 = (bf16[64,4096]{1,0:T(8,128)(2,1)S(1)}, bf16[64,4096]{1,0:T(8,128)(2,1)S(1)}, u32[]{:S(2)}, u32[]{:S(2)}) collective-permute-start(bf16[64,4096]{1,0:T(8,128)(2,1)S(1)} %collective-permute-done.19.refs_9_), channel_id=1, source_target_pairs={{0,2},{1,3},{2,6},{3,7},{4,0},{5,1},{6,10},{7,11},{8,4},{9,5},{10,... | collective-permute-start | bytes 1572872 | tf_op jit(solution)/shard_map/ppermute | solution.py:372
  82.7 3.8 %collective-permute-done.16.refs_1_ = bf16[768,512]{1,0:T(8,128)(2,1)S(1)} collective-permute-done((bf16[768,512]{1,0:T(8,128)(2,1)S(1)}, bf16[768,512]{1,0:T(8,128)(2,1)S(1)}, u32[]{:S(2)}, u32[]{:S(2)}) %collective-permute-start.16) | collective-permute-done | bytes 786464 | tf_op jit(solution)/shard_map/ppermute | solution.py:378
  86.6 3.3 %query.7 = (f32[512,512]{1,0:T(8,128)S(1)}, f32[512,512]{1,0:T(8,128)S(1)}) custom-call(s32[10]{0:T(128)S(1)} %get-tuple-element.62.scalar_ref, bf16[256,1024]{1,0:T(8,128)(2,1)S(1)} %copy-done.1, bf16[768,512]{1,0:T(8,128)(2,1)S(1)} %collective-permute-done.16.refs_1_, bf16[512,4096]{1,0:T(8,128)(2,1)} %collective-permute-done.5.refs_5_.refs_3_.refs_9_.refs_2_, ...), custom_call_target="tpu_custom_call" | custom-call | flops 1955000064 | bytes 1000 | tf_op jit(solution)/shard_map/query/pallas_call | solution.py:172
  90.0 3.7 %collective-permute-done.22.refs_10_ = bf16[64,4096]{1,0:T(8,128)(2,1)S(1)} collective-permute-done((bf16[64,4096]{1,0:T(8,128)(2,1)S(1)}, bf16[64,4096]{1,0:T(8,128)(2,1)S(1)}, u32[]{:S(2)}, u32[]{:S(2)}) %collective-permute-start.22) | collective-permute-done | bytes 524320 | tf_op jit(solution)/shard_map/ppermute | solution.py:372
  94.6 1.6 %collective-permute-start.27 = (bf16[32,4096]{1,0:T(8,128)(2,1)S(1)}, bf16[32,4096]{1,0:T(8,128)(2,1)S(1)}, u32[]{:S(2)}, u32[]{:S(2)}) collective-permute-start(bf16[32,4096]{1,0:T(8,128)(2,1)S(1)} %slice.63), channel_id=1, source_target_pairs={{0,2},{1,3},{2,6},{3,7},{4,0},{5,1},{6,10},{7,11},{8,4},{9,5},{10,... | collective-permute-start | bytes 786440 | tf_op jit(solution)/shard_map/ppermute | solution.py:372
  96.3 6.8 %attend.3.refs_1_ = bf16[512,512]{1,0:T(8,128)(2,1)S(1)} custom-call(f32[3]{0:T(128)S(1)} %compare_select_fusion.9.bias_ref, s32[3]{0:T(128)S(1)} %compare_convert_fusion.swap_ref, f32[512,512]{1,0:T(8,128)S(1)} %get-tuple-element.67.refs_0_, f32[512,512]{1,0:T(8,128)S(1)} %collective-permute-done.20.refs_1_, ...), custom_call_target="tpu_custom_call" | custom-call | flops 3910000128 | bytes 1000 | tf_op jit(solution)/shard_map/attend/pallas_call | solution.py:260
  105.1 9.4 %project.1 = bf16[512,4096]{1,0:T(8,128)(2,1)} custom-call(s32[18]{0:T(128)S(1)} %pad_add_fusion.place_ref, bf16[512,512]{1,0:T(8,128)(2,1)S(1)} %attend.2.refs_0_, bf16[512,512]{1,0:T(8,128)(2,1)S(1)} %attend.3.refs_1_, bf16[64,4096]{1,0:T(8,128)(2,1)S(1)} %copy-done.3, bf16[64,4096]{1,0:T(8,128)(2,1)S(1)} %collective-permute-done.10.refs_3_, ...), custom_call_target="tpu_custom_call" | custom-call | flops 4294967296 | bytes 13631488 | tf_op jit(solution)/shard_map/project/pallas_call | solution.py:331
  (89 shorter events, 18.8 us)
Async XLA Ops:
  0.0 35.2 %collective-permute-start.5 = (bf16[512,4096]{1,0:T(8,128)(2,1)}, bf16[512,4096]{1,0:T(8,128)(2,1)}, u32[]{:S(2)}, u32[]{:S(2)}) collective-permute-start(bf16[512,4096]{1,0:T(8,128)(2,1)} %refs_3_.1), channel_id=1, source_target_pairs={{0,1},{1,0},{2,3},{3,2},{4,5},{5,4},{6,7},{7,6},{8,9},{9,8},{10,11... | collective-permute-start | bytes 12582920 | tf_op jit(solution)/shard_map/ppermute | solution.py:372
  2.4 15.4 %collective-permute-start.3 = (bf16[256,1024]{1,0:T(8,128)(2,1)}, bf16[256,1024]{1,0:T(8,128)(2,1)S(1)}, u32[]{:S(2)}, u32[]{:S(2)}) collective-permute-start(bf16[256,1024]{1,0:T(8,128)(2,1)} %pack.1.refs_4_), channel_id=1, source_target_pairs={{0,2},{1,3},{2,6},{3,7},{4,0},{5,1},{6,10},{7,11},{8,4},{9,5},{10,... | collective-permute-start | bytes 1572872 | tf_op jit(solution)/shard_map/ppermute | solution.py:372
  5.0 14.5 %collective-permute-start = (bf16[256,1024]{1,0:T(8,128)(2,1)}, bf16[256,1024]{1,0:T(8,128)(2,1)S(1)}, u32[]{:S(2)}, u32[]{:S(2)}) collective-permute-start(bf16[256,1024]{1,0:T(8,128)(2,1)} %pack.1.refs_4_), channel_id=1, source_target_pairs={{0,4},{1,5},{2,0},{3,1},{4,8},{5,9},{6,2},{7,3},{8,12},{9,13},{10,... | collective-permute-start | bytes 1572872 | tf_op jit(solution)/shard_map/ppermute | solution.py:372
  17.8 13.8 %collective-permute-start.4 = (bf16[256,1024]{1,0:T(8,128)(2,1)S(1)}, bf16[256,1024]{1,0:T(8,128)(2,1)S(1)}, u32[]{:S(2)}, u32[]{:S(2)}) collective-permute-start(bf16[256,1024]{1,0:T(8,128)(2,1)S(1)} %collective-permute-done.3.refs_2_.refs_6_), channel_id=1, source_target_pairs={{0,2},{1,3},{2,6},{3,7},{4,0},{5,1},{6,10},{7,11},{8,4},{9,5},{10,... | collective-permute-start | bytes 1572872 | tf_op jit(solution)/shard_map/ppermute | solution.py:372
  19.5 13.6 %collective-permute-start.1 = (bf16[256,1024]{1,0:T(8,128)(2,1)S(1)}, bf16[256,1024]{1,0:T(8,128)(2,1)S(1)}, u32[]{:S(2)}, u32[]{:S(2)}) collective-permute-start(bf16[256,1024]{1,0:T(8,128)(2,1)S(1)} %collective-permute-done.refs_1_.refs_5_), channel_id=1, source_target_pairs={{0,4},{1,5},{2,0},{3,1},{4,8},{5,9},{6,2},{7,3},{8,12},{9,13},{10,... | collective-permute-start | bytes 1572872 | tf_op jit(solution)/shard_map/ppermute | solution.py:372
  19.9 19.2 %collective-permute-start.6 = (bf16[512,512]{1,0:T(8,128)(2,1)S(1)}, bf16[512,512]{1,0:T(8,128)(2,1)S(1)}, u32[]{:S(2)}, u32[]{:S(2)}) collective-permute-start(bf16[512,512]{1,0:T(8,128)(2,1)S(1)} %pad_maximum_fusion.4), channel_id=1, source_target_pairs={{0,16},{16,0},{1,17},{17,1},{2,18},{18,2},{3,19},{19,3},{4,20},{20... | collective-permute-start | bytes 1572872 | tf_op jit(solution)/shard_map/ppermute | solution.py:378
  31.6 12.9 %collective-permute-start.7 = (bf16[256,1024]{1,0:T(8,128)(2,1)S(1)}, bf16[256,1024]{1,0:T(8,128)(2,1)S(1)}, u32[]{:S(2)}, u32[]{:S(2)}) collective-permute-start(bf16[256,1024]{1,0:T(8,128)(2,1)S(1)} %collective-permute-done.4.refs_4_.refs_8_), channel_id=1, source_target_pairs={{0,2},{1,3},{2,6},{3,7},{4,0},{5,1},{6,10},{7,11},{8,4},{9,5},{10,... | collective-permute-start | bytes 1572872 | tf_op jit(solution)/shard_map/ppermute | solution.py:372
  33.1 12.4 %collective-permute-start.2 = (bf16[256,1024]{1,0:T(8,128)(2,1)S(1)}, bf16[256,1024]{1,0:T(8,128)(2,1)S(1)}, u32[]{:S(2)}, u32[]{:S(2)}) collective-permute-start(bf16[256,1024]{1,0:T(8,128)(2,1)S(1)} %collective-permute-done.1.refs_3_.refs_7_), channel_id=1, source_target_pairs={{0,4},{1,5},{2,0},{3,1},{4,8},{5,9},{6,2},{7,3},{8,12},{9,13},{10,... | collective-permute-start | bytes 1572872 | tf_op jit(solution)/shard_map/ppermute | solution.py:372
  33.7 13.9 %collective-permute-start.8 = (bf16[512,512]{1,0:T(8,128)(2,1)S(1)}, bf16[512,512]{1,0:T(8,128)(2,1)S(1)}, u32[]{:S(2)}, u32[]{:S(2)}) collective-permute-start(bf16[512,512]{1,0:T(8,128)(2,1)S(1)} %pad_maximum_fusion.5), channel_id=1, source_target_pairs={{0,16},{16,0},{1,17},{17,1},{2,18},{18,2},{3,19},{19,3},{4,20},{20... | collective-permute-start | bytes 1572872 | tf_op jit(solution)/shard_map/ppermute | solution.py:378
  45.5 8.9 %collective-permute-start.12 = (bf16[128,1024]{1,0:T(8,128)(2,1)S(1)}, bf16[128,1024]{1,0:T(8,128)(2,1)S(1)}, u32[]{:S(2)}, u32[]{:S(2)}) collective-permute-start(bf16[128,1024]{1,0:T(8,128)(2,1)S(1)} %slice.58), channel_id=1, source_target_pairs={{0,2},{1,3},{2,6},{3,7},{4,0},{5,1},{6,10},{7,11},{8,4},{9,5},{10,... | collective-permute-start | bytes 786440 | tf_op jit(solution)/shard_map/ppermute | solution.py:372
  51.6 11.6 %collective-permute-start.13 = (bf16[64,4096]{1,0:T(8,128)(2,1)S(1)}, bf16[64,4096]{1,0:T(8,128)(2,1)S(1)}, u32[]{:S(2)}, u32[]{:S(2)}) collective-permute-start(bf16[64,4096]{1,0:T(8,128)(2,1)S(1)} %copy-done.3), channel_id=1, source_target_pairs={{0,2},{1,3},{2,6},{3,7},{4,0},{5,1},{6,10},{7,11},{8,4},{9,5},{10,... | collective-permute-start | bytes 1572872 | tf_op jit(solution)/shard_map/ppermute | solution.py:372
  53.2 11.6 %collective-permute-start.9 = (bf16[64,4096]{1,0:T(8,128)(2,1)S(1)}, bf16[64,4096]{1,0:T(8,128)(2,1)S(1)}, u32[]{:S(2)}, u32[]{:S(2)}) collective-permute-start(bf16[64,4096]{1,0:T(8,128)(2,1)S(1)} %copy-done.3), channel_id=1, source_target_pairs={{0,4},{1,5},{2,0},{3,1},{4,8},{5,9},{6,2},{7,3},{8,12},{9,13},{10,... | collective-permute-start | bytes 1572872 | tf_op jit(solution)/shard_map/ppermute | solution.py:372
  53.6 11.3 %collective-permute-start.10 = (bf16[64,4096]{1,0:T(8,128)(2,1)S(1)}, bf16[64,4096]{1,0:T(8,128)(2,1)S(1)}, u32[]{:S(2)}, u32[]{:S(2)}) collective-permute-start(bf16[64,4096]{1,0:T(8,128)(2,1)S(1)} %copy-done.3), channel_id=1, source_target_pairs={{0,1},{1,0},{2,3},{3,2},{4,5},{5,4},{6,7},{7,6},{8,9},{9,8},{10,11... | collective-permute-start | bytes 1572872 | tf_op jit(solution)/shard_map/ppermute | solution.py:372
  58.0 9.2 %collective-permute-start.15 = (bf16[3,512,256]{2,1,0:T(8,128)(2,1)S(1)}, bf16[3,512,256]{2,1,0:T(8,128)(2,1)S(1)}, u32[]{:S(2)}, u32[]{:S(2)}) collective-permute-start(bf16[3,512,256]{2,1,0:T(8,128)(2,1)S(1)} %get-tuple-element.55), channel_id=1, source_target_pairs={{0,1},{1,0},{2,3},{3,2},{4,5},{5,4},{6,7},{7,6},{8,9},{9,8},{10,11... | collective-permute-start | bytes 2359304 | tf_op jit(solution)/shard_map/ppermute | solution.py:372
  58.1 10.7 %collective-permute-start.14 = (f32[512,512]{1,0:T(8,128)S(1)}, f32[512,512]{1,0:T(8,128)S(1)}, u32[]{:S(2)}, u32[]{:S(2)}) collective-permute-start(f32[512,512]{1,0:T(8,128)S(1)} %get-tuple-element.60), channel_id=1, source_target_pairs={{0,1},{1,0},{2,3},{3,2},{4,5},{5,4},{6,7},{7,6},{8,9},{9,8},{10,11... | collective-permute-start | bytes 3145736 | tf_op jit(solution)/shard_map/ppermute | solution.py:372
  64.9 14.4 %collective-permute-start.18 = (bf16[128,4096]{1,0:T(8,128)(2,1)S(1)}, bf16[128,4096]{1,0:T(8,128)(2,1)S(1)}, u32[]{:S(2)}, u32[]{:S(2)}) collective-permute-start(bf16[128,4096]{1,0:T(8,128)(2,1)S(1)} %pad_maximum_fusion), channel_id=1, source_target_pairs={{0,1},{1,0},{2,3},{3,2},{4,5},{5,4},{6,7},{7,6},{8,9},{9,8},{10,11... | collective-permute-start | bytes 3145736 | tf_op jit(solution)/shard_map/ppermute | solution.py:372
  65.0 14.3 %collective-permute-start.19 = (bf16[64,4096]{1,0:T(8,128)(2,1)S(1)}, bf16[64,4096]{1,0:T(8,128)(2,1)S(1)}, u32[]{:S(2)}, u32[]{:S(2)}) collective-permute-start(bf16[64,4096]{1,0:T(8,128)(2,1)S(1)} %collective-permute-done.13.refs_6_), channel_id=1, source_target_pairs={{0,2},{1,3},{2,6},{3,7},{4,0},{5,1},{6,10},{7,11},{8,4},{9,5},{10,... | collective-permute-start | bytes 1572872 | tf_op jit(solution)/shard_map/ppermute | solution.py:372
  66.6 14.0 %collective-permute-start.17 = (bf16[64,4096]{1,0:T(8,128)(2,1)S(1)}, bf16[64,4096]{1,0:T(8,128)(2,1)S(1)}, u32[]{:S(2)}, u32[]{:S(2)}) collective-permute-start(bf16[64,4096]{1,0:T(8,128)(2,1)S(1)} %collective-permute-done.9.refs_4_), channel_id=1, source_target_pairs={{0,4},{1,5},{2,0},{3,1},{4,8},{5,9},{6,2},{7,3},{8,12},{9,13},{10,... | collective-permute-start | bytes 1572872 | tf_op jit(solution)/shard_map/ppermute | solution.py:372
  67.2 19.4 %collective-permute-start.16 = (bf16[768,512]{1,0:T(8,128)(2,1)S(1)}, bf16[768,512]{1,0:T(8,128)(2,1)S(1)}, u32[]{:S(2)}, u32[]{:S(2)}) collective-permute-start(bf16[768,512]{1,0:T(8,128)(2,1)S(1)} %pad_maximum_fusion.3), channel_id=1, source_target_pairs={{0,16},{16,0},{1,17},{17,1},{2,18},{18,2},{3,19},{19,3},{4,20},{20... | collective-permute-start | bytes 2359304 | tf_op jit(solution)/shard_map/ppermute | solution.py:378
  80.6 13.2 %collective-permute-start.22 = (bf16[64,4096]{1,0:T(8,128)(2,1)S(1)}, bf16[64,4096]{1,0:T(8,128)(2,1)S(1)}, u32[]{:S(2)}, u32[]{:S(2)}) collective-permute-start(bf16[64,4096]{1,0:T(8,128)(2,1)S(1)} %collective-permute-done.17.refs_7_), channel_id=1, source_target_pairs={{0,4},{1,5},{2,0},{3,1},{4,8},{5,9},{6,2},{7,3},{8,12},{9,13},{10,... | collective-permute-start | bytes 1572872 | tf_op jit(solution)/shard_map/ppermute | solution.py:372
  81.0 12.9 %collective-permute-start.23 = (bf16[64,4096]{1,0:T(8,128)(2,1)S(1)}, bf16[64,4096]{1,0:T(8,128)(2,1)S(1)}, u32[]{:S(2)}, u32[]{:S(2)}) collective-permute-start(bf16[64,4096]{1,0:T(8,128)(2,1)S(1)} %collective-permute-done.19.refs_9_), channel_id=1, source_target_pairs={{0,2},{1,3},{2,6},{3,7},{4,0},{5,1},{6,10},{7,11},{8,4},{9,5},{10,... | collective-permute-start | bytes 1572872 | tf_op jit(solution)/shard_map/ppermute | solution.py:372
  82.7 11.4 %collective-permute-start.21 = (bf16[128,4096]{1,0:T(8,128)(2,1)S(1)}, bf16[128,4096]{1,0:T(8,128)(2,1)S(1)}, u32[]{:S(2)}, u32[]{:S(2)}) collective-permute-start(bf16[128,4096]{1,0:T(8,128)(2,1)S(1)} %pad_maximum_fusion.1), channel_id=1, source_target_pairs={{0,1},{1,0},{2,3},{3,2},{4,5},{5,4},{6,7},{7,6},{8,9},{9,8},{10,11... | collective-permute-start | bytes 3145736 | tf_op jit(solution)/shard_map/ppermute | solution.py:372
  94.0 11.1 %collective-permute-start.24 = (bf16[128,4096]{1,0:T(8,128)(2,1)S(1)}, bf16[128,4096]{1,0:T(8,128)(2,1)S(1)}, u32[]{:S(2)}, u32[]{:S(2)}) collective-permute-start(bf16[128,4096]{1,0:T(8,128)(2,1)S(1)} %pad_maximum_fusion.2), channel_id=1, source_target_pairs={{0,1},{1,0},{2,3},{3,2},{4,5},{5,4},{6,7},{7,6},{8,9},{9,8},{10,11... | collective-permute-start | bytes 3145736 | tf_op jit(solution)/shard_map/ppermute | solution.py:372
  94.1 9.0 %collective-permute-start.25 = (bf16[32,4096]{1,0:T(8,128)(2,1)S(1)}, bf16[32,4096]{1,0:T(8,128)(2,1)S(1)}, u32[]{:S(2)}, u32[]{:S(2)}) collective-permute-start(bf16[32,4096]{1,0:T(8,128)(2,1)S(1)} %slice.62), channel_id=1, source_target_pairs={{0,4},{1,5},{2,0},{3,1},{4,8},{5,9},{6,2},{7,3},{8,12},{9,13},{10,... | collective-permute-start | bytes 786440 | tf_op jit(solution)/shard_map/ppermute | solution.py:372
  (9 other events, 101.7 us)
